TPU v7x, 32 devices: a whole 2x2x4 slice. The times are simulated.
32 devices in a mesh: dp: 4 (over y, core), fsdp: 8 (over z, x).
Axes of the slice: x: 2, y: 2, z: 4, core: 2. Of those that a mesh axis runs over, the one named last changes fastest.
Arguments:
- small_images: bfloat16 [64, 196, 256], P(('dp', 'fsdp')), may hold values from -6 to 6
- large_images: bfloat16 [256, 784, 256], P(('dp', 'fsdp')), may hold values from -6 to 6
- small_cot: bfloat16 [64, 196, 256], P(('dp', 'fsdp'))
- large_cot: bfloat16 [256, 784, 256], P(('dp', 'fsdp'))
- counts: int32 [32, 2], P(('dp', 'fsdp')), may hold values from 0 to 8, as said below
- qkv_master: float32 [256, 768], P(('dp', 'fsdp')), may hold values from -0.25 to 0.25
- qkv_first: float32 [256, 768], P(('dp', 'fsdp')), may hold values from -0.015625 to 0.015625
- qkv_second: float32 [256, 768], P(('dp', 'fsdp')), may hold values from 1.2715658e-06 to 5.086263e-06
- proj_master: float32 [256, 256], P(None, ('dp', 'fsdp')), may hold values from -0.75 to 0.75
- proj_first: float32 [256, 256], P(None, ('dp', 'fsdp')), may hold values from -0.015625 to 0.015625
- proj_second: float32 [256, 256], P(None, ('dp', 'fsdp')), may hold values from 1.2715658e-06 to 5.086263e-06
- fc1_master: float32 [256, 1024], P(('dp', 'fsdp')), may hold values from -0.375 to 0.375
- fc1_first: float32 [256, 1024], P(('dp', 'fsdp')), may hold values from -0.015625 to 0.015625
- fc1_second: float32 [256, 1024], P(('dp', 'fsdp')), may hold values from 1.2715658e-06 to 5.086263e-06
- fc2_master: float32 [1024, 256], P(None, ('dp', 'fsdp')), may hold values from -0.1875 to 0.1875
- fc2_first: float32 [1024, 256], P(None, ('dp', 'fsdp')), may hold values from -0.015625 to 0.015625
- fc2_second: float32 [1024, 256], P(None, ('dp', 'fsdp')), may hold values from 1.2715658e-06 to 5.086263e-06
- vec_master: float32 [22, 256], P(None, ('dp', 'fsdp'))
- vec_first: float32 [22, 256], P(None, ('dp', 'fsdp')), may hold values from -0.015625 to 0.015625
- vec_second: float32 [22, 256], P(None, ('dp', 'fsdp')), may hold values from 1.2715658e-06 to 5.086263e-06
Outputs:
- small_output: bfloat16 [64, 196, 256], P(('dp', 'fsdp'))
- large_output: bfloat16 [256, 784, 256], P(('dp', 'fsdp'))
- small_input_grad: float32 [64, 196, 256], P(('dp', 'fsdp'))
- large_input_grad: float32 [256, 784, 256], P(('dp', 'fsdp'))
- qkv_new: float32 [256, 768], P(('dp', 'fsdp'))
- qkv_first_new: float32 [256, 768], P(('dp', 'fsdp'))
- qkv_second_new: float32 [256, 768], P(('dp', 'fsdp'))
- qkv_copy: bfloat16 [256, 768], P(('dp', 'fsdp'))
- proj_new: float32 [256, 256], P(None, ('dp', 'fsdp'))
- proj_first_new: float32 [256, 256], P(None, ('dp', 'fsdp'))
- proj_second_new: float32 [256, 256], P(None, ('dp', 'fsdp'))
- proj_copy: bfloat16 [256, 256], P(None, ('dp', 'fsdp'))
- fc1_new: float32 [256, 1024], P(('dp', 'fsdp'))
- fc1_first_new: float32 [256, 1024], P(('dp', 'fsdp'))
- fc1_second_new: float32 [256, 1024], P(('dp', 'fsdp'))
- fc1_copy: bfloat16 [256, 1024], P(('dp', 'fsdp'))
- fc2_new: float32 [1024, 256], P(None, ('dp', 'fsdp'))
- fc2_first_new: float32 [1024, 256], P(None, ('dp', 'fsdp'))
- fc2_second_new: float32 [1024, 256], P(None, ('dp', 'fsdp'))
- fc2_copy: bfloat16 [1024, 256], P(None, ('dp', 'fsdp'))
- vec_new: float32 [22, 256], P(None, ('dp', 'fsdp'))
- vec_first_new: float32 [22, 256], P(None, ('dp', 'fsdp'))
- vec_second_new: float32 [22, 256], P(None, ('dp', 'fsdp'))
- vec_copy: bfloat16 [22, 256], P(None, ('dp', 'fsdp'))
- grad_norm: float32 [], replicated
Inputs may be any that keep to these rules, and one draw needn't show every extreme that they name: counts[d, 0] and counts[d, 1] are the live image slots of the first and second bucket on device d (devices in the order dp, then fsdp); the slots below the count are live. The first is at most 2 and equals it on some device, the second at most 8 and equals it on some device.
All inputs are finite; a program needn't handle non-finite values.
Results may differ from a plain program's by a relative error of at most 0.008.
The roundings to bfloat16 on the way count: a program that leaves them out, or rounds other values in their place, can miss the bound.
Values may be sent and summed in bfloat16 or wider, within the bound.
No kernel may reach another device: no remote copies, remote signals or barrier semaphores. Data moves between devices by JAX's collectives and lax.ppermute only.
A program may use at most 448 MiB of HBM per device.

v0:
```python
import math

import jax
import jax.numpy as jnp
from jax import lax
from jax.sharding import PartitionSpec as P

HEADS = 8
STRIPE = 7
STEP = 10


epsilon = 1e-05
clip_norm = 1.0
beta_one = 0.5
beta_two = 0.5
rate_matrix = 0.1
rate_vector = 0.5
decay_matrix = 0.05
adam_epsilon = 1e-08


def layer_norm(values, gain_row, shift_row):
    centered = values - jnp.mean(values, axis=-1, keepdims=True)
    variance = jnp.mean(centered * centered, axis=-1, keepdims=True)
    return centered * lax.rsqrt(variance + epsilon) * gain_row + shift_row


def gelu_exact(values):
    return jax.nn.gelu(values, approximate=False)


def to_stripes(values, grid_side, vertical):
    image_count, model_width = (values.shape[0], values.shape[-1])
    if vertical:
        image_grid = values.reshape(
            image_count, grid_side, grid_side // STRIPE, STRIPE, model_width
        )
        image_grid = jnp.transpose(image_grid, (0, 2, 1, 3, 4))
        return image_grid.reshape(
            image_count * (grid_side // STRIPE), grid_side * STRIPE, model_width
        )
    return values.reshape(image_count * (grid_side // STRIPE), grid_side * STRIPE, model_width)


def from_stripes(values, image_count, grid_side, vertical):
    model_width = values.shape[-1]
    if vertical:
        image_grid = values.reshape(
            image_count, grid_side // STRIPE, grid_side, STRIPE, model_width
        )
        values = jnp.transpose(image_grid, (0, 2, 1, 3, 4))
    return values.reshape(image_count, grid_side * grid_side, model_width)


def position_term(values, kernel, offset, grid_side, vertical):
    image_count, cell_count, model_width = values.shape
    image_grid = values.reshape(image_count, grid_side, grid_side, model_width)
    padded = jnp.pad(image_grid, ((0, 0), (1, 1), (1, 1), (0, 0)))
    stripe_place = jnp.arange(grid_side) % STRIPE
    upper_mask = (stripe_place != 0).astype(jnp.float32)
    lower_mask = (stripe_place != STRIPE - 1).astype(jnp.float32)
    accumulated = jnp.zeros_like(image_grid) + offset
    for row_step in range(3):
        for col_step in range(3):
            shifted = (
                padded[:, row_step : row_step + grid_side, col_step : col_step + grid_side]
                * kernel[3 * row_step + col_step]
            )
            stripe_step = col_step if vertical else row_step
            if stripe_step != 1:
                keep_mask = upper_mask if stripe_step == 0 else lower_mask
                mask_shape = (1, 1, grid_side, 1) if vertical else (1, grid_side, 1, 1)
                shifted = shifted * keep_mask.reshape(mask_shape)
            accumulated = accumulated + shifted
    return accumulated.reshape(image_count, cell_count, model_width)


def split_heads(values):
    head_count = HEADS // 2
    return values.reshape(
        values.shape[0], values.shape[1], head_count, values.shape[2] // head_count
    )


def attend_forward(query_rows, key_rows, value_rows):
    score_scale = query_rows.shape[-1] ** (-0.5)
    scores = (
        jnp.einsum("bqhe,bkhe->bhqk", query_rows, key_rows, preferred_element_type=jnp.float32)
        * score_scale
    )
    row_max = jnp.max(scores, axis=-1, keepdims=True)
    exponent = jnp.exp(scores - row_max)
    row_total = jnp.sum(exponent, axis=-1, keepdims=True)
    probabilities = (exponent / row_total).astype(jnp.bfloat16)
    mixed_heads = jnp.einsum(
        "bhqk,bkhe->bqhe", probabilities, value_rows, preferred_element_type=jnp.float32
    )
    return (mixed_heads, row_max + jnp.log(row_total))


def attend_backward(query_rows, key_rows, value_rows, log_total, grad_mixed):
    score_scale = query_rows.shape[-1] ** (-0.5)
    scores = (
        jnp.einsum("bqhe,bkhe->bhqk", query_rows, key_rows, preferred_element_type=jnp.float32)
        * score_scale
    )
    probabilities = jnp.exp(scores - log_total)
    grad_probs = jnp.einsum(
        "bqhe,bkhe->bhqk", grad_mixed, value_rows, preferred_element_type=jnp.float32
    )
    inner_sum = jnp.sum(grad_probs * probabilities, axis=-1, keepdims=True)
    grad_scores = (probabilities * (grad_probs - inner_sum)).astype(jnp.bfloat16)
    grad_query = (
        jnp.einsum("bhqk,bkhe->bqhe", grad_scores, key_rows, preferred_element_type=jnp.float32)
        * score_scale
    )
    grad_key = (
        jnp.einsum("bhqk,bqhe->bkhe", grad_scores, query_rows, preferred_element_type=jnp.float32)
        * score_scale
    )
    grad_value = jnp.einsum(
        "bhqk,bqhe->bkhe",
        probabilities.astype(jnp.bfloat16),
        grad_mixed,
        preferred_element_type=jnp.float32,
    )
    return (grad_query, grad_key, grad_value)


def mixer_forward(query_rows, key_rows, value_rows, kernel, offset, grid_side):
    image_count, cell_count, model_width = query_rows.shape
    half_width = model_width // 2
    results = []
    log_totals = []
    for branch_index, vertical in enumerate((False, True)):
        channel_part = slice(branch_index * half_width, (branch_index + 1) * half_width)
        pieces = [
            split_heads(to_stripes(tensor[..., channel_part], grid_side, vertical))
            for tensor in (query_rows, key_rows, value_rows)
        ]
        mixed_heads, log_total = attend_forward(pieces[0], pieces[1], pieces[2])
        mixed_heads = mixed_heads.reshape(mixed_heads.shape[0], mixed_heads.shape[1], half_width)
        results.append(
            from_stripes(mixed_heads, image_count, grid_side, vertical)
            + position_term(
                value_rows[..., channel_part].astype(jnp.float32),
                kernel[:, channel_part],
                offset[channel_part],
                grid_side,
                vertical,
            )
        )
        log_totals.append(log_total)
    return (jnp.concatenate(results, axis=-1), log_totals)


def mixer_backward(
    query_rows, key_rows, value_rows, log_totals, grad_mixed, kernel, offset, grid_side
):
    image_count, cell_count, model_width = query_rows.shape
    half_width = model_width // 2
    query_grads, key_grads, value_grads, kernel_grads, offset_grads = ([], [], [], [], [])
    for branch_index, vertical in enumerate((False, True)):
        channel_part = slice(branch_index * half_width, (branch_index + 1) * half_width)
        pieces = [
            split_heads(to_stripes(tensor[..., channel_part], grid_side, vertical))
            for tensor in (query_rows, key_rows, value_rows, grad_mixed)
        ]
        head_grads = attend_backward(
            pieces[0], pieces[1], pieces[2], log_totals[branch_index], pieces[3]
        )
        head_grads = [
            from_stripes(
                tensor.reshape(tensor.shape[0], tensor.shape[1], half_width),
                image_count,
                grid_side,
                vertical,
            )
            for tensor in head_grads
        ]

        def local_term(values, kernel_part, offset_part):
            return position_term(values, kernel_part, offset_part, grid_side, vertical)

        ignored, term_back = jax.vjp(
            local_term,
            value_rows[..., channel_part].astype(jnp.float32),
            kernel[:, channel_part],
            offset[channel_part],
        )
        value_pos, kernel_part_grad, offset_part_grad = term_back(
            grad_mixed[..., channel_part].astype(jnp.float32)
        )
        query_grads.append(head_grads[0])
        key_grads.append(head_grads[1])
        value_grads.append(head_grads[2] + value_pos)
        kernel_grads.append(kernel_part_grad)
        offset_grads.append(offset_part_grad)
    return (
        jnp.concatenate(query_grads, axis=-1),
        jnp.concatenate(key_grads, axis=-1),
        jnp.concatenate(value_grads, axis=-1),
        jnp.concatenate(kernel_grads, axis=-1),
        jnp.concatenate(offset_grads, axis=-1),
    )


def adamw_update(weight, first, second, gradient, rate, decay):
    first = beta_one * first + (1.0 - beta_one) * gradient
    second = beta_two * second + (1.0 - beta_two) * gradient * gradient
    first_hat = first / (1.0 - beta_one**STEP)
    second_hat = second / (1.0 - beta_two**STEP)
    weight = weight - rate * (first_hat / (jnp.sqrt(second_hat) + adam_epsilon) + decay * weight)
    return (weight, first, second)


def on_device(
    small_images,
    large_images,
    small_cot,
    large_cot,
    counts,
    qkv_master,
    qkv_first,
    qkv_second,
    proj_master,
    proj_first,
    proj_second,
    fc1_master,
    fc1_first,
    fc1_second,
    fc2_master,
    fc2_first,
    fc2_second,
    vec_master,
    vec_first,
    vec_second,
):
    qkv_low = qkv_master.astype(jnp.bfloat16)
    proj_low = proj_master.astype(jnp.bfloat16)
    fc1_low = fc1_master.astype(jnp.bfloat16)
    fc2_low = fc2_master.astype(jnp.bfloat16)
    qkv_w, proj_w, vec_w = (
        lax.all_gather(qkv_low, ("dp", "fsdp"), axis=0, tiled=True),
        lax.all_gather(proj_low, ("dp", "fsdp"), axis=1, tiled=True),
        lax.all_gather(vec_master.astype(jnp.bfloat16), ("dp", "fsdp"), axis=1, tiled=True),
    )
    vectors = vec_w.astype(jnp.float32)
    model_width = vectors.shape[1]
    kernel = vectors[9:18]
    hidden_bias = vectors[18:].reshape(-1)
    states = []
    for images, cotangent, bucket_index in (
        (small_images, small_cot, 0),
        (large_images, large_cot, 1),
    ):
        grid_side = math.isqrt(images.shape[1])
        inputs = images.astype(jnp.float32)
        normed = layer_norm(inputs, vectors[0], vectors[1]).astype(jnp.bfloat16)
        joint_proj = jnp.einsum("nld,de->nle", normed, qkv_w, preferred_element_type=jnp.float32)
        query_rows = (joint_proj[..., :model_width] + vectors[2]).astype(jnp.bfloat16)
        key_rows = joint_proj[..., model_width : 2 * model_width].astype(jnp.bfloat16)
        value_rows = (joint_proj[..., 2 * model_width :] + vectors[3]).astype(jnp.bfloat16)
        mixed, log_totals = mixer_forward(
            query_rows, key_rows, value_rows, kernel, vectors[8], grid_side
        )
        mixed = mixed.astype(jnp.bfloat16)
        middle = (
            inputs
            + jnp.einsum("nle,ed->nld", mixed, proj_w, preferred_element_type=jnp.float32)
            + vectors[4]
        )
        live_mask = (jnp.arange(images.shape[0], dtype=jnp.int32) < counts[0, bucket_index]).astype(
            jnp.float32
        )[:, None, None]
        states.append(
            {
                "inputs": inputs,
                "normed": normed,
                "query": query_rows,
                "keys": key_rows,
                "value": value_rows,
                "totals": log_totals,
                "mixed": mixed,
                "middle": middle,
                "side": grid_side,
                "cotangent": cotangent,
                "live": live_mask,
            }
        )
    fc1_w, fc2_w = (
        lax.all_gather(fc1_low, ("dp", "fsdp"), axis=0, tiled=True),
        lax.all_gather(fc2_low, ("dp", "fsdp"), axis=1, tiled=True),
    )
    results = []
    for state in states:
        normed_two = layer_norm(state["middle"], vectors[5], vectors[6]).astype(jnp.bfloat16)
        hidden = (
            jnp.einsum("nld,df->nlf", normed_two, fc1_w, preferred_element_type=jnp.float32)
            + hidden_bias
        )
        active = gelu_exact(hidden).astype(jnp.bfloat16)
        result = (
            state["middle"]
            + jnp.einsum("nlf,fd->nld", active, fc2_w, preferred_element_type=jnp.float32)
            + vectors[7]
        )
        results.append((result * state["live"]).astype(jnp.bfloat16))
        state["normed_two"] = normed_two
        state["hidden"] = hidden
        state["active"] = active
    fc1_w, fc2_w = (
        lax.all_gather(fc1_low, ("dp", "fsdp"), axis=0, tiled=True),
        lax.all_gather(fc2_low, ("dp", "fsdp"), axis=1, tiled=True),
    )
    zero_row = jnp.zeros((model_width,), jnp.float32)
    vector_grads = [zero_row] * 9
    kernel_grad = jnp.zeros_like(kernel)
    hidden_bias_grad = jnp.zeros_like(hidden_bias)
    grad_fc1 = jnp.zeros(fc1_w.shape, jnp.float32)
    grad_fc2 = jnp.zeros(fc2_w.shape, jnp.float32)
    for state in states:
        grad_out = state["cotangent"].astype(jnp.float32) * state["live"]
        grad_low = grad_out.astype(jnp.bfloat16)
        grad_fc2 = grad_fc2 + jnp.einsum(
            "nlf,nld->fd", state["active"], grad_low, preferred_element_type=jnp.float32
        )
        vector_grads[7] = vector_grads[7] + jnp.sum(grad_out, axis=(0, 1))
        grad_active = jnp.einsum("nld,fd->nlf", grad_low, fc2_w, preferred_element_type=jnp.float32)
        ignored, gelu_back = jax.vjp(gelu_exact, state["hidden"])
        grad_hidden = gelu_back(grad_active)[0].astype(jnp.bfloat16)
        grad_fc1 = grad_fc1 + jnp.einsum(
            "nld,nlf->df", state["normed_two"], grad_hidden, preferred_element_type=jnp.float32
        )
        hidden_bias_grad = hidden_bias_grad + jnp.sum(grad_hidden.astype(jnp.float32), axis=(0, 1))
        grad_normed_two = jnp.einsum(
            "nlf,df->nld", grad_hidden, fc1_w, preferred_element_type=jnp.float32
        )
        ignored, norm_back = jax.vjp(layer_norm, state["middle"], vectors[5], vectors[6])
        grad_middle, gain_grad, shift_grad = norm_back(grad_normed_two)
        vector_grads[5] = vector_grads[5] + gain_grad
        vector_grads[6] = vector_grads[6] + shift_grad
        state["grad_middle"] = grad_out + grad_middle
    fc1_shard, fc2_shard = (
        lax.psum_scatter(grad_fc1, ("dp", "fsdp"), scatter_dimension=0, tiled=True),
        lax.psum_scatter(grad_fc2, ("dp", "fsdp"), scatter_dimension=1, tiled=True),
    )
    qkv_w, proj_w = (
        lax.all_gather(qkv_low, ("dp", "fsdp"), axis=0, tiled=True),
        lax.all_gather(proj_low, ("dp", "fsdp"), axis=1, tiled=True),
    )
    grad_qkv = jnp.zeros(qkv_w.shape, jnp.float32)
    grad_proj = jnp.zeros(proj_w.shape, jnp.float32)
    input_grads = []
    for state in states:
        middle_low = state["grad_middle"].astype(jnp.bfloat16)
        grad_proj = grad_proj + jnp.einsum(
            "nle,nld->ed", state["mixed"], middle_low, preferred_element_type=jnp.float32
        )
        vector_grads[4] = vector_grads[4] + jnp.sum(middle_low.astype(jnp.float32), axis=(0, 1))
        grad_mixed = jnp.einsum(
            "nld,ed->nle", middle_low, proj_w, preferred_element_type=jnp.float32
        ).astype(jnp.bfloat16)
        grad_query, grad_key, grad_value, kernel_part, offset_part = mixer_backward(
            state["query"],
            state["keys"],
            state["value"],
            state["totals"],
            grad_mixed,
            kernel,
            vectors[8],
            state["side"],
        )
        kernel_grad = kernel_grad + kernel_part
        vector_grads[8] = vector_grads[8] + offset_part
        grad_query = grad_query.astype(jnp.bfloat16)
        grad_key = grad_key.astype(jnp.bfloat16)
        grad_value = grad_value.astype(jnp.bfloat16)
        vector_grads[2] = vector_grads[2] + jnp.sum(grad_query.astype(jnp.float32), axis=(0, 1))
        vector_grads[3] = vector_grads[3] + jnp.sum(grad_value.astype(jnp.float32), axis=(0, 1))
        joint_grad = jnp.concatenate([grad_query, grad_key, grad_value], axis=-1)
        grad_qkv = grad_qkv + jnp.einsum(
            "nld,nle->de", state["normed"], joint_grad, preferred_element_type=jnp.float32
        )
        grad_normed = jnp.einsum(
            "nle,de->nld", joint_grad, qkv_w, preferred_element_type=jnp.float32
        )
        ignored, norm_back = jax.vjp(layer_norm, state["inputs"], vectors[0], vectors[1])
        grad_inputs, gain_grad, shift_grad = norm_back(grad_normed)
        vector_grads[0] = vector_grads[0] + gain_grad
        vector_grads[1] = vector_grads[1] + shift_grad
        input_grads.append(state["grad_middle"] + grad_inputs)
    grad_vec = jnp.concatenate(
        [jnp.stack(vector_grads, axis=0), kernel_grad, hidden_bias_grad.reshape(-1, model_width)],
        axis=0,
    )
    qkv_shard, proj_shard, vec_shard = (
        lax.psum_scatter(grad_qkv, ("dp", "fsdp"), scatter_dimension=0, tiled=True),
        lax.psum_scatter(grad_proj, ("dp", "fsdp"), scatter_dimension=1, tiled=True),
        lax.psum_scatter(grad_vec, ("dp", "fsdp"), scatter_dimension=1, tiled=True),
    )
    local_squares = jnp.float32(0.0)
    for gradient in (qkv_shard, proj_shard, fc1_shard, fc2_shard, vec_shard):
        local_squares = local_squares + jnp.sum(gradient * gradient)
    grad_total = jnp.sqrt(lax.psum(local_squares, ("dp", "fsdp")))
    clip_factor = jnp.minimum(1.0, clip_norm / (grad_total + 1e-06))
    qkv_new, qkv_first_new, qkv_second_new = adamw_update(
        qkv_master, qkv_first, qkv_second, qkv_shard * clip_factor, rate_matrix, decay_matrix
    )
    proj_new, proj_first_new, proj_second_new = adamw_update(
        proj_master, proj_first, proj_second, proj_shard * clip_factor, rate_matrix, decay_matrix
    )
    fc1_new, fc1_first_new, fc1_second_new = adamw_update(
        fc1_master, fc1_first, fc1_second, fc1_shard * clip_factor, rate_matrix, decay_matrix
    )
    fc2_new, fc2_first_new, fc2_second_new = adamw_update(
        fc2_master, fc2_first, fc2_second, fc2_shard * clip_factor, rate_matrix, decay_matrix
    )
    vec_new, vec_first_new, vec_second_new = adamw_update(
        vec_master, vec_first, vec_second, vec_shard * clip_factor, rate_vector, 0.0
    )
    return (
        results[0],
        results[1],
        input_grads[0],
        input_grads[1],
        qkv_new,
        qkv_first_new,
        qkv_second_new,
        qkv_new.astype(jnp.bfloat16),
        proj_new,
        proj_first_new,
        proj_second_new,
        proj_new.astype(jnp.bfloat16),
        fc1_new,
        fc1_first_new,
        fc1_second_new,
        fc1_new.astype(jnp.bfloat16),
        fc2_new,
        fc2_first_new,
        fc2_second_new,
        fc2_new.astype(jnp.bfloat16),
        vec_new,
        vec_first_new,
        vec_second_new,
        vec_new.astype(jnp.bfloat16),
        grad_total,
    )


def solution(mesh):
    return jax.shard_map(
        on_device,
        mesh=mesh,
        in_specs=(
            P(("dp", "fsdp"), None, None),
            P(("dp", "fsdp"), None, None),
            P(("dp", "fsdp"), None, None),
            P(("dp", "fsdp"), None, None),
            P(("dp", "fsdp"), None),
            P(("dp", "fsdp"), None),
            P(("dp", "fsdp"), None),
            P(("dp", "fsdp"), None),
            P(None, ("dp", "fsdp")),
            P(None, ("dp", "fsdp")),
            P(None, ("dp", "fsdp")),
            P(("dp", "fsdp"), None),
            P(("dp", "fsdp"), None),
            P(("dp", "fsdp"), None),
            P(None, ("dp", "fsdp")),
            P(None, ("dp", "fsdp")),
            P(None, ("dp", "fsdp")),
            P(None, ("dp", "fsdp")),
            P(None, ("dp", "fsdp")),
            P(None, ("dp", "fsdp")),
        ),
        out_specs=(
            P(("dp", "fsdp"), None, None),
            P(("dp", "fsdp"), None, None),
            P(("dp", "fsdp"), None, None),
            P(("dp", "fsdp"), None, None),
            P(("dp", "fsdp"), None),
            P(("dp", "fsdp"), None),
            P(("dp", "fsdp"), None),
            P(("dp", "fsdp"), None),
            P(None, ("dp", "fsdp")),
            P(None, ("dp", "fsdp")),
            P(None, ("dp", "fsdp")),
            P(None, ("dp", "fsdp")),
            P(("dp", "fsdp"), None),
            P(("dp", "fsdp"), None),
            P(("dp", "fsdp"), None),
            P(("dp", "fsdp"), None),
            P(None, ("dp", "fsdp")),
            P(None, ("dp", "fsdp")),
            P(None, ("dp", "fsdp")),
            P(None, ("dp", "fsdp")),
            P(None, ("dp", "fsdp")),
            P(None, ("dp", "fsdp")),
            P(None, ("dp", "fsdp")),
            P(None, ("dp", "fsdp")),
            P(),
        ),
        check_vma=False,
    )
```

profile of v0, /device:TPU:1, one launch (start us, length us, event | category | flops | bytes accessed | tf_op | source)
XLA Modules:
  0.0 1636.0 jit_solution(7319773651105035306)
XLA Ops:
  9.5 62.4 %all_gather.19 = bf16[22,256]{0,1:T(8,128)(2,1)S(1)} all-gather(bf16[22,8]{0,1:T(8,128)(2,1)S(1)} %convert_element_type.342), channel_id=1, replica_groups=mesh['dp'=4,'fsdp'=8] {'dp','fsdp'}, dimensions={1}, use_global_device_ids=true | all-gather | bytes 11616 | tf_op jit(solution)/shard_map/all_gather | solution.py:247
  87.9 63.0 %all_gather.21 = bf16[256,256]{0,1:T(8,128)(2,1)S(1)} all-gather(bf16[256,8]{0,1:T(8,128)(2,1)S(1)} %convert_element_type.354), channel_id=1, replica_groups=mesh['dp'=4,'fsdp'=8] {'dp','fsdp'}, dimensions={1}, use_global_device_ids=true | all-gather | bytes 135168 | tf_op jit(solution)/shard_map/all_gather | solution.py:246
  153.9 68.2 %all_gather.20 = bf16[256,768]{1,0:T(8,128)(2,1)S(1)} all-gather(bf16[8,768]{1,0:T(8,128)(2,1)} %convert_element_type.345), channel_id=1, replica_groups=mesh['dp'=4,'fsdp'=8] {'dp','fsdp'}, dimensions={0}, use_global_device_ids=true | all-gather | bytes 405504 | tf_op jit(solution)/shard_map/all_gather | solution.py:245
  222.1 71.2 %all_gather.23 = bf16[1024,256]{0,1:T(8,128)(2,1)} all-gather(bf16[1024,8]{0,1:T(8,128)(2,1)} %convert_element_type.358), channel_id=1, replica_groups=mesh['dp'=4,'fsdp'=8] {'dp','fsdp'}, dimensions={1}, use_global_device_ids=true | all-gather | bytes 540672 | tf_op jit(solution)/shard_map/all_gather | solution.py:294
  293.2 74.1 %all_gather.22 = bf16[256,1024]{1,0:T(8,128)(2,1)} all-gather(bf16[8,1024]{1,0:T(8,128)(2,1)} %convert_element_type.356), channel_id=1, replica_groups=mesh['dp'=4,'fsdp'=8] {'dp','fsdp'}, dimensions={0}, use_global_device_ids=true | all-gather | bytes 540672 | tf_op jit(solution)/shard_map/all_gather | solution.py:293
  555.7 13.9 multiply_reduce_fusion.2
  582.1 12.7 fusion.44
  619.9 14.1 multiply_reduce_fusion.3
  682.6 16.6 %fusion.37 = (u8[784,1024]{1,0:T(8,128)(4,1)S(1)}, u8[784,1024]{1,0:T(8,128)(4,1)S(1)}, f32[8,784,1024]{2,1,0:T(8,128)}) fusion(f32[1024]{0:T(1024)S(1)} %bitcast.426, bf16[256,1024]{1,0:T(8,128)(2,1)S(1)} %copy-done.123, f32[8,784,256]{2,1,0:T(8,128)S(1)} %get-tuple-element.345, f32[256]{0:T(256)S(1)} %copy-done.179, f32[256]{0:T(256)S(1)} %copy-done.153, ...), kind=kOutput, calls=%fused_computation.81 | convolution fusion | flops 3384672256 | bytes 34298880 | tf_op jit(solution)/shard_map/nld,df->nlf/dot_general | solution.py:300
  699.2 61.9 %multiply_convert_fusion.2 = (bf16[8,784,1024]{2,1,0:T(8,128)(2,1)}, f32[8,784,1024]{2,1,0:T(8,128)}) fusion(f32[8,784,1024]{2,1,0:T(8,128)} %get-tuple-element.346, f32[1024]{0:T(1024)S(1)} %bitcast.427, u8[784,1024]{1,0:T(8,128)(4,1)S(1)} %get-tuple-element.126, u8[784,1024]{1,0:T(8,128)(4,1)S(1)} %get-tuple-element.125), kind=kLoop, calls=%fused_computation.19 | loop fusion | flops 455999488 | bytes 65835008 | tf_op jit(solution)/shard_map/convert_element_type | solution.py:303
  761.2 24.9 %convert_reduce_fusion = (f32[1024]{0:T(1024)}, bf16[8,784,1024]{2,1,0:T(8,128)(2,1)}) fusion(f32[8,784,1024]{2,1,0:T(8,128)} %get-tuple-element.261, bf16[1024,256]{0,1:T(8,128)(2,1)} %all_gather.23, bf16[8,784,256]{2,1,0:T(8,128)(2,1)S(1)} %copy-done.25, f32[8]{0:T(128)S(1)} %copy-done.246, f32[8,784,1024]{2,1,0:T(8,128)} %get-tuple-element.346, ...), kind=kOutput, calls=%fused_computation.17 | convolution fusion | flops 3402333184 | bytes 67969056 | tf_op jit(solution)/shard_map/nld,fd->nlf/dot_general | solution.py:330
  786.1 14.9 multiply_reduce_fusion.4
  838.0 12.0 multiply_reduce_fusion.24
  856.3 12.4 multiply_reduce_fusion.15
  885.7 15.0 fusion.49
  900.8 19.1 %multiply_reduce_fusion = (f32[32,4,196]{2,1,0:T(4,128)S(1)}, f32[32,4,196,196]{2,3,1,0:T(8,128)}) fusion(f32[32,4,196,196]{2,3,1,0:T(8,128)} %get-tuple-element.341, f32[32,4,196]{2,1,0:T(4,128)S(1)} %bitcast.380, bf16[32,196,4,32]{1,3,2,0:T(8,128)(2,1)S(1)} %copy.492, bf16[32,196,4,32]{1,3,2,0:T(8,128)(2,1)} %copy.438), kind=kOutput, calls=%fused_computation.2 | convolution fusion | flops 334347776 | bytes 42749952 | tf_op jit(solution)/shard_map/bqhe,bkhe->bhqk/dot_general | solution.py:109
  919.9 21.8 %multiply_convert_fusion = bf16[32,4,196,196]{2,3,1,0:T(8,128)(2,1)} fusion(f32[32,4,196,196]{2,3,1,0:T(8,128)} %get-tuple-element.357, f32[32,4,196,196]{2,3,1,0:T(8,128)} %get-tuple-element.341, f32[32,4,196]{2,1,0:T(4,128)S(1)} %get-tuple-element.356, f32[32,4,196]{2,1,0:T(4,128)S(1)} %bitcast.381), kind=kLoop, calls=%fused_computation.1 | loop fusion | flops 24586240 | bytes 49373184 | tf_op jit(solution)/shard_map/convert_element_type | solution.py:113
  968.7 15.0 fusion.46
  983.7 25.6 %multiply_reduce_fusion.1 = (f32[32,4,196]{2,1,0:T(4,128)S(1)}, f32[32,4,196,196]{2,3,1,0:T(8,128)}) fusion(f32[32,4,196,196]{2,3,1,0:T(8,128)} %get-tuple-element.343, f32[32,4,196]{2,1,0:T(4,128)S(1)} %bitcast.383, bf16[32,196,4,32]{1,0,3,2:T(8,128)(2,1)} %reshape_reshape.124, bf16[32,196,4,32]{1,0,3,2:T(8,128)(2,1)S(1)} %reshape_reshape.140), kind=kOutput, calls=%fused_computation.5 | convolution fusion | flops 334347776 | bytes 42749952 | tf_op jit(solution)/shard_map/bqhe,bkhe->bhqk/dot_general | solution.py:109
  1009.3 22.0 %multiply_convert_fusion.1 = bf16[32,4,196,196]{2,3,1,0:T(8,128)(2,1)} fusion(f32[32,4,196,196]{2,3,1,0:T(8,128)} %get-tuple-element.355, f32[32,4,196,196]{2,3,1,0:T(8,128)} %get-tuple-element.343, f32[32,4,196]{2,1,0:T(4,128)S(1)} %get-tuple-element.354, f32[32,4,196]{2,1,0:T(4,128)S(1)} %bitcast.384), kind=kLoop, calls=%fused_computation.4 | loop fusion | flops 24586240 | bytes 49373184 | tf_op jit(solution)/shard_map/convert_element_type | solution.py:113
  1291.4 45.5 %all-reduce.76 = f32[22,256]{1,0:T(8,128)S(1)} all-reduce(f32[22,256]{1,0:T(8,128)S(1)} %concatenate.89), channel_id=6, replica_groups=mesh['dp'=4,'fsdp'=8] {'dp','fsdp'}, use_global_device_ids=true, to_apply=%region_94.95.clone | all-reduce | flops 5632 | bytes 45056
  1353.5 87.2 %reduce-scatter.10.cloned.1.call-done = f32[8,1024]{1,0:T(8,128)} async-done(((f32[256,1024]{1,0:T(8,128)}), f32[8,1024]{1,0:T(8,128)}) %reduce-scatter.10.cloned.1.call-update) | async-done | bytes 32784 | tf_op jit(solution)/shard_map/reduce_scatter | solution.py:346
  1442.7 131.3 %reduce-scatter.12.cloned.1.call-done = f32[1024,8]{0,1:T(8,128)} async-done(((f32[1024,256]{0,1:T(8,128)}), f32[1024,8]{0,1:T(8,128)}) %reduce-scatter.12.cloned.1.call-update) | async-done | bytes 32784 | tf_op jit(solution)/shard_map/reduce_scatter | solution.py:347
  1576.8 44.0 %psum.7 = f32[]{:T(128)} all-reduce(f32[]{:T(128)S(6)} %add.1014), channel_id=1, replica_groups=mesh['dp'=4,'fsdp'=8] {'dp','fsdp'}, use_global_device_ids=true, to_apply=%region_96.97 | all-reduce | flops 1 | bytes 8 | tf_op jit(solution)/shard_map/psum | solution.py:406
  (872 shorter events, 663.7 us)
Async XLA Ops:
  7.3 1342.3 %reduce-scatter.8.cloned.1.call-start = ((), (), s32[]{:S(2)}) async-start(), calls=%async_computation.5 | async-start | bytes 270336 | tf_op jit(solution)/shard_map/reduce_scatter | solution.py:400
  73.8 363.6 %copy-start.152 = (f32[256]{0:T(256)}, f32[256]{0:T(256)S(1)}, u32[]{:S(2)}) copy-start(f32[256]{0:T(256)S(1)} %get-tuple-element.197) | copy-start | bytes 3076
  73.8 366.5 %copy-start.150 = (f32[256]{0:T(256)}, f32[256]{0:T(256)S(1)}, u32[]{:S(2)}) copy-start(f32[256]{0:T(256)S(1)} %get-tuple-element.202) | copy-start | bytes 3076
  80.8 286.6 %copy-start.148 = (f32[2,196]{1,0:T(2,128)}, f32[2,196]{1,0:T(2,128)S(1)}, u32[]{:S(2)}) copy-start(f32[2,196]{1,0:T(2,128)S(1)} %broadcast_multiply_fusion.31) | copy-start | bytes 4708
  151.0 276.1 %copy-start.66 = (bf16[256,256]{0,1:T(8,128)(2,1)}, bf16[256,256]{0,1:T(8,128)(2,1)S(1)}, u32[]{:S(2)}) copy-start(bf16[256,256]{0,1:T(8,128)(2,1)S(1)} %all_gather.21) | copy-start | bytes 393220
  222.1 145.3 %copy-start.64 = (bf16[256,768]{1,0:T(8,128)(2,1)}, bf16[256,768]{1,0:T(8,128)(2,1)S(1)}, u32[]{:S(2)}) copy-start(bf16[256,768]{1,0:T(8,128)(2,1)S(1)} %all_gather.20) | copy-start | bytes 1179652
  812.6 538.2 %reduce-scatter.6.cloned.1.call-start = ((), (), s32[]{:S(2)}) async-start(), calls=%async_computation.4 | async-start | bytes 811008 | tf_op jit(solution)/shard_map/reduce_scatter | solution.py:399
  1212.1 228.6 %reduce-scatter.10.cloned.1.call-start = ((), (), s32[]{:S(2)}) async-start(), calls=%async_computation.6 | async-start | bytes 1081344 | tf_op jit(solution)/shard_map/reduce_scatter | solution.py:346
  1224.7 349.3 %reduce-scatter.12.cloned.1.call-start = ((), (), s32[]{:S(2)}) async-start(), calls=%async_computation.7 | async-start | bytes 1081344 | tf_op jit(solution)/shard_map/reduce_scatter | solution.py:347
  1337.5 284.0 %copy-start.177 = (f32[22,8]{0,1:T(8,128)S(1)}, f32[22,8]{0,1:T(8,128)}, u32[]{:S(2)}) copy-start(f32[22,8]{0,1:T(8,128)} %param.37) | copy-start | bytes 2116
  1337.5 284.0 %copy-start.239 = (f32[22,8]{0,1:T(8,128)S(1)}, f32[22,8]{0,1:T(8,128)}, u32[]{:S(2)}) copy-start(f32[22,8]{0,1:T(8,128)} %param.38) | copy-start | bytes 2116
  1337.5 284.0 %copy-start.240 = (f32[22,8]{0,1:T(8,128)S(1)}, f32[22,8]{0,1:T(8,128)}, u32[]{:S(2)}) copy-start(f32[22,8]{0,1:T(8,128)} %param.39) | copy-start | bytes 2116
  1337.6 284.7 %copy-start.164 = (f32[256,8]{0,1:T(8,128)S(1)}, f32[256,8]{0,1:T(8,128)}, u32[]{:S(2)}) copy-start(f32[256,8]{0,1:T(8,128)} %param.28) | copy-start | bytes 24580
  1337.6 284.7 %copy-start.225 = (f32[256,8]{0,1:T(8,128)S(1)}, f32[256,8]{0,1:T(8,128)}, u32[]{:S(2)}) copy-start(f32[256,8]{0,1:T(8,128)} %param.29) | copy-start | bytes 24580
  1337.6 284.6 %copy-start.226 = (f32[256,8]{0,1:T(8,128)S(1)}, f32[256,8]{0,1:T(8,128)}, u32[]{:S(2)}) copy-start(f32[256,8]{0,1:T(8,128)} %param.30) | copy-start | bytes 24580
  1337.6 286.0 %copy-start.143 = (f32[8,768]{1,0:T(8,128)S(1)}, f32[8,768]{1,0:T(8,128)}, u32[]{:S(2)}) copy-start(f32[8,768]{1,0:T(8,128)} %param.25) | copy-start | bytes 73732
  1337.6 286.0 %copy-start.168 = (f32[8,768]{1,0:T(8,128)S(1)}, f32[8,768]{1,0:T(8,128)}, u32[]{:S(2)}) copy-start(f32[8,768]{1,0:T(8,128)} %param.26) | copy-start | bytes 73732
  1337.6 286.0 %copy-start.169 = (f32[8,768]{1,0:T(8,128)S(1)}, f32[8,768]{1,0:T(8,128)}, u32[]{:S(2)}) copy-start(f32[8,768]{1,0:T(8,128)} %param.27) | copy-start | bytes 73732
  1337.6 287.3 %copy-start.140 = (f32[1024,8]{0,1:T(8,128)S(1)}, f32[1024,8]{0,1:T(8,128)}, u32[]{:S(2)}) copy-start(f32[1024,8]{0,1:T(8,128)} %param.34) | copy-start | bytes 98308
  1337.6 287.3 %copy-start.159 = (f32[1024,8]{0,1:T(8,128)S(1)}, f32[1024,8]{0,1:T(8,128)}, u32[]{:S(2)}) copy-start(f32[1024,8]{0,1:T(8,128)} %param.35) | copy-start | bytes 98308
  1337.7 287.3 %copy-start.160 = (f32[1024,8]{0,1:T(8,128)S(1)}, f32[1024,8]{0,1:T(8,128)}, u32[]{:S(2)}) copy-start(f32[1024,8]{0,1:T(8,128)} %param.36) | copy-start | bytes 98308
  1337.7 288.7 %copy-start.142 = (f32[8,1024]{1,0:T(8,128)S(1)}, f32[8,1024]{1,0:T(8,128)}, u32[]{:S(2)}) copy-start(f32[8,1024]{1,0:T(8,128)} %param.31) | copy-start | bytes 98308
  1337.7 288.7 %copy-start.161 = (f32[8,1024]{1,0:T(8,128)S(1)}, f32[8,1024]{1,0:T(8,128)}, u32[]{:S(2)}) copy-start(f32[8,1024]{1,0:T(8,128)} %param.32) | copy-start | bytes 98308
  1337.7 288.7 %copy-start.162 = (f32[8,1024]{1,0:T(8,128)S(1)}, f32[8,1024]{1,0:T(8,128)}, u32[]{:S(2)}) copy-start(f32[8,1024]{1,0:T(8,128)} %param.33) | copy-start | bytes 98308
  (270 other events, 2431.3 us)
Sparse Core Ops, SparseCore 0:
  812.7 129.7 reduce-scatter.7
  1212.2 98.1 reduce-scatter.5
  1312.7 127.9 reduce-scatter.9
  1442.8 131.2 reduce-scatter.11
where the time goes:
time: 1650 us; the launch traced here: 1640 us
  blocking collectives  428 us (26%)
  local copies, waits for them, and re-layouts  350 us (21%)
  matrix products  315 us (19%)
  other arithmetic  300 us (18%)
  waiting for transfers between devices  219 us (13%)
  between operations  23.2 us (1%)
    reduce_scatter x1, waiting for transfers between devices, on_device(): lax.psum_scatter(grad_fc2, ('dp', 'fsdp'), scatter_dimension=1, tiled=True)  131 us
    another operation x24, local copies, waits for them, and re-layouts, split_heads(): values.reshape(values.shape[0], values.shape[1], head_count, values.shape...  97.7 us
    reduce_scatter x1, waiting for transfers between devices, on_device(): lax.psum_scatter(grad_fc1, ('dp', 'fsdp'), scatter_dimension=0, tiled=True)  87.2 us
    all_gather x1, blocking collectives, on_device(): lax.all_gather(fc1_low, ('dp', 'fsdp'), axis=0, tiled=True)  74.1 us
    all_gather x1, blocking collectives, on_device(): lax.all_gather(fc2_low, ('dp', 'fsdp'), axis=1, tiled=True)  71.2 us
    all_gather x1, blocking collectives, on_device(): lax.all_gather(qkv_low, ('dp', 'fsdp'), axis=0, tiled=True)  68.2 us
    convert_element_type x2, other arithmetic, on_device(): active = gelu_exact(hidden).astype(jnp.bfloat16)  66.6 us
    all_gather x1, blocking collectives, on_device(): lax.all_gather(proj_low, ('dp', 'fsdp'), axis=1, tiled=True)  63 us
  transfers between devices with their start and end apart: 4, of which 2 were waited for; matrix products, arithmetic and copies ran while one was open for 29% of the time, Pallas kernels for 0%

commit v1 on v0

v1 whole, which is shorter than its diff:
```python
import functools
import math

import jax
import jax.numpy as jnp
from jax import lax
from jax.experimental import pallas as pl
from jax.experimental.pallas import tpu as pltpu
from jax.sharding import PartitionSpec as P

HEADS = 8
STRIPE = 7
STEP = 10
LANES = 128

epsilon = 1e-05
clip_norm = 1.0
beta_one = 0.5
beta_two = 0.5
rate_matrix = 0.1
rate_vector = 0.5
decay_matrix = 0.05
adam_epsilon = 1e-08

BF = jnp.bfloat16
F32 = jnp.float32
FAR = -1e30

TAIL = 0.36
TAIL_POLY = (
    0.143705181,
    0.141884706,
    0.139098811,
    0.0282579301,
    0.178465629,
    -0.177935249,
    0.0465224759,
)


def dot_nn(a, b):
    return lax.dot_general(a, b, (((1,), (0,)), ((), ())), preferred_element_type=F32)


def dot_nt(a, b):
    return lax.dot_general(a, b, (((1,), (1,)), ((), ())), preferred_element_type=F32)


def dot_tn(a, b):
    return lax.dot_general(a, b, (((0,), (0,)), ((), ())), preferred_element_type=F32)


def fold_rows(v):
    return jnp.sum(v.reshape(v.shape[0] // 8, 8, v.shape[1]), axis=0)


def row_mean(v):
    return jnp.sum(v, axis=-1, keepdims=True) * (1.0 / v.shape[-1])


def gelu_parts(u):
    magnitude = jnp.abs(u)
    t = 1.0 / (1.0 + TAIL * magnitude)
    bell = jnp.exp(-0.5 * u * u)
    poly = jnp.full_like(t, TAIL_POLY[-1])
    for c in TAIL_POLY[-2::-1]:
        poly = poly * t + c
    low_side = poly * t * bell
    phi = jnp.where(u >= 0.0, 1.0 - low_side, low_side)
    return u * phi, phi + u * bell * (1.0 / math.sqrt(2.0 * math.pi))


def shift_down(v, n):
    return jnp.concatenate([jnp.zeros((n, v.shape[1]), v.dtype), v[:-n]], axis=0)


def shift_up(v, n):
    return jnp.concatenate([v[n:], jnp.zeros((n, v.shape[1]), v.dtype)], axis=0)


class Shape:
    def __init__(self, side):
        self.side = side
        self.wide = -(-side // 16) * 16
        self.stripes = side // STRIPE
        self.rows = STRIPE * self.wide
        self.queries = -(-self.rows // LANES) * LANES
        self.all = side * self.wide
        self.deep = -(-self.all // LANES) * LANES
        self.square = self.wide * self.wide

    def scratch(self, d, ff):
        s = self
        both = 2 * s.stripes
        return {
            "raw": ((s.side * s.side, d), F32),
            "x": ((s.all, d), F32),
            "gy": ((s.all, d), F32),
            "n1": ((s.all, d), F32),
            "r1": ((s.all, LANES), F32),
            "out": ((s.all, d), F32),
            "dx1": ((s.all, d), F32),
            "tq": ((3, s.square, LANES), F32),
            "o": ((s.all + s.square, LANES), F32),
            "dq": ((3, s.all + s.square, LANES), F32),
            "tb": ((3, s.all, LANES), BF),
            "q": ((both, s.queries, 2 * LANES), BF),
            "k": ((both, s.queries, 2 * LANES), BF),
            "v": ((both, s.queries, LANES), BF),
            "da": ((both, s.queries, LANES), BF),
            "p": ((both, HEADS // 2, s.queries, s.queries), BF),
            "ds": ((HEADS // 2, s.queries, s.queries), BF),
            "h1": ((s.deep, d), BF),
            "a": ((s.deep, d), BF),
            "h2": ((s.deep, d), BF),
            "gyb": ((s.deep, d), BF),
            "e1": ((s.deep, d), BF),
            "z": ((s.deep, ff), BF),
            "du": ((s.deep, ff), BF),
            "dqkv": ((s.deep, 3 * d), BF),
        }


def head_masks(width):
    lane = lax.broadcasted_iota(jnp.int32, (1, width), 1)
    e = LANES // (HEADS // 2)
    return [
        jnp.where((lane // e == h) | (lane == LANES), 1.0, 0.0).astype(BF)
        for h in range(HEADS // 2)
    ]


def pick_heads(parts):
    e = LANES // (HEADS // 2)
    lane = lax.broadcasted_iota(jnp.int32, parts[0].shape, 1)
    out = parts[-1]
    for h in range(len(parts) - 2, -1, -1):
        out = jnp.where(lane < (h + 1) * e, parts[h], out)
    return out


def place_mask(s, width):
    row = lax.broadcasted_iota(jnp.int32, (s.rows, width), 0)
    return lax.rem(row, s.wide) < s.side


def start_scratch(s, b):
    for name in ("x", "gy", "tq", "o", "dq", "tb", "q", "k", "v", "da", "p", "ds"):
        b[name][...] = jnp.zeros(b[name].shape, b[name].dtype)
    for name in ("h1", "a", "h2", "gyb", "e1", "z", "du", "dqkv"):
        if s.deep > s.all:
            tail = (s.deep - s.all, b[name].shape[1])
            b[name][s.all :, :] = jnp.zeros(tail, BF)
    lane = lax.broadcasted_iota(jnp.int32, (s.rows, LANES), 1)
    one = jnp.where(lane == 0, 1.0, 0.0)
    far = jnp.where((lane == 0) & ~place_mask(s, LANES), FAR, 0.0)
    for sb in range(2 * s.stripes):
        b["q"][sb, 0 : s.rows, LANES:] = one.astype(BF)
        b["k"][sb, 0 : s.rows, LANES:] = far.astype(BF)


def conv_rows(v, taps, s, flip):
    before = pltpu.roll(v, 1, 0)
    after = pltpu.roll(v, v.shape[0] - 1, 0)
    sides = (after, v, before) if flip else (before, v, after)
    mixed = []
    for a in range(3):
        mixed.append(sides[0] * taps[a][0] + sides[1] * taps[a][1] + sides[2] * taps[a][2])
    if flip:
        return mixed[1] + shift_down(mixed[2], s.wide) + shift_up(mixed[0], s.wide)
    return mixed[1] + shift_down(mixed[0], s.wide) + shift_up(mixed[2], s.wide)


def image_step(s, b, x_ref, cot_ref, y_ref, dx_ref, w_ref, g_ref, vec, kern, gv, gk, gb1):
    d = x_ref.shape[-1]
    ff = 4 * d
    heads = HEADS // 2
    e = LANES // heads
    scale = e**-0.5
    o_qkv, o_proj, o_fc1, o_fc2 = 0, 3 * d, 4 * d, 4 * d + ff
    mask = place_mask(s, LANES)

    def rows_of(t):
        return pl.ds(pl.multiple_of(t * s.rows, 16), s.rows)

    for src, dst in ((x_ref, "x"), (cot_ref, "gy")):
        b["raw"][...] = src[0].astype(F32)
        for r in range(s.side):
            b[dst][r * s.wide : r * s.wide + s.side, :] = b["raw"][
                r * s.side : (r + 1) * s.side, :
            ]

    def phase_a(t, carry):
        rows = rows_of(t)
        x = b["x"][rows, :]
        centered = x - row_mean(x)
        inverse = lax.rsqrt(row_mean(centered * centered) + epsilon)
        n1 = centered * inverse
        b["n1"][rows, :] = n1
        b["r1"][rows, :] = jnp.broadcast_to(inverse, (s.rows, LANES))
        h1 = (n1 * vec[0:1, :] + vec[1:2, :]).astype(BF)
        b["h1"][rows, :] = h1
        joint = dot_nn(h1, w_ref[:, o_qkv : o_qkv + 3 * d])
        q = joint[:, 0:d] + vec[2:3, :]
        k = joint[:, d : 2 * d]
        v = joint[:, 2 * d :] + vec[3:4, :]
        b["q"][t, 0 : s.rows, 0:LANES] = q[:, 0:LANES].astype(BF)
        b["k"][t, 0 : s.rows, 0:LANES] = k[:, 0:LANES].astype(BF)
        b["v"][t, 0 : s.rows, :] = jnp.where(mask, v[:, 0:LANES], 0.0).astype(BF)
        b["tq"][0, rows, :] = q[:, LANES:]
        b["tq"][1, rows, :] = k[:, LANES:]
        b["tq"][2, rows, :] = v[:, LANES:]
        return carry

    lax.fori_loop(0, s.stripes, phase_a, 0)

    for which, name in enumerate(("q", "k", "v")):
        for c in range(s.side):
            piece = b["tq"][which, pl.ds(c, s.wide, stride=s.wide), :]
            b[name][
                s.stripes + c // STRIPE,
                s.wide * (c % STRIPE) : s.wide * (c % STRIPE + 1),
                0:LANES,
            ] = piece.astype(BF)

    def taps_of(branch):
        rows9 = kern[branch]
        return [[rows9[3 * a + c : 3 * a + c + 1, :] for c in range(3)] for a in range(3)], rows9[
            9:10, :
        ]

    masks_wide = head_masks(2 * LANES)
    masks_one = head_masks(LANES)

    def phase_b(sb, carry):
        q = b["q"][sb]
        k = b["k"][sb, 0 : s.rows, :]
        k4 = jnp.concatenate([k * m for m in masks_wide], axis=0)
        s4 = dot_nt(k4, q)
        v = b["v"][sb].astype(F32)
        vt = jnp.transpose(v).astype(BF)
        parts = []
        for h in range(heads):
            sh = s4[h * s.rows : (h + 1) * s.rows, :]
            top = jnp.max(sh, axis=0, keepdims=True)
            ex = jnp.exp((sh - top) * scale)
            total = jnp.sum(ex, axis=0, keepdims=True)
            b["p"][sb, h, 0 : s.rows, :] = (ex * (1.0 / total)).astype(BF)
            parts.append(dot_nn(vt[h * e : (h + 1) * e, :], b["p"][sb, h]))
        o = jnp.transpose(jnp.concatenate(parts, axis=0))[0 : s.rows, :]
        taps, offset = taps_of(sb // s.stripes)
        pos = conv_rows(v[0 : s.rows, :], taps, s, False) + offset
        b["o"][rows_of(sb), :] = o + pos
        return carry

    lax.fori_loop(0, 2 * s.stripes, phase_b, 0)

    def turn_back(src_at, dst_at):
        for r in range(s.side):
            piece = src_at(pl.ds(s.all + r, s.wide, stride=s.wide))
            dst_at(slice(s.wide * r, s.wide * (r + 1)), piece.astype(BF))

    def put_a(rows, piece):
        b["a"][rows, LANES:] = piece

    turn_back(lambda rows: b["o"][rows, :], put_a)

    def phase_c(t, carry):
        rows = rows_of(t)
        b["a"][rows, 0:LANES] = b["o"][rows, :].astype(BF)
        x1 = b["x"][rows, :] + dot_nt(b["a"][rows, :], w_ref[:, o_proj : o_proj + d]) + vec[4:5, :]
        centered = x1 - row_mean(x1)
        inverse = lax.rsqrt(row_mean(centered * centered) + epsilon)
        n2 = centered * inverse
        h2 = (n2 * vec[5:6, :] + vec[6:7, :]).astype(BF)
        b["h2"][rows, :] = h2
        gy = b["gy"][rows, :]
        gyb = gy.astype(BF)
        b["gyb"][rows, :] = gyb
        out = x1 + vec[7:8, :]
        dh2 = jnp.zeros((s.rows, d), F32)
        for j in range(4):
            c1 = slice(o_fc1 + j * d, o_fc1 + (j + 1) * d)
            c2 = slice(o_fc2 + j * d, o_fc2 + (j + 1) * d)
            cj = slice(j * d, (j + 1) * d)
            u = dot_nn(h2, w_ref[:, c1]) + vec[18 + j : 19 + j, :]
            z, slope = gelu_parts(u)
            z = z.astype(BF)
            b["z"][rows, cj] = z
            out = out + dot_nt(z, w_ref[:, c2])
            du = (dot_nn(gyb, w_ref[:, c2]) * slope).astype(BF)
            b["du"][rows, cj] = du
            dh2 = dh2 + dot_nt(du, w_ref[:, c1])
            gb1[j] += fold_rows(du.astype(F32))
        b["out"][rows, :] = out
        dn = dh2 * vec[5:6, :]
        dx1 = gy + inverse * (dn - row_mean(dn) - n2 * row_mean(dn * n2))
        b["dx1"][rows, :] = dx1
        e1 = dx1.astype(BF)
        b["e1"][rows, :] = e1
        gv[5] += fold_rows(dh2 * n2)
        gv[6] += fold_rows(dh2)
        gv[7] += fold_rows(gy)
        gv[4] += fold_rows(e1.astype(F32))
        da = dot_nn(e1, w_ref[:, o_proj : o_proj + d])
        b["da"][t, 0 : s.rows, :] = da[:, 0:LANES].astype(BF)
        b["tq"][0, rows, :] = da[:, LANES:]
        return carry

    lax.fori_loop(0, s.stripes, phase_c, 0)

    for r in range(s.side):
        b["raw"][r * s.side : (r + 1) * s.side, :] = b["out"][
            r * s.wide : r * s.wide + s.side, :
        ]
    y_ref[0] = b["raw"][...].astype(BF)

    for c in range(s.side):
        piece = b["tq"][0, pl.ds(c, s.wide, stride=s.wide), :]
        b["da"][
            s.stripes + c // STRIPE, s.wide * (c % STRIPE) : s.wide * (c % STRIPE + 1), :
        ] = piece.astype(BF)

    def phase_d(sb, carry):
        branch = sb // s.stripes
        v = b["v"][sb, 0 : s.rows, :]
        da = b["da"][sb]
        v4 = jnp.concatenate([v * m for m in masks_one], axis=0)
        dp4 = dot_nt(v4, da)
        kt = jnp.transpose(b["k"][sb, :, 0:LANES].astype(F32)).astype(BF)
        parts = []
        for h in range(heads):
            ph = b["p"][sb, h, 0 : s.rows, :].astype(F32)
            pd = ph * dp4[h * s.rows : (h + 1) * s.rows, :]
            inner = jnp.sum(pd, axis=0, keepdims=True)
            b["ds"][h, 0 : s.rows, :] = (pd - ph * inner).astype(BF)
            parts.append(dot_nn(kt[h * e : (h + 1) * e, :], b["ds"][h]))
        dq = jnp.transpose(jnp.concatenate(parts, axis=0))[0 : s.rows, :] * scale
        ds4 = jnp.concatenate([b["ds"][h, 0 : s.rows, :] for h in range(heads)], axis=0)
        dk4 = dot_nn(ds4, b["q"][sb, :, 0:LANES])
        dk = pick_heads([dk4[h * s.rows : (h + 1) * s.rows, :] for h in range(heads)]) * scale
        p4 = jnp.concatenate([b["p"][sb, h, 0 : s.rows, :] for h in range(heads)], axis=0)
        dv4 = dot_nn(p4, da)
        dv = pick_heads([dv4[h * s.rows : (h + 1) * s.rows, :] for h in range(heads)])
        taps, offset = taps_of(branch)
        dac = da[0 : s.rows, :].astype(F32)
        vf = v.astype(F32)
        dv = jnp.where(mask, dv + conv_rows(dac, taps, s, True), 0.0)
        rows = rows_of(sb)
        b["dq"][0, rows, :] = dq
        b["dq"][1, rows, :] = dk
        b["dq"][2, rows, :] = dv
        sides = (pltpu.roll(vf, 1, 0), vf, pltpu.roll(vf, s.rows - 1, 0))
        for c in range(3):
            gk[branch, c] += fold_rows(dac[s.wide :] * sides[c][: -s.wide])
            gk[branch, 3 + c] += fold_rows(dac * sides[c])
            gk[branch, 6 + c] += fold_rows(dac[: -s.wide] * sides[c][s.wide :])
        gk[branch, 9] += fold_rows(dac)
        return carry

    lax.fori_loop(0, 2 * s.stripes, phase_d, 0)

    for which in range(3):

        def put_b(rows, piece, which=which):
            b["dqkv"][rows, which * d + LANES : (which + 1) * d] = piece

        turn_back(lambda rows, which=which: b["dq"][which, rows, :], put_b)

    def phase_e(t, carry):
        rows = rows_of(t)
        for which in range(3):
            b["dqkv"][rows, which * d : which * d + LANES] = b["dq"][which, rows, :].astype(BF)
        dqkv = b["dqkv"][rows, :]
        gv[2] += fold_rows(dqkv[:, 0:d].astype(F32))
        gv[3] += fold_rows(dqkv[:, 2 * d :].astype(F32))
        dh1 = dot_nt(dqkv, w_ref[:, o_qkv : o_qkv + 3 * d])
        n1 = b["n1"][rows, :]
        r1 = b["r1"][rows, :]
        dn = dh1 * vec[0:1, :]
        back = dn - row_mean(dn) - n1 * row_mean(dn * n1)
        b["out"][rows, :] = b["dx1"][rows, :] + back * jnp.concatenate([r1, r1], axis=1)
        gv[0] += fold_rows(dh1 * n1)
        gv[1] += fold_rows(dh1)
        return carry

    lax.fori_loop(0, s.stripes, phase_e, 0)

    for r in range(s.side):
        dx_ref[0, r * s.side : (r + 1) * s.side, :] = b["out"][
            r * s.wide : r * s.wide + s.side, :
        ]

    for left, right, start, width in (
        ("h1", "dqkv", o_qkv, 3 * d),
        ("e1", "a", o_proj, d),
        ("h2", "du", o_fc1, ff),
        ("gyb", "z", o_fc2, ff),
    ):
        turned = b[left][...]
        for j in range(0, width, d):
            g_ref[:, start + j : start + j + d] += dot_tn(turned, b[right][:, j : j + d])


def block_kernel(names, sizes, small, large, counts, xs, xl, cs, cl, w_ref, *rest):
    ys, yl, ds, dl, g_ref = rest[:5]
    vec, kern, gv, gk, gb1 = rest[5:10]
    scratch = rest[10:]
    few = dict(zip(names[: sizes[0]], scratch[: sizes[0]]))
    many = dict(zip(names[sizes[0] :], scratch[sizes[0] :]))
    step = pl.program_id(0)
    d = xs.shape[-1]
    small_steps = sizes[1]
    small_shape, large_shape = small, large

    @pl.when(step == 0)
    def _():
        start_scratch(small_shape, few)
        start_scratch(large_shape, many)
        for ref in (gv, gk, gb1, g_ref):
            ref[...] = jnp.zeros(ref.shape, ref.dtype)
        vec[...] = jnp.transpose(w_ref[:, 12 * d :].astype(F32))[0:32, :]
        for branch in range(2):
            lanes = slice(branch * LANES, (branch + 1) * LANES)
            for a in range(3):
                for c in range(3):
                    row = 9 + (3 * c + a if branch else 3 * a + c)
                    kern[branch, 3 * a + c : 3 * a + c + 1, :] = vec[row : row + 1, lanes]
            kern[branch, 9:10, :] = vec[8:9, lanes]

    def one(s, b, slot, live, x_ref, cot_ref, y_ref, dx_ref):
        @pl.when(slot < live)
        def _():
            image_step(s, b, x_ref, cot_ref, y_ref, dx_ref, w_ref, g_ref, vec, kern, gv, gk, gb1)

        @pl.when(slot >= live)
        def _():
            y_ref[...] = jnp.zeros(y_ref.shape, y_ref.dtype)
            dx_ref[...] = jnp.zeros(dx_ref.shape, dx_ref.dtype)

    @pl.when(step < small_steps)
    def _():
        one(small_shape, few, step, counts[0, 0], xs, cs, ys, ds)

    @pl.when(step >= small_steps)
    def _():
        one(large_shape, many, step - small_steps, counts[0, 1], xl, cl, yl, dl)

    @pl.when(step == pl.num_programs(0) - 1)
    def _():
        rows = []
        for i in range(8):
            rows.append(jnp.sum(gv[i], axis=0, keepdims=True))

        def taps_row(index, branch):
            return jnp.sum(gk[branch, index], axis=0, keepdims=True)

        rows.append(jnp.concatenate([taps_row(9, 0), taps_row(9, 1)], axis=1))
        for a in range(3):
            for c in range(3):
                rows.append(
                    jnp.concatenate([taps_row(3 * a + c, 0), taps_row(3 * c + a, 1)], axis=1)
                )
        for j in range(4):
            rows.append(jnp.sum(gb1[j], axis=0, keepdims=True))
        rows.append(jnp.zeros((LANES - len(rows), d), F32))
        g_ref[:, 12 * d :] = jnp.transpose(jnp.concatenate(rows, axis=0))


def run_block(small_images, large_images, small_cot, large_cot, counts, weights):
    few, small_cells, d = small_images.shape
    many, large_cells, _ = large_images.shape
    small = Shape(math.isqrt(small_cells))
    large = Shape(math.isqrt(large_cells))
    width = weights.shape[1]
    small_scratch = small.scratch(d, 4 * d)
    large_scratch = large.scratch(d, 4 * d)
    names = tuple(small_scratch) + tuple(large_scratch)
    spaces = [
        pltpu.VMEM(shape, dtype)
        for shape, dtype in list(small_scratch.values()) + list(large_scratch.values())
    ]

    def small_at(i):
        return (jnp.minimum(i, few - 1), 0, 0)

    def large_at(i):
        return (jnp.maximum(i - few, 0), 0, 0)

    small_block = pl.BlockSpec((1, small_cells, d), small_at)
    large_block = pl.BlockSpec((1, large_cells, d), large_at)
    whole = pl.BlockSpec((d, width), lambda i: (0, 0), pipeline_mode=pl.Buffered(1))
    return pl.pallas_call(
        functools.partial(block_kernel, names, (len(small_scratch), few), small, large),
        grid=(few + many,),
        in_specs=[
            pl.BlockSpec(memory_space=pltpu.SMEM),
            small_block,
            large_block,
            small_block,
            large_block,
            whole,
        ],
        out_specs=[small_block, large_block, small_block, large_block, whole],
        out_shape=[
            jax.ShapeDtypeStruct(small_images.shape, BF),
            jax.ShapeDtypeStruct(large_images.shape, BF),
            jax.ShapeDtypeStruct(small_images.shape, F32),
            jax.ShapeDtypeStruct(large_images.shape, F32),
            jax.ShapeDtypeStruct((d, width), F32),
        ],
        scratch_shapes=[
            pltpu.VMEM((32, d), F32),
            pltpu.VMEM((2, 16, LANES), F32),
            pltpu.VMEM((8, 8, d), F32),
            pltpu.VMEM((2, 16, 8, LANES), F32),
            pltpu.VMEM((4, 8, d), F32),
        ]
        + spaces,
        compiler_params=pltpu.CompilerParams(
            dimension_semantics=("arbitrary",), vmem_limit_bytes=60 * 2**20
        ),
    )(counts, small_images, large_images, small_cot, large_cot, weights)


def adamw_update(weight, first, second, gradient, rate, decay):
    first = beta_one * first + (1.0 - beta_one) * gradient
    second = beta_two * second + (1.0 - beta_two) * gradient * gradient
    first_hat = first / (1.0 - beta_one**STEP)
    second_hat = second / (1.0 - beta_two**STEP)
    weight = weight - rate * (first_hat / (jnp.sqrt(second_hat) + adam_epsilon) + decay * weight)
    return (weight, first, second)


AXES = ("dp", "fsdp")


def on_device(
    small_images,
    large_images,
    small_cot,
    large_cot,
    counts,
    *state,
):
    masters = [state[i] for i in range(0, 15, 3)]
    turned = (False, True, False, True, True)
    d = small_images.shape[-1]
    own = [m.T if t else m for m, t in zip(masters, turned)]
    shard_rows = own[0].shape[0]
    pad = jnp.zeros((shard_rows, LANES - own[4].shape[1]), F32)
    packed = jnp.concatenate(own + [pad], axis=1).astype(BF)
    weights = lax.all_gather(packed, AXES, axis=0, tiled=True)
    small_out, large_out, small_back, large_back, grads = run_block(
        small_images, large_images, small_cot, large_cot, counts, weights
    )
    shard = lax.psum_scatter(grads, AXES, scatter_dimension=0, tiled=True)
    total = jnp.sqrt(lax.psum(jnp.sum(shard * shard), AXES))
    clip_factor = jnp.minimum(1.0, clip_norm / (total + 1e-06))
    outs = [small_out, large_out, small_back, large_back]
    place = 0
    for i, t in enumerate(turned):
        master, first, second = state[3 * i : 3 * i + 3]
        width = own[i].shape[1]
        part = shard[:, place : place + width]
        place += width
        grad = (part.T if t else part) * clip_factor
        rate, decay = (rate_vector, 0.0) if i == 4 else (rate_matrix, decay_matrix)
        new, first_new, second_new = adamw_update(master, first, second, grad, rate, decay)
        outs += [new, first_new, second_new, new.astype(BF)]
    return (*outs, total)


def solution(mesh):
    cells = P(AXES, None, None)
    rows = P(AXES, None)
    columns = P(None, AXES)
    weights = [rows, columns, rows, columns, columns]
    return jax.shard_map(
        on_device,
        mesh=mesh,
        in_specs=(cells,) * 4 + (rows,) + tuple(w for w in weights for _ in range(3)),
        out_specs=(cells,) * 4 + tuple(w for w in weights for _ in range(4)) + (P(),),
        check_vma=False,
    )
```

time: 1650 us -> 530 us (0.32)
  blocking collectives: 428 us -> 40.2 us
  local copies, waits for them, and re-layouts: 350 us -> 6.57 us
  matrix products: 315 us -> 0 us
  other arithmetic: 300 us -> 12.4 us
  Pallas kernels: 0 us -> 256 us
  waiting for transfers between devices: 219 us -> 198 us
    all_gather x5 -> x0, blocking collectives: 339 us -> none  [the longest x1 74.1 us: on_device(): lax.all_gather(fc1_low, ('dp', 'fsdp'), axis=0, tiled=True)]
    dot_general x48 -> x0, matrix products: 315 us -> none  [the longest x4 45.6 us: attend_backward(): jnp.einsum('bqhe,bkhe->bhqk', grad_mixed, value_rows, preferred_element_t...]
    pallas_call x0 -> x1, Pallas kernels: none -> 256 us  [run_block(): pl.pallas_call(functools.partial(block_kernel, names, (len(small_scratch)...]
    reduce_scatter x4 -> x0, waiting for transfers between devices: 219 us -> none  [the longest x1 131 us: on_device(): lax.psum_scatter(grad_fc2, ('dp', 'fsdp'), scatter_dimension=1, tiled=True)]
    another operation x48 -> x0, local copies, waits for them, and re-layouts: 181 us -> none  [the longest x24 97.7 us: split_heads(): values.reshape(values.shape[0], values.shape[1], head_count, values.shape...]
    unnamed x4 -> x3, waiting for transfers between devices: 0.07 us -> 143 us
    convert_element_type x28 -> x5, other arithmetic: 137 us -> 7.2 us  [on_device(): outs += [new, first_new, second_new, new.astype(BF)]]
    reduce_sum x32 -> x1, other arithmetic: 105 us -> 1.52 us  [on_device(): total = jnp.sqrt(lax.psum(jnp.sum(shard * shard), AXES))]
  transfers between devices with their start and end apart: 4 -> 2, of which waited for: 2 -> 2; matrix products, arithmetic and copies ran while one was open for 29% -> 1% of each run, Pallas kernels for 0% -> 0%
where the time goes in v1:
time: 530 us; the launch traced here: 529 us
  Pallas kernels  256 us (48%)
  waiting for transfers between devices  198 us (37%)
  blocking collectives  40.2 us (8%)
  between operations  16.1 us (3%)
  other arithmetic  12.4 us (2%)
  local copies, waits for them, and re-layouts  6.57 us (1%)
    pallas_call x1, Pallas kernels, run_block(): pl.pallas_call(functools.partial(block_kernel, names, (len(small_scratch)...  256 us
    unnamed x3, waiting for transfers between devices  143 us
    all_gather x1, waiting for transfers between devices, on_device(): weights = lax.all_gather(packed, AXES, axis=0, tiled=True)  54.6 us
    psum x1, blocking collectives, on_device(): total = jnp.sqrt(lax.psum(jnp.sum(shard * shard), AXES))  40.2 us
  transfers between devices with their start and end apart: 2, of which 2 were waited for; matrix products, arithmetic and copies ran while one was open for 1% of the time, Pallas kernels for 0%

profile of v1, /device:TPU:1, one launch (start us, length us, event | category | flops | bytes accessed | tf_op | source)
XLA Modules:
  0.0 528.6 jit_solution(10492174172626921856)
XLA Ops:
  7.2 0.0 all-gather.2.cloned.1.call-start
  7.2 0.7 convert.20
  8.0 0.7 convert_bitcast_fusion.1
  8.7 0.8 convert.22
  9.4 0.8 convert_bitcast_fusion
  10.2 0.7 convert_bitcast_fusion.2
  10.9 0.7 concatenate.4
  11.6 0.0 all-reduce.3.cloned.1.call-start
  11.7 1.6 copy.49.xs
  13.3 1.6 copy.50.cs
  15.0 54.6 %all-gather.2.cloned.1.call-done.w_ref = bf16[256,3200]{1,0:T(8,128)(2,1)} async-done(((bf16[8,3200]{1,0:T(8,128)(2,1)}), bf16[256,3200]{1,0:T(8,128)(2,1)}) %all-gather.2.cloned.1.call-update) | async-done | bytes 1638416 | tf_op jit(solution)/shard_map/all_gather | solution.py:553
  69.5 255.5 %shard_map.387 = (bf16[2,196,256]{2,1,0:T(8,128)(2,1)}, bf16[8,784,256]{2,1,0:T(8,128)(2,1)}, f32[2,196,256]{2,1,0:T(8,128)}, f32[8,784,256]{2,1,0:T(8,128)}, f32[256,3200]{1,0:T(8,128)}) custom-call(s32[1,2]{1,0:T(1,128)} %counts.1, bf16[2,196,256]{2,1,0:T(8,128)(2,1)} %copy.49.xs, bf16[8,784,256]{2,1,0:T(8,128)(2,1)} %xl.1, bf16[2,196,256]{2,1,0:T(8,128)(2,1)} %copy.50.cs, ...), custom_call_target="tpu_custom_call" | custom-call | tf_op jit(solution)/shard_map/pallas_call | solution.py:493
  325.2 0.0 all-reduce.3.cloned.1.call-update
  325.3 0.7 copy-done.1
  326.0 0.8 copy.51
  326.8 143.1 %all-reduce.3.cloned.1.call-done = f32[256,3200]{1,0:T(8,128)} async-done(((f32[256,3200]{1,0:T(8,128)}), f32[256,3200]{1,0:T(8,128)}) %all-reduce.3.cloned.1.call-update) | async-done | bytes 3276816
  469.9 1.5 fusion
  471.4 1.0 copy.52
  472.4 40.2 %psum.7 = f32[]{:T(128)} all-reduce(f32[]{:T(128)} %fusion), channel_id=1, replica_groups=mesh['dp'=4,'fsdp'=8] {'dp','fsdp'}, use_global_device_ids=true, to_apply=%region_2.0 | all-reduce | flops 1 | bytes 8 | tf_op jit(solution)/shard_map/psum | solution.py:558
  513.4 1.4 fusion.17
  514.8 1.4 fusion.15
  516.2 1.5 fusion.13
  517.7 1.5 fusion.11
  519.3 1.4 fusion.9
  (35 shorter events, 0.1 us)
Async XLA Ops:
  7.2 62.3 %all-gather.2.cloned.1.call-start = ((), (), s32[]{:S(2)}) async-start(), calls=%async_computation | async-start | bytes 1689600 | tf_op jit(solution)/shard_map/all_gather | solution.py:553
  11.6 458.3 %all-reduce.3.cloned.1.call-start = ((), (), s32[]{:S(2)}) async-start(), calls=%async_computation.1 | async-start | bytes 6553600
  325.0 0.9 copy-start.1
  325.0 146.4 %copy-start = (f32[2,196,256]{2,1,0:T(8,128)S(1)}, f32[2,196,256]{2,1,0:T(8,128)}, u32[]{:S(2)}) copy-start(f32[2,196,256]{2,1,0:T(8,128)} %get-tuple-element.62) | copy-start | bytes 1204228
  325.1 188.3 %copy-start.4 = (f32[8,768]{1,0:T(8,128)S(1)}, f32[8,768]{1,0:T(8,128)}, u32[]{:S(2)}) copy-start(f32[8,768]{1,0:T(8,128)} %param.25) | copy-start | bytes 73732
  325.1 188.3 %copy-start.10 = (f32[8,768]{1,0:T(8,128)S(1)}, f32[8,768]{1,0:T(8,128)}, u32[]{:S(2)}) copy-start(f32[8,768]{1,0:T(8,128)} %param.26) | copy-start | bytes 73732
  325.1 188.3 %copy-start.11 = (f32[8,768]{1,0:T(8,128)S(1)}, f32[8,768]{1,0:T(8,128)}, u32[]{:S(2)}) copy-start(f32[8,768]{1,0:T(8,128)} %param.27) | copy-start | bytes 73732
  325.1 189.7 %copy-start.9 = (f32[256,8]{0,1:T(8,128)S(1)}, f32[256,8]{0,1:T(8,128)}, u32[]{:S(2)}) copy-start(f32[256,8]{0,1:T(8,128)} %param.28) | copy-start | bytes 24580
  325.1 189.7 %copy-start.13 = (f32[256,8]{0,1:T(8,128)S(1)}, f32[256,8]{0,1:T(8,128)}, u32[]{:S(2)}) copy-start(f32[256,8]{0,1:T(8,128)} %param.29) | copy-start | bytes 24580
  325.1 189.7 %copy-start.14 = (f32[256,8]{0,1:T(8,128)S(1)}, f32[256,8]{0,1:T(8,128)}, u32[]{:S(2)}) copy-start(f32[256,8]{0,1:T(8,128)} %param.30) | copy-start | bytes 24580
  325.1 191.1 %copy-start.2 = (f32[8,1024]{1,0:T(8,128)S(1)}, f32[8,1024]{1,0:T(8,128)}, u32[]{:S(2)}) copy-start(f32[8,1024]{1,0:T(8,128)} %param.31) | copy-start | bytes 98308
  325.1 191.1 %copy-start.5 = (f32[8,1024]{1,0:T(8,128)S(1)}, f32[8,1024]{1,0:T(8,128)}, u32[]{:S(2)}) copy-start(f32[8,1024]{1,0:T(8,128)} %param.32) | copy-start | bytes 98308
  325.1 191.1 %copy-start.6 = (f32[8,1024]{1,0:T(8,128)S(1)}, f32[8,1024]{1,0:T(8,128)}, u32[]{:S(2)}) copy-start(f32[8,1024]{1,0:T(8,128)} %param.33) | copy-start | bytes 98308
  325.2 192.6 %copy-start.3 = (f32[1024,8]{0,1:T(8,128)S(1)}, f32[1024,8]{0,1:T(8,128)}, u32[]{:S(2)}) copy-start(f32[1024,8]{0,1:T(8,128)} %param.34) | copy-start | bytes 98308
  325.2 192.6 %copy-start.7 = (f32[1024,8]{0,1:T(8,128)S(1)}, f32[1024,8]{0,1:T(8,128)}, u32[]{:S(2)}) copy-start(f32[1024,8]{0,1:T(8,128)} %param.35) | copy-start | bytes 98308
  325.2 192.6 %copy-start.8 = (f32[1024,8]{0,1:T(8,128)S(1)}, f32[1024,8]{0,1:T(8,128)}, u32[]{:S(2)}) copy-start(f32[1024,8]{0,1:T(8,128)} %param.36) | copy-start | bytes 98308
  325.2 194.1 %copy-start.12 = (f32[22,8]{0,1:T(8,128)S(1)}, f32[22,8]{0,1:T(8,128)}, u32[]{:S(2)}) copy-start(f32[22,8]{0,1:T(8,128)} %param.37) | copy-start | bytes 2116
  325.2 194.0 %copy-start.15 = (f32[22,8]{0,1:T(8,128)S(1)}, f32[22,8]{0,1:T(8,128)}, u32[]{:S(2)}) copy-start(f32[22,8]{0,1:T(8,128)} %param.38) | copy-start | bytes 2116
  325.2 194.0 %copy-start.16 = (f32[22,8]{0,1:T(8,128)S(1)}, f32[22,8]{0,1:T(8,128)}, u32[]{:S(2)}) copy-start(f32[22,8]{0,1:T(8,128)} %param.39) | copy-start | bytes 2116
Sparse Core Ops, SparseCore 0:
  11.8 57.7 all-gather.1
  325.4 144.4 all-reduce.2

commit v2 on v1

--- a/solution.py
+++ b/solution.py
@@ -25,17 +25,7 @@
 BF = jnp.bfloat16
 F32 = jnp.float32
 FAR = -1e30
-
-TAIL = 0.36
-TAIL_POLY = (
-    0.143705181,
-    0.141884706,
-    0.139098811,
-    0.0282579301,
-    0.178465629,
-    -0.177935249,
-    0.0465224759,
-)
+SKIP = set()
 
 
 def dot_nn(a, b):
@@ -59,14 +49,8 @@
 
 
 def gelu_parts(u):
-    magnitude = jnp.abs(u)
-    t = 1.0 / (1.0 + TAIL * magnitude)
+    phi = 0.5 * lax.erf(u * math.sqrt(0.5)) + 0.5
     bell = jnp.exp(-0.5 * u * u)
-    poly = jnp.full_like(t, TAIL_POLY[-1])
-    for c in TAIL_POLY[-2::-1]:
-        poly = poly * t + c
-    low_side = poly * t * bell
-    phi = jnp.where(u >= 0.0, 1.0 - low_side, low_side)
     return u * phi, phi + u * bell * (1.0 / math.sqrt(2.0 * math.pi))
 
 
@@ -103,7 +87,6 @@
             "tq": ((3, s.square, LANES), F32),
             "o": ((s.all + s.square, LANES), F32),
             "dq": ((3, s.all + s.square, LANES), F32),
-            "tb": ((3, s.all, LANES), BF),
             "q": ((both, s.queries, 2 * LANES), BF),
             "k": ((both, s.queries, 2 * LANES), BF),
             "v": ((both, s.queries, LANES), BF),
@@ -145,8 +128,21 @@
 
 
 def start_scratch(s, b):
-    for name in ("x", "gy", "tq", "o", "dq", "tb", "q", "k", "v", "da", "p", "ds"):
-        b[name][...] = jnp.zeros(b[name].shape, b[name].dtype)
+    for name in ("x", "gy"):
+        b[name][...] = jnp.zeros(b[name].shape, F32)
+    tail = jnp.zeros((s.square - s.all, LANES), F32)
+    for which in range(3):
+        b["tq"][which, s.all :, :] = tail
+        b["dq"][which, 2 * s.all :, :] = tail
+    b["o"][2 * s.all :, :] = tail
+    extra = s.queries - s.rows
+    for sb in range(2 * s.stripes):
+        for name in ("q", "k", "v", "da"):
+            b[name][sb, s.rows :, :] = jnp.zeros((extra, b[name].shape[2]), BF)
+        for h in range(HEADS // 2):
+            b["p"][sb, h, s.rows :, :] = jnp.zeros((extra, s.queries), BF)
+    for h in range(HEADS // 2):
+        b["ds"][h, s.rows :, :] = jnp.zeros((extra, s.queries), BF)
     for name in ("h1", "a", "h2", "gyb", "e1", "z", "du", "dqkv"):
         if s.deep > s.all:
             tail = (s.deep - s.all, b[name].shape[1])
@@ -212,10 +208,10 @@
         b["tq"][2, rows, :] = v[:, LANES:]
         return carry
 
-    lax.fori_loop(0, s.stripes, phase_a, 0)
+    lax.fori_loop(0, 0 if 'a' in SKIP else s.stripes, phase_a, 0, unroll=True)
 
     for which, name in enumerate(("q", "k", "v")):
-        for c in range(s.side):
+        for c in range(0 if 't' in SKIP else s.side):
             piece = b["tq"][which, pl.ds(c, s.wide, stride=s.wide), :]
             b[name][
                 s.stripes + c // STRIPE,
@@ -253,10 +249,10 @@
         b["o"][rows_of(sb), :] = o + pos
         return carry
 
-    lax.fori_loop(0, 2 * s.stripes, phase_b, 0)
+    lax.fori_loop(0, 0 if 'b' in SKIP else 2 * s.stripes, phase_b, 0, unroll=True)
 
     def turn_back(src_at, dst_at):
-        for r in range(s.side):
+        for r in range(0 if 't' in SKIP else s.side):
             piece = src_at(pl.ds(s.all + r, s.wide, stride=s.wide))
             dst_at(slice(s.wide * r, s.wide * (r + 1)), piece.astype(BF))
 
@@ -307,7 +303,7 @@
         b["tq"][0, rows, :] = da[:, LANES:]
         return carry
 
-    lax.fori_loop(0, s.stripes, phase_c, 0)
+    lax.fori_loop(0, 0 if 'c' in SKIP else s.stripes, phase_c, 0, unroll=True)
 
     for r in range(s.side):
         b["raw"][r * s.side : (r + 1) * s.side, :] = b["out"][
@@ -358,7 +354,7 @@
         gk[branch, 9] += fold_rows(dac)
         return carry
 
-    lax.fori_loop(0, 2 * s.stripes, phase_d, 0)
+    lax.fori_loop(0, 0 if 'd' in SKIP else 2 * s.stripes, phase_d, 0, unroll=True)
 
     for which in range(3):
 
@@ -384,7 +380,7 @@
         gv[1] += fold_rows(dh1)
         return carry
 
-    lax.fori_loop(0, s.stripes, phase_e, 0)
+    lax.fori_loop(0, 0 if 'e' in SKIP else s.stripes, phase_e, 0, unroll=True)
 
     for r in range(s.side):
         dx_ref[0, r * s.side : (r + 1) * s.side, :] = b["out"][
@@ -397,15 +393,35 @@
         ("h2", "du", o_fc1, ff),
         ("gyb", "z", o_fc2, ff),
     ):
+        if 'f' in SKIP: break
         turned = b[left][...]
         for j in range(0, width, d):
             g_ref[:, start + j : start + j + d] += dot_tn(turned, b[right][:, j : j + d])
 
 
-def block_kernel(names, sizes, small, large, counts, xs, xl, cs, cl, w_ref, *rest):
-    ys, yl, ds, dl, g_ref = rest[:5]
-    vec, kern, gv, gk, gb1 = rest[5:10]
-    scratch = rest[10:]
+def place_rows(order, me, near, far, full):
+    size = near.shape[1]
+    for i, mask in enumerate(order):
+        piece = near[i] if i < near.shape[0] else far[i - near.shape[0]]
+        start = pl.multiple_of((me[0] ^ mask) * size, 8)
+        full[pl.ds(start, size), :] = piece.astype(F32)
+
+
+def split_rows(order, me, full, keep, send):
+    size = keep.shape[1]
+    for i, mask in enumerate(order):
+        start = pl.multiple_of((me[0] ^ mask) * size, 8)
+        piece = full[pl.ds(start, size), :]
+        if i < keep.shape[0]:
+            keep[i] = piece
+        else:
+            send[i - keep.shape[0]] = piece.astype(send.dtype)
+
+
+def block_kernel(orders, names, sizes, small, large, me, counts, xs, xl, cs, cl, near, far, *rest):
+    ys, yl, ds, dl, keep, send = rest[:6]
+    vec, kern, gv, gk, gb1, w_ref, g_ref = rest[6:13]
+    scratch = rest[13:]
     few = dict(zip(names[: sizes[0]], scratch[: sizes[0]]))
     many = dict(zip(names[sizes[0] :], scratch[sizes[0] :]))
     step = pl.program_id(0)
@@ -417,6 +433,8 @@
     def _():
         start_scratch(small_shape, few)
         start_scratch(large_shape, many)
+        place_rows(orders[0], me, near, far, g_ref)
+        w_ref[...] = g_ref[...].astype(BF)
         for ref in (gv, gk, gb1, g_ref):
             ref[...] = jnp.zeros(ref.shape, ref.dtype)
         vec[...] = jnp.transpose(w_ref[:, 12 * d :].astype(F32))[0:32, :]
@@ -465,14 +483,16 @@
             rows.append(jnp.sum(gb1[j], axis=0, keepdims=True))
         rows.append(jnp.zeros((LANES - len(rows), d), F32))
         g_ref[:, 12 * d :] = jnp.transpose(jnp.concatenate(rows, axis=0))
-
-
-def run_block(small_images, large_images, small_cot, large_cot, counts, weights):
+        split_rows(orders[1], me, g_ref, keep, send)
+
+
+def run_block(small_images, large_images, small_cot, large_cot, counts, me, near, far, orders):
     few, small_cells, d = small_images.shape
     many, large_cells, _ = large_images.shape
     small = Shape(math.isqrt(small_cells))
     large = Shape(math.isqrt(large_cells))
-    width = weights.shape[1]
+    width = near.shape[2]
+    blocks, size = near.shape[0], near.shape[1]
     small_scratch = small.scratch(d, 4 * d)
     large_scratch = large.scratch(d, 4 * d)
     names = tuple(small_scratch) + tuple(large_scratch)
@@ -489,25 +509,28 @@
 
     small_block = pl.BlockSpec((1, small_cells, d), small_at)
     large_block = pl.BlockSpec((1, large_cells, d), large_at)
-    whole = pl.BlockSpec((d, width), lambda i: (0, 0), pipeline_mode=pl.Buffered(1))
+    whole = pl.BlockSpec((blocks, size, width), lambda i: (0, 0, 0), pipeline_mode=pl.Buffered(1))
     return pl.pallas_call(
-        functools.partial(block_kernel, names, (len(small_scratch), few), small, large),
+        functools.partial(block_kernel, orders, names, (len(small_scratch), few), small, large),
         grid=(few + many,),
         in_specs=[
+            pl.BlockSpec(memory_space=pltpu.SMEM),
             pl.BlockSpec(memory_space=pltpu.SMEM),
             small_block,
             large_block,
             small_block,
             large_block,
             whole,
+            whole,
         ],
-        out_specs=[small_block, large_block, small_block, large_block, whole],
+        out_specs=[small_block, large_block, small_block, large_block, whole, whole],
         out_shape=[
             jax.ShapeDtypeStruct(small_images.shape, BF),
             jax.ShapeDtypeStruct(large_images.shape, BF),
             jax.ShapeDtypeStruct(small_images.shape, F32),
             jax.ShapeDtypeStruct(large_images.shape, F32),
-            jax.ShapeDtypeStruct((d, width), F32),
+            jax.ShapeDtypeStruct((blocks, size, width), F32),
+            jax.ShapeDtypeStruct((blocks, size, width), F32),
         ],
         scratch_shapes=[
             pltpu.VMEM((32, d), F32),
@@ -515,12 +538,77 @@
             pltpu.VMEM((8, 8, d), F32),
             pltpu.VMEM((2, 16, 8, LANES), F32),
             pltpu.VMEM((4, 8, d), F32),
+            pltpu.VMEM((d, width), BF),
+            pltpu.VMEM((d, width), F32),
         ]
         + spaces,
         compiler_params=pltpu.CompilerParams(
             dimension_semantics=("arbitrary",), vmem_limit_bytes=60 * 2**20
         ),
-    )(counts, small_images, large_images, small_cot, large_cot, weights)
+    )(me, counts, small_images, large_images, small_cot, large_cot, near, far)
+
+
+AXES = ("dp", "fsdp")
+ROWS = 8
+GROUPS = ((2, 4, 6), (1, 16, 17), (8,))
+
+
+def gather_order():
+    order = [0]
+    for group in GROUPS:
+        order = order + [o ^ m for m in group for o in order]
+    return order
+
+
+def scatter_order():
+    order = [0]
+    for group in GROUPS:
+        order = [o ^ m for o in (0, *group) for m in order]
+    return order
+
+
+def swap(value, mask, count):
+    return lax.ppermute(value, AXES, [(i, i ^ mask) for i in range(count)])
+
+
+def pack_kernel(*refs):
+    out = refs[-1]
+    place = 0
+    for ref in refs[:-1]:
+        width = ref.shape[1]
+        out[:, place : place + width] = ref[...].astype(BF)
+        place += width
+    out[:, place:] = jnp.zeros((out.shape[0], out.shape[1] - place), BF)
+
+
+def sum_kernel(own, *refs):
+    parts, shard, squares = refs[:-2], refs[-2], refs[-1]
+    total = own[...]
+    for part in parts:
+        total = total + part[...].astype(F32)
+    shard[...] = total
+    square = total * total
+    lanes = square[:, 0:LANES]
+    for j in range(LANES, square.shape[1], LANES):
+        lanes = lanes + square[:, j : j + LANES]
+    squares[...] = lanes
+
+
+def update_kernel(widths, shard, own_squares, far_squares, *refs):
+    state, outs = refs[: 3 * len(widths)], refs[3 * len(widths) :]
+    both = own_squares[...] + far_squares[...]
+    total = jnp.sqrt(jnp.sum(jnp.sum(both, axis=0, keepdims=True), axis=1, keepdims=True))
+    clip_factor = jnp.minimum(1.0, clip_norm / (total + 1e-06))
+    outs[-1][...] = total
+    place = 0
+    for i, width in enumerate(widths):
+        master, first, second = (ref[...] for ref in state[3 * i : 3 * i + 3])
+        gradient = shard[:, place : place + width] * clip_factor
+        place += width
+        rate, decay = (rate_vector, 0.0) if i == 4 else (rate_matrix, decay_matrix)
+        new, first, second = adamw_update(master, first, second, gradient, rate, decay)
+        for out, value in zip(outs[4 * i : 4 * i + 4], (new, first, second, new)):
+            out[...] = value.astype(out.dtype)
 
 
 def adamw_update(weight, first, second, gradient, rate, decay):
@@ -532,43 +620,90 @@
     return (weight, first, second)
 
 
-AXES = ("dp", "fsdp")
-
-
-def on_device(
-    small_images,
-    large_images,
-    small_cot,
-    large_cot,
-    counts,
-    *state,
-):
-    masters = [state[i] for i in range(0, 15, 3)]
+def gather_rows(packed, count):
+    held = packed[None]
+    for group in GROUPS[:-1]:
+        held = jnp.concatenate([held] + [swap(held, m, count) for m in group], axis=0)
+    return held, swap(held, GROUPS[-1][0], count)
+
+
+def scatter_rows(keep, send, count):
+    held = keep + swap(send, GROUPS[-1][0], count).astype(F32)
+    for group in GROUPS[-2::-1]:
+        parts = len(group) + 1
+        size = held.shape[0] // parts
+        pieces = [held[i * size : (i + 1) * size] for i in range(parts)]
+        arrived = [swap(p.astype(BF), m, count) for p, m in zip(pieces[1:], group)]
+        if group is GROUPS[0]:
+            return pieces[0][0], [a[0] for a in arrived]
+        held = pieces[0]
+        for a in arrived:
+            held = held + a.astype(F32)
+
+
+def on_device(small_images, large_images, small_cot, large_cot, counts, *state):
+    d = small_images.shape[-1]
+    count = d // state[0].shape[0]
     turned = (False, True, False, True, True)
-    d = small_images.shape[-1]
-    own = [m.T if t else m for m, t in zip(masters, turned)]
-    shard_rows = own[0].shape[0]
-    pad = jnp.zeros((shard_rows, LANES - own[4].shape[1]), F32)
-    packed = jnp.concatenate(own + [pad], axis=1).astype(BF)
-    weights = lax.all_gather(packed, AXES, axis=0, tiled=True)
-    small_out, large_out, small_back, large_back, grads = run_block(
-        small_images, large_images, small_cot, large_cot, counts, weights
+    state = [v.T if turned[i // 3] else v for i, v in enumerate(state)]
+    masters = state[0::3]
+    widths = tuple(m.shape[1] for m in masters)
+    size = masters[0].shape[0]
+    width = sum(widths[:4]) + LANES
+    packed = pl.pallas_call(
+        pack_kernel, out_shape=jax.ShapeDtypeStruct((size, width), BF)
+    )(*masters)
+    by_pairs = size == ROWS and (lax.axis_size("dp"), lax.axis_size("fsdp")) == (4, 8)
+    if by_pairs:
+        near, far = gather_rows(packed, count)
+        me = lax.axis_index("dp") * lax.axis_size("fsdp") + lax.axis_index("fsdp")
+        orders = (gather_order(), scatter_order())
+    else:
+        whole = lax.all_gather(packed, AXES, axis=0, tiled=True).reshape(2, -1, ROWS, width)
+        near, far = whole[0], whole[1]
+        me = jnp.int32(0)
+        orders = (range(d // ROWS), range(d // ROWS))
+    small_out, large_out, small_back, large_back, keep, send = run_block(
+        small_images,
+        large_images,
+        small_cot,
+        large_cot,
+        counts,
+        me.astype(jnp.int32).reshape(1),
+        near,
+        far,
+        orders,
     )
-    shard = lax.psum_scatter(grads, AXES, scatter_dimension=0, tiled=True)
-    total = jnp.sqrt(lax.psum(jnp.sum(shard * shard), AXES))
-    clip_factor = jnp.minimum(1.0, clip_norm / (total + 1e-06))
-    outs = [small_out, large_out, small_back, large_back]
-    place = 0
-    for i, t in enumerate(turned):
-        master, first, second = state[3 * i : 3 * i + 3]
-        width = own[i].shape[1]
-        part = shard[:, place : place + width]
-        place += width
-        grad = (part.T if t else part) * clip_factor
-        rate, decay = (rate_vector, 0.0) if i == 4 else (rate_matrix, decay_matrix)
-        new, first_new, second_new = adamw_update(master, first, second, grad, rate, decay)
-        outs += [new, first_new, second_new, new.astype(BF)]
-    return (*outs, total)
+    if by_pairs:
+        own, arrived = scatter_rows(keep, send, count)
+    else:
+        whole = jnp.concatenate([keep, send], axis=0).reshape(d, width)
+        own = lax.psum_scatter(whole, AXES, scatter_dimension=0, tiled=True)
+        arrived = []
+    shard, squares = pl.pallas_call(
+        sum_kernel,
+        out_shape=[
+            jax.ShapeDtypeStruct((size, width), F32),
+            jax.ShapeDtypeStruct((size, LANES), F32),
+        ],
+    )(own, *arrived)
+    if by_pairs:
+        for group in GROUPS[:-1]:
+            other = [swap(squares, m, count) for m in group]
+            squares = (squares + other[0]) + (other[1] + other[2])
+        far_squares = swap(squares, GROUPS[-1][0], count)
+    else:
+        squares = lax.psum(squares, AXES)
+        far_squares = jnp.zeros_like(squares)
+    new_shapes = []
+    for m in masters:
+        new_shapes += [jax.ShapeDtypeStruct(m.shape, F32)] * 3 + [jax.ShapeDtypeStruct(m.shape, BF)]
+    updated = pl.pallas_call(
+        functools.partial(update_kernel, widths),
+        out_shape=new_shapes + [jax.ShapeDtypeStruct((1, 1), F32)],
+    )(shard, squares, far_squares, *state)
+    outs = [v.T if turned[i // 4] else v for i, v in enumerate(updated[:-1])]
+    return (small_out, large_out, small_back, large_back, *outs, updated[-1][0, 0])
 
 
 def solution(mesh):

time: 530 us -> 254 us (0.48)
  waiting for transfers between devices: 198 us -> 31.9 us
  Pallas kernels: 256 us -> 116 us
  starting transfers between devices: 0.08 us -> 91 us
  blocking collectives: 40.2 us -> 0 us
  between operations: 16.1 us -> 0.8 us
  other arithmetic: 12.4 us -> 3.3 us
    unnamed x3 -> x0, waiting for transfers between devices: 143 us -> none
    pallas_call x1 -> x4, Pallas kernels: 256 us -> 116 us  [the longest x1 111 us: run_block(): pl.pallas_call(functools.partial(block_kernel, orders, names, (len(small_...]
    ppermute x0 -> x21, starting transfers between devices: none -> 91 us  [swap(): return lax.ppermute(value, AXES, [(i, i ^ mask) for i in range(count)])]
    all_gather x1 -> x0, waiting for transfers between devices: 54.6 us -> none  [on_device(): weights = lax.all_gather(packed, AXES, axis=0, tiled=True)]
    psum x1 -> x0, blocking collectives: 40.2 us -> none  [on_device(): total = jnp.sqrt(lax.psum(jnp.sum(shard * shard), AXES))]
    ppermute x0 -> x21, waiting for transfers between devices: none -> 31.9 us  [swap(): return lax.ppermute(value, AXES, [(i, i ^ mask) for i in range(count)])]
    convert_element_type x5 -> x0, other arithmetic: 7.2 us -> none  [on_device(): outs += [new, first_new, second_new, new.astype(BF)]]
  transfers between devices with their start and end apart: 2 -> 21, of which waited for: 2 -> 16; matrix products, arithmetic and copies ran while one was open for 1% -> 2% of each run, Pallas kernels for 0% -> 0%
where the time goes in v2:
time: 254 us; the launch traced here: 250 us
  Pallas kernels  116 us (46%)
  starting transfers between devices  91 us (36%)
  waiting for transfers between devices  31.9 us (13%)
  local copies, waits for them, and re-layouts  6.97 us (3%)
  other arithmetic  3.3 us (1%)
    pallas_call x1, Pallas kernels, run_block(): pl.pallas_call(functools.partial(block_kernel, orders, names, (len(small_...  111 us
    ppermute x21, starting transfers between devices, swap(): return lax.ppermute(value, AXES, [(i, i ^ mask) for i in range(count)])  91 us
    ppermute x21, waiting for transfers between devices, swap(): return lax.ppermute(value, AXES, [(i, i ^ mask) for i in range(count)])  31.9 us
    unnamed x32, local copies, waits for them, and re-layouts  6.24 us
  transfers between devices with their start and end apart: 21, of which 16 were waited for; matrix products, arithmetic and copies ran while one was open for 2% of the time, Pallas kernels for 0%

profile of v2, /device:TPU:1, one launch (start us, length us, event | category | flops | bytes accessed | tf_op | source)
XLA Modules:
  0.0 250.0 jit_solution(10012421979532399591)
XLA Ops:
  0.7 1.5 shard_map.387
  2.2 4.2 %collective-permute-start.2 = (bf16[1,8,3200]{2,1,0:T(8,128)(2,1)}, bf16[1,8,3200]{2,1,0:T(8,128)(2,1)S(1)}, u32[]{:S(2)}, u32[]{:S(2)}) collective-permute-start(bf16[1,8,3200]{2,1,0:T(8,128)(2,1)} %bitcast.30), channel_id=1, source_target_pairs={{0,6},{1,7},{2,4},{3,5},{4,2},{5,3},{6,0},{7,1},{8,14},{9,15},{10,... | collective-permute-start | bytes 153608 | tf_op jit(solution)/shard_map/ppermute | solution.py:571
  8.1 2.9 %collective-permute-done.1 = bf16[1,8,3200]{2,1,0:T(8,128)(2,1)S(1)} collective-permute-done((bf16[1,8,3200]{2,1,0:T(8,128)(2,1)}, bf16[1,8,3200]{2,1,0:T(8,128)(2,1)S(1)}, u32[]{:S(2)}, u32[]{:S(2)}) %collective-permute-start.1) | collective-permute-done | bytes 51232 | tf_op jit(solution)/shard_map/ppermute | solution.py:571
  11.8 2.2 collective-permute-start.5
  14.6 7.8 %collective-permute-done.3 = bf16[4,8,3200]{2,1,0:T(8,128)(2,1)S(1)} collective-permute-done((bf16[4,8,3200]{2,1,0:T(8,128)(2,1)S(1)}, bf16[4,8,3200]{2,1,0:T(8,128)(2,1)S(1)}, u32[]{:S(2)}, u32[]{:S(2)}) %collective-permute-start.3) | collective-permute-done | bytes 204832 | tf_op jit(solution)/shard_map/ppermute | solution.py:571
  22.3 1.3 collective-permute-done.4
  23.7 1.2 collective-permute-start.6
  27.8 111.0 %shard_map.388 = (bf16[2,196,256]{2,1,0:T(8,128)(2,1)}, bf16[8,784,256]{2,1,0:T(8,128)(2,1)}, f32[2,196,256]{2,1,0:T(8,128)}, f32[8,784,256]{2,1,0:T(8,128)}, f3...) custom-call(s32[1]{0:T(128)} %bitcast.me, s32[1,2]{1,0:T(1,128)} %counts.1, bf16[2,196,256]{2,1,0:T(8,128)(2,1)} %copy.45.xs, ...), custom_call_target="tpu_custom_call" | custom-call | tf_op jit(solution)/shard_map/pallas_call | solution.py:513
  138.9 3.7 %collective-permute-done.7 = f32[16,8,3200]{2,1,0:T(8,128)S(1)} collective-permute-done((f32[16,8,3200]{2,1,0:T(8,128)}, f32[16,8,3200]{2,1,0:T(8,128)S(1)}, u32[]{:S(2)}, u32[]{:S(2)}) %collective-permute-start.7) | collective-permute-done | bytes 1638432 | tf_op jit(solution)/shard_map/ppermute | solution.py:571
  142.6 1.7 fusion.4
  144.4 40.0 %collective-permute-start.8 = (bf16[4,8,3200]{2,1,0:T(8,128)(2,1)S(1)}, bf16[4,8,3200]{2,1,0:T(8,128)(2,1)S(1)}, u32[]{:S(2)}, u32[]{:S(2)}) collective-permute-start(bf16[4,8,3200]{2,1,0:T(8,128)(2,1)S(1)} %get-tuple-element.112), channel_id=1, source_target_pairs={{0,1},{1,0},{2,3},{3,2},{4,5},{5,4},{6,7},{7,6},{8,9},{9,8},{10,11... | collective-permute-start | bytes 614408 | tf_op jit(solution)/shard_map/ppermute | solution.py:571
  184.4 1.3 collective-permute-start.9
  185.6 3.9 %collective-permute-done.8 = bf16[4,8,3200]{2,1,0:T(8,128)(2,1)S(1)} collective-permute-done((bf16[4,8,3200]{2,1,0:T(8,128)(2,1)S(1)}, bf16[4,8,3200]{2,1,0:T(8,128)(2,1)S(1)}, u32[]{:S(2)}, u32[]{:S(2)}) %collective-permute-start.8) | collective-permute-done | bytes 204832 | tf_op jit(solution)/shard_map/ppermute | solution.py:571
  189.5 3.4 %collective-permute-done.10 = bf16[4,8,3200]{2,1,0:T(8,128)(2,1)S(1)} collective-permute-done((bf16[4,8,3200]{2,1,0:T(8,128)(2,1)S(1)}, bf16[4,8,3200]{2,1,0:T(8,128)(2,1)S(1)}, u32[]{:S(2)}, u32[]{:S(2)}) %collective-permute-start.10) | collective-permute-done | bytes 204832 | tf_op jit(solution)/shard_map/ppermute | solution.py:571
  192.9 2.0 collective-permute-done.9
  195.0 22.3 %collective-permute-start.13 = (bf16[1,8,3200]{2,1,0:T(8,128)(2,1)S(1)}, bf16[1,8,3200]{2,1,0:T(8,128)(2,1)S(1)}, u32[]{:S(2)}, u32[]{:S(2)}) collective-permute-start(bf16[1,8,3200]{2,1,0:T(8,128)(2,1)S(1)} %get-tuple-element.115), channel_id=1, source_target_pairs={{0,6},{1,7},{2,4},{3,5},{4,2},{5,3},{6,0},{7,1},{8,14},{9,15},{10,... | collective-permute-start | bytes 153608 | tf_op jit(solution)/shard_map/ppermute | solution.py:571
  217.3 6.5 %collective-permute-start.12 = (bf16[1,8,3200]{2,1,0:T(8,128)(2,1)S(1)}, bf16[1,8,3200]{2,1,0:T(8,128)(2,1)S(1)}, u32[]{:S(2)}, u32[]{:S(2)}) collective-permute-start(bf16[1,8,3200]{2,1,0:T(8,128)(2,1)S(1)} %get-tuple-element.116), channel_id=1, source_target_pairs={{0,4},{1,5},{2,6},{3,7},{4,0},{5,1},{6,2},{7,3},{8,12},{9,13},{10,... | collective-permute-start | bytes 153608 | tf_op jit(solution)/shard_map/ppermute | solution.py:571
  227.3 1.6 shard_map.389
  228.9 2.3 collective-permute-start.16
  231.3 1.1 collective-permute-start.14
  233.4 1.4 collective-permute-done.15
  235.5 1.3 collective-permute-start.19
  239.6 6.1 %collective-permute-start.20 = (f32[8,128]{1,0:T(8,128)S(1)}, f32[8,128]{1,0:T(8,128)S(1)}, u32[]{:S(2)}, u32[]{:S(2)}) collective-permute-start(f32[8,128]{1,0:T(8,128)S(1)} %add_add_fusion.own_squares), channel_id=1, source_target_pairs={{0,8},{1,9},{2,10},{3,11},{4,12},{5,13},{6,14},{7,15},{8,0},{9,1},... | collective-permute-start | bytes 12296 | tf_op jit(solution)/shard_map/ppermute | solution.py:571
  248.1 1.9 shard_map.390
  (63 shorter events, 16.7 us)
Async XLA Ops:
  0.7 25.0 %copy-start.5 = (bf16[2,196,256]{2,0,1:T(2,128)(2,1)S(1)}, bf16[2,196,256]{2,0,1:T(2,128)(2,1)}, u32[]{:S(2)}) copy-start(bf16[2,196,256]{2,0,1:T(2,128)(2,1)} %param.22) | copy-start | bytes 602116
  2.2 5.9 %collective-permute-start.2 = (bf16[1,8,3200]{2,1,0:T(8,128)(2,1)}, bf16[1,8,3200]{2,1,0:T(8,128)(2,1)S(1)}, u32[]{:S(2)}, u32[]{:S(2)}) collective-permute-start(bf16[1,8,3200]{2,1,0:T(8,128)(2,1)} %bitcast.30), channel_id=1, source_target_pairs={{0,6},{1,7},{2,4},{3,5},{4,2},{5,3},{6,0},{7,1},{8,14},{9,15},{10,... | collective-permute-start | bytes 153608 | tf_op jit(solution)/shard_map/ppermute | solution.py:571
  6.3 4.6 %collective-permute-start.1 = (bf16[1,8,3200]{2,1,0:T(8,128)(2,1)}, bf16[1,8,3200]{2,1,0:T(8,128)(2,1)S(1)}, u32[]{:S(2)}, u32[]{:S(2)}) collective-permute-start(bf16[1,8,3200]{2,1,0:T(8,128)(2,1)} %bitcast.31), channel_id=1, source_target_pairs={{0,4},{1,5},{2,6},{3,7},{4,0},{5,1},{6,2},{7,3},{8,12},{9,13},{10,... | collective-permute-start | bytes 153608 | tf_op jit(solution)/shard_map/ppermute | solution.py:571
  6.3 4.6 %collective-permute-start = (bf16[1,8,3200]{2,1,0:T(8,128)(2,1)}, bf16[1,8,3200]{2,1,0:T(8,128)(2,1)S(1)}, u32[]{:S(2)}, u32[]{:S(2)}) collective-permute-start(bf16[1,8,3200]{2,1,0:T(8,128)(2,1)} %bitcast.32), channel_id=1, source_target_pairs={{0,2},{1,3},{2,0},{3,1},{4,6},{5,7},{6,4},{7,5},{8,10},{9,11},{10,... | collective-permute-start | bytes 153608 | tf_op jit(solution)/shard_map/ppermute | solution.py:571
  11.8 11.9 %collective-permute-start.5 = (bf16[4,8,3200]{2,1,0:T(8,128)(2,1)S(1)}, bf16[4,8,3200]{2,1,0:T(8,128)(2,1)S(1)}, u32[]{:S(2)}, u32[]{:S(2)}) collective-permute-start(bf16[4,8,3200]{2,1,0:T(8,128)(2,1)S(1)} %pad_maximum_fusion), channel_id=1, source_target_pairs={{0,17},{1,16},{2,19},{3,18},{4,21},{5,20},{6,23},{7,22},{8,25},{9,... | collective-permute-start | bytes 614408 | tf_op jit(solution)/shard_map/ppermute | solution.py:571
  14.0 9.6 %collective-permute-start.4 = (bf16[4,8,3200]{2,1,0:T(8,128)(2,1)S(1)}, bf16[4,8,3200]{2,1,0:T(8,128)(2,1)S(1)}, u32[]{:S(2)}, u32[]{:S(2)}) collective-permute-start(bf16[4,8,3200]{2,1,0:T(8,128)(2,1)S(1)} %pad_maximum_fusion), channel_id=1, source_target_pairs={{0,16},{1,17},{2,18},{3,19},{4,20},{5,21},{6,22},{7,23},{8,24},{9,... | collective-permute-start | bytes 614408 | tf_op jit(solution)/shard_map/ppermute | solution.py:571
  14.3 8.1 %collective-permute-start.3 = (bf16[4,8,3200]{2,1,0:T(8,128)(2,1)S(1)}, bf16[4,8,3200]{2,1,0:T(8,128)(2,1)S(1)}, u32[]{:S(2)}, u32[]{:S(2)}) collective-permute-start(bf16[4,8,3200]{2,1,0:T(8,128)(2,1)S(1)} %pad_maximum_fusion), channel_id=1, source_target_pairs={{0,1},{1,0},{2,3},{3,2},{4,5},{5,4},{6,7},{7,6},{8,9},{9,8},{10,11... | collective-permute-start | bytes 614408 | tf_op jit(solution)/shard_map/ppermute | solution.py:571
  23.7 3.2 %collective-permute-start.6 = (bf16[16,8,3200]{2,1,0:T(8,128)(2,1)S(1)}, bf16[16,8,3200]{2,1,0:T(8,128)(2,1)S(1)}, u32[]{:S(2)}, u32[]{:S(2)}) collective-permute-start(bf16[16,8,3200]{2,1,0:T(8,128)(2,1)S(1)} %constant_dynamic-update-slice_fusion.near), channel_id=1, source_target_pairs={{0,8},{1,9},{2,10},{3,11},{4,12},{5,13},{6,14},{7,15},{8,0},{9,1},... | collective-permute-start | bytes 2457608 | tf_op jit(solution)/shard_map/ppermute | solution.py:571
  138.8 3.8 %collective-permute-start.7 = (f32[16,8,3200]{2,1,0:T(8,128)}, f32[16,8,3200]{2,1,0:T(8,128)S(1)}, u32[]{:S(2)}, u32[]{:S(2)}) collective-permute-start(f32[16,8,3200]{2,1,0:T(8,128)} %get-tuple-element.59), channel_id=1, source_target_pairs={{0,8},{1,9},{2,10},{3,11},{4,12},{5,13},{6,14},{7,15},{8,0},{9,1},... | collective-permute-start | bytes 4915208 | tf_op jit(solution)/shard_map/ppermute | solution.py:571
  144.3 101.4 %copy-start.3 = (bf16[2,196,256]{2,1,0:T(8,128)(2,1)S(1)}, bf16[2,196,256]{2,1,0:T(8,128)(2,1)}, u32[]{:S(2)}) copy-start(bf16[2,196,256]{2,1,0:T(8,128)(2,1)} %get-tuple-element.83) | copy-start | bytes 602116
  144.3 102.2 %copy-start.2 = (f32[2,196,256]{2,1,0:T(8,128)S(1)}, f32[2,196,256]{2,1,0:T(8,128)}, u32[]{:S(2)}) copy-start(f32[2,196,256]{2,1,0:T(8,128)} %get-tuple-element.85) | copy-start | bytes 1204228
  144.4 45.2 %collective-permute-start.8 = (bf16[4,8,3200]{2,1,0:T(8,128)(2,1)S(1)}, bf16[4,8,3200]{2,1,0:T(8,128)(2,1)S(1)}, u32[]{:S(2)}, u32[]{:S(2)}) collective-permute-start(bf16[4,8,3200]{2,1,0:T(8,128)(2,1)S(1)} %get-tuple-element.112), channel_id=1, source_target_pairs={{0,1},{1,0},{2,3},{3,2},{4,5},{5,4},{6,7},{7,6},{8,9},{9,8},{10,11... | collective-permute-start | bytes 614408 | tf_op jit(solution)/shard_map/ppermute | solution.py:571
  184.4 8.5 %collective-permute-start.10 = (bf16[4,8,3200]{2,1,0:T(8,128)(2,1)S(1)}, bf16[4,8,3200]{2,1,0:T(8,128)(2,1)S(1)}, u32[]{:S(2)}, u32[]{:S(2)}) collective-permute-start(bf16[4,8,3200]{2,1,0:T(8,128)(2,1)S(1)} %get-tuple-element.113), channel_id=1, source_target_pairs={{0,17},{1,16},{2,19},{3,18},{4,21},{5,20},{6,23},{7,22},{8,25},{9,... | collective-permute-start | bytes 614408 | tf_op jit(solution)/shard_map/ppermute | solution.py:571
  184.4 10.5 %collective-permute-start.9 = (bf16[4,8,3200]{2,1,0:T(8,128)(2,1)S(1)}, bf16[4,8,3200]{2,1,0:T(8,128)(2,1)S(1)}, u32[]{:S(2)}, u32[]{:S(2)}) collective-permute-start(bf16[4,8,3200]{2,1,0:T(8,128)(2,1)S(1)} %get-tuple-element.114), channel_id=1, source_target_pairs={{0,16},{1,17},{2,18},{3,19},{4,20},{5,21},{6,22},{7,23},{8,24},{9,... | collective-permute-start | bytes 614408 | tf_op jit(solution)/shard_map/ppermute | solution.py:571
  195.0 29.6 %collective-permute-start.13 = (bf16[1,8,3200]{2,1,0:T(8,128)(2,1)S(1)}, bf16[1,8,3200]{2,1,0:T(8,128)(2,1)S(1)}, u32[]{:S(2)}, u32[]{:S(2)}) collective-permute-start(bf16[1,8,3200]{2,1,0:T(8,128)(2,1)S(1)} %get-tuple-element.115), channel_id=1, source_target_pairs={{0,6},{1,7},{2,4},{3,5},{4,2},{5,3},{6,0},{7,1},{8,14},{9,15},{10,... | collective-permute-start | bytes 153608 | tf_op jit(solution)/shard_map/ppermute | solution.py:571
  217.3 8.4 %collective-permute-start.12 = (bf16[1,8,3200]{2,1,0:T(8,128)(2,1)S(1)}, bf16[1,8,3200]{2,1,0:T(8,128)(2,1)S(1)}, u32[]{:S(2)}, u32[]{:S(2)}) collective-permute-start(bf16[1,8,3200]{2,1,0:T(8,128)(2,1)S(1)} %get-tuple-element.116), channel_id=1, source_target_pairs={{0,4},{1,5},{2,6},{3,7},{4,0},{5,1},{6,2},{7,3},{8,12},{9,13},{10,... | collective-permute-start | bytes 153608 | tf_op jit(solution)/shard_map/ppermute | solution.py:571
  223.7 3.0 %collective-permute-start.11 = (bf16[1,8,3200]{2,1,0:T(8,128)(2,1)S(1)}, bf16[1,8,3200]{2,1,0:T(8,128)(2,1)S(1)}, u32[]{:S(2)}, u32[]{:S(2)}) collective-permute-start(bf16[1,8,3200]{2,1,0:T(8,128)(2,1)S(1)} %get-tuple-element.117), channel_id=1, source_target_pairs={{0,2},{1,3},{2,0},{3,1},{4,6},{5,7},{6,4},{7,5},{8,10},{9,11},{10,... | collective-permute-start | bytes 153608 | tf_op jit(solution)/shard_map/ppermute | solution.py:571
  228.9 4.5 %collective-permute-start.16 = (f32[8,128]{1,0:T(8,128)}, f32[8,128]{1,0:T(8,128)S(1)}, u32[]{:S(2)}, u32[]{:S(2)}) collective-permute-start(f32[8,128]{1,0:T(8,128)} %get-tuple-element.61), channel_id=1, source_target_pairs={{0,6},{1,7},{2,4},{3,5},{4,2},{5,3},{6,0},{7,1},{8,14},{9,15},{10,... | collective-permute-start | bytes 12296 | tf_op jit(solution)/shard_map/ppermute | solution.py:571
  231.2 3.6 %collective-permute-start.15 = (f32[8,128]{1,0:T(8,128)}, f32[8,128]{1,0:T(8,128)S(1)}, u32[]{:S(2)}, u32[]{:S(2)}) collective-permute-start(f32[8,128]{1,0:T(8,128)} %get-tuple-element.61), channel_id=1, source_target_pairs={{0,4},{1,5},{2,6},{3,7},{4,0},{5,1},{6,2},{7,3},{8,12},{9,13},{10,... | collective-permute-start | bytes 12296 | tf_op jit(solution)/shard_map/ppermute | solution.py:571
  231.3 3.5 %collective-permute-start.14 = (f32[8,128]{1,0:T(8,128)}, f32[8,128]{1,0:T(8,128)S(1)}, u32[]{:S(2)}, u32[]{:S(2)}) collective-permute-start(f32[8,128]{1,0:T(8,128)} %get-tuple-element.61), channel_id=1, source_target_pairs={{0,2},{1,3},{2,0},{3,1},{4,6},{5,7},{6,4},{7,5},{8,10},{9,11},{10,... | collective-permute-start | bytes 12296 | tf_op jit(solution)/shard_map/ppermute | solution.py:571
  235.5 3.6 %collective-permute-start.19 = (f32[8,128]{1,0:T(8,128)S(1)}, f32[8,128]{1,0:T(8,128)S(1)}, u32[]{:S(2)}, u32[]{:S(2)}) collective-permute-start(f32[8,128]{1,0:T(8,128)S(1)} %add_add_fusion.1), channel_id=1, source_target_pairs={{0,17},{1,16},{2,19},{3,18},{4,21},{5,20},{6,23},{7,22},{8,25},{9,... | collective-permute-start | bytes 12296 | tf_op jit(solution)/shard_map/ppermute | solution.py:571
  236.8 2.5 collective-permute-start.18
  237.1 2.5 collective-permute-start.17
  239.6 7.9 %collective-permute-start.20 = (f32[8,128]{1,0:T(8,128)S(1)}, f32[8,128]{1,0:T(8,128)S(1)}, u32[]{:S(2)}, u32[]{:S(2)}) collective-permute-start(f32[8,128]{1,0:T(8,128)S(1)} %add_add_fusion.own_squares), channel_id=1, source_target_pairs={{0,8},{1,9},{2,10},{3,11},{4,12},{5,13},{6,14},{7,15},{8,0},{9,1},... | collective-permute-start | bytes 12296 | tf_op jit(solution)/shard_map/ppermute | solution.py:571
  (8 other events, 40.6 us)

commit v3 on v2

--- a/solution.py
+++ b/solution.py
@@ -25,7 +25,7 @@
 BF = jnp.bfloat16
 F32 = jnp.float32
 FAR = -1e30
-SKIP = set()
+LOG2E = 1.0 / math.log(2.0)
 
 
 def dot_nn(a, b):
@@ -50,8 +50,9 @@
 
 def gelu_parts(u):
     phi = 0.5 * lax.erf(u * math.sqrt(0.5)) + 0.5
-    bell = jnp.exp(-0.5 * u * u)
-    return u * phi, phi + u * bell * (1.0 / math.sqrt(2.0 * math.pi))
+    root = u * math.sqrt(0.5 * LOG2E)
+    bell = jnp.exp2(math.log2(1.0 / math.sqrt(2.0 * math.pi)) - root * root)
+    return u * phi, phi + u * bell
 
 
 def shift_down(v, n):
@@ -92,7 +93,8 @@
             "v": ((both, s.queries, LANES), BF),
             "da": ((both, s.queries, LANES), BF),
             "p": ((both, HEADS // 2, s.queries, s.queries), BF),
-            "ds": ((HEADS // 2, s.queries, s.queries), BF),
+            "ot": ((both, LANES, s.queries), F32),
+            "ds": ((2, HEADS // 2, s.queries, s.queries), BF),
             "h1": ((s.deep, d), BF),
             "a": ((s.deep, d), BF),
             "h2": ((s.deep, d), BF),
@@ -141,8 +143,9 @@
             b[name][sb, s.rows :, :] = jnp.zeros((extra, b[name].shape[2]), BF)
         for h in range(HEADS // 2):
             b["p"][sb, h, s.rows :, :] = jnp.zeros((extra, s.queries), BF)
-    for h in range(HEADS // 2):
-        b["ds"][h, s.rows :, :] = jnp.zeros((extra, s.queries), BF)
+    for i in range(2):
+        for h in range(HEADS // 2):
+            b["ds"][i, h, s.rows :, :] = jnp.zeros((extra, s.queries), BF)
     for name in ("h1", "a", "h2", "gyb", "e1", "z", "du", "dqkv"):
         if s.deep > s.all:
             tail = (s.deep - s.all, b[name].shape[1])
@@ -167,6 +170,14 @@
     return mixed[1] + shift_down(mixed[0], s.wide) + shift_up(mixed[2], s.wide)
 
 
+def take_turns(*makers):
+    running = [m for m in makers if m is not None]
+    while running:
+        for m in list(running):
+            if next(m, running) is running:
+                running.remove(m)
+
+
 def image_step(s, b, x_ref, cot_ref, y_ref, dx_ref, w_ref, g_ref, vec, kern, gv, gk, gb1):
     d = x_ref.shape[-1]
     ff = 4 * d
@@ -177,7 +188,7 @@
     mask = place_mask(s, LANES)
 
     def rows_of(t):
-        return pl.ds(pl.multiple_of(t * s.rows, 16), s.rows)
+        return slice(t * s.rows, (t + 1) * s.rows)
 
     for src, dst in ((x_ref, "x"), (cot_ref, "gy")):
         b["raw"][...] = src[0].astype(F32)
@@ -186,7 +197,7 @@
                 r * s.side : (r + 1) * s.side, :
             ]
 
-    def phase_a(t, carry):
+    def phase_a(t):
         rows = rows_of(t)
         x = b["x"][rows, :]
         centered = x - row_mean(x)
@@ -206,18 +217,19 @@
         b["tq"][0, rows, :] = q[:, LANES:]
         b["tq"][1, rows, :] = k[:, LANES:]
         b["tq"][2, rows, :] = v[:, LANES:]
-        return carry
-
-    lax.fori_loop(0, 0 if 'a' in SKIP else s.stripes, phase_a, 0, unroll=True)
+
+    for t in range(s.stripes):
+        phase_a(t)
+
+    def turned(cells):
+        grid = cells.reshape(s.wide, s.wide, LANES)
+        return jnp.swapaxes(grid, 0, 1)[0 : s.side].reshape(s.all, LANES)
 
     for which, name in enumerate(("q", "k", "v")):
-        for c in range(0 if 't' in SKIP else s.side):
-            piece = b["tq"][which, pl.ds(c, s.wide, stride=s.wide), :]
-            b[name][
-                s.stripes + c // STRIPE,
-                s.wide * (c % STRIPE) : s.wide * (c % STRIPE + 1),
-                0:LANES,
-            ] = piece.astype(BF)
+        piece = turned(b["tq"][which])
+        for t in range(s.stripes):
+            part = piece[t * s.rows : (t + 1) * s.rows]
+            b[name][s.stripes + t, 0 : s.rows, 0:LANES] = part.astype(BF)
 
     def taps_of(branch):
         rows9 = kern[branch]
@@ -228,7 +240,7 @@
     masks_wide = head_masks(2 * LANES)
     masks_one = head_masks(LANES)
 
-    def phase_b(sb, carry):
+    def phase_b(sb):
         q = b["q"][sb]
         k = b["k"][sb, 0 : s.rows, :]
         k4 = jnp.concatenate([k * m for m in masks_wide], axis=0)
@@ -239,29 +251,24 @@
         for h in range(heads):
             sh = s4[h * s.rows : (h + 1) * s.rows, :]
             top = jnp.max(sh, axis=0, keepdims=True)
-            ex = jnp.exp((sh - top) * scale)
+            ex = jnp.exp2((sh - top) * (scale * LOG2E))
             total = jnp.sum(ex, axis=0, keepdims=True)
             b["p"][sb, h, 0 : s.rows, :] = (ex * (1.0 / total)).astype(BF)
             parts.append(dot_nn(vt[h * e : (h + 1) * e, :], b["p"][sb, h]))
-        o = jnp.transpose(jnp.concatenate(parts, axis=0))[0 : s.rows, :]
+            yield
+        ot = jnp.concatenate(parts, axis=0)
+        b["ot"][sb] = ot
+        o = jnp.transpose(ot)[0 : s.rows, :]
         taps, offset = taps_of(sb // s.stripes)
         pos = conv_rows(v[0 : s.rows, :], taps, s, False) + offset
         b["o"][rows_of(sb), :] = o + pos
-        return carry
-
-    lax.fori_loop(0, 0 if 'b' in SKIP else 2 * s.stripes, phase_b, 0, unroll=True)
-
-    def turn_back(src_at, dst_at):
-        for r in range(0 if 't' in SKIP else s.side):
-            piece = src_at(pl.ds(s.all + r, s.wide, stride=s.wide))
-            dst_at(slice(s.wide * r, s.wide * (r + 1)), piece.astype(BF))
-
-    def put_a(rows, piece):
-        b["a"][rows, LANES:] = piece
-
-    turn_back(lambda rows: b["o"][rows, :], put_a)
-
-    def phase_c(t, carry):
+
+    for sb in range(2 * s.stripes):
+        take_turns(phase_b(sb))
+
+    b["a"][0 : s.all, LANES:] = turned(b["o"][s.all :, :]).astype(BF)
+
+    def phase_c(t):
         rows = rows_of(t)
         b["a"][rows, 0:LANES] = b["o"][rows, :].astype(BF)
         x1 = b["x"][rows, :] + dot_nt(b["a"][rows, :], w_ref[:, o_proj : o_proj + d]) + vec[4:5, :]
@@ -274,7 +281,6 @@
         gyb = gy.astype(BF)
         b["gyb"][rows, :] = gyb
         out = x1 + vec[7:8, :]
-        dh2 = jnp.zeros((s.rows, d), F32)
         for j in range(4):
             c1 = slice(o_fc1 + j * d, o_fc1 + (j + 1) * d)
             c2 = slice(o_fc2 + j * d, o_fc2 + (j + 1) * d)
@@ -283,11 +289,13 @@
             z, slope = gelu_parts(u)
             z = z.astype(BF)
             b["z"][rows, cj] = z
-            out = out + dot_nt(z, w_ref[:, c2])
-            du = (dot_nn(gyb, w_ref[:, c2]) * slope).astype(BF)
+            du = dot_nn(gyb, w_ref[:, c2]) * slope
+            gb1[j] += fold_rows(du)
+            du = du.astype(BF)
             b["du"][rows, cj] = du
-            dh2 = dh2 + dot_nt(du, w_ref[:, c1])
-            gb1[j] += fold_rows(du.astype(F32))
+            yield
+        out = out + dot_nt(b["z"][rows, :], w_ref[:, o_fc2 : o_fc2 + ff])
+        dh2 = dot_nt(b["du"][rows, :], w_ref[:, o_fc1 : o_fc1 + ff])
         b["out"][rows, :] = out
         dn = dh2 * vec[5:6, :]
         dx1 = gy + inverse * (dn - row_mean(dn) - n2 * row_mean(dn * n2))
@@ -301,43 +309,29 @@
         da = dot_nn(e1, w_ref[:, o_proj : o_proj + d])
         b["da"][t, 0 : s.rows, :] = da[:, 0:LANES].astype(BF)
         b["tq"][0, rows, :] = da[:, LANES:]
-        return carry
-
-    lax.fori_loop(0, 0 if 'c' in SKIP else s.stripes, phase_c, 0, unroll=True)
-
-    for r in range(s.side):
-        b["raw"][r * s.side : (r + 1) * s.side, :] = b["out"][
-            r * s.wide : r * s.wide + s.side, :
-        ]
-    y_ref[0] = b["raw"][...].astype(BF)
-
-    for c in range(s.side):
-        piece = b["tq"][0, pl.ds(c, s.wide, stride=s.wide), :]
-        b["da"][
-            s.stripes + c // STRIPE, s.wide * (c % STRIPE) : s.wide * (c % STRIPE + 1), :
-        ] = piece.astype(BF)
-
-    def phase_d(sb, carry):
+
+    def phase_d(sb):
         branch = sb // s.stripes
         v = b["v"][sb, 0 : s.rows, :]
         da = b["da"][sb]
         v4 = jnp.concatenate([v * m for m in masks_one], axis=0)
         dp4 = dot_nt(v4, da)
+        mixed = jnp.transpose(da.astype(F32)) * b["ot"][sb]
         kt = jnp.transpose(b["k"][sb, :, 0:LANES].astype(F32)).astype(BF)
         parts = []
         for h in range(heads):
             ph = b["p"][sb, h, 0 : s.rows, :].astype(F32)
-            pd = ph * dp4[h * s.rows : (h + 1) * s.rows, :]
-            inner = jnp.sum(pd, axis=0, keepdims=True)
-            b["ds"][h, 0 : s.rows, :] = (pd - ph * inner).astype(BF)
-            parts.append(dot_nn(kt[h * e : (h + 1) * e, :], b["ds"][h]))
+            inner = jnp.sum(mixed[h * e : (h + 1) * e, :], axis=0, keepdims=True)
+            dp = dp4[h * s.rows : (h + 1) * s.rows, :]
+            b["ds"][sb % 2, h, 0 : s.rows, :] = (ph * (dp - inner)).astype(BF)
+            parts.append(dot_nn(kt[h * e : (h + 1) * e, :], b["ds"][sb % 2, h]))
+            yield
         dq = jnp.transpose(jnp.concatenate(parts, axis=0))[0 : s.rows, :] * scale
-        ds4 = jnp.concatenate([b["ds"][h, 0 : s.rows, :] for h in range(heads)], axis=0)
-        dk4 = dot_nn(ds4, b["q"][sb, :, 0:LANES])
-        dk = pick_heads([dk4[h * s.rows : (h + 1) * s.rows, :] for h in range(heads)]) * scale
-        p4 = jnp.concatenate([b["p"][sb, h, 0 : s.rows, :] for h in range(heads)], axis=0)
-        dv4 = dot_nn(p4, da)
-        dv = pick_heads([dv4[h * s.rows : (h + 1) * s.rows, :] for h in range(heads)])
+        ds4 = jnp.concatenate([b["ds"][sb % 2, h, 0 : s.rows, :] for h in range(heads)], axis=1)
+        p4 = jnp.concatenate([b["p"][sb, h, 0 : s.rows, :] for h in range(heads)], axis=1)
+        q = b["q"][sb, :, 0:LANES]
+        dk = dot_nn(ds4, jnp.concatenate([q * m for m in masks_one], axis=0)) * scale
+        dv = dot_nn(p4, jnp.concatenate([da * m for m in masks_one], axis=0))
         taps, offset = taps_of(branch)
         dac = da[0 : s.rows, :].astype(F32)
         vf = v.astype(F32)
@@ -352,18 +346,39 @@
             gk[branch, 3 + c] += fold_rows(dac * sides[c])
             gk[branch, 6 + c] += fold_rows(dac[: -s.wide] * sides[c][s.wide :])
         gk[branch, 9] += fold_rows(dac)
-        return carry
-
-    lax.fori_loop(0, 0 if 'd' in SKIP else 2 * s.stripes, phase_d, 0, unroll=True)
+
+    for t in range(s.stripes + 1):
+        take_turns(
+            phase_c(t) if t < s.stripes else None, phase_d(t - 1) if t > 0 else None
+        )
+
+    for r in range(s.side):
+        b["raw"][r * s.side : (r + 1) * s.side, :] = b["out"][
+            r * s.wide : r * s.wide + s.side, :
+        ]
+    y_ref[0] = b["raw"][...].astype(BF)
+
+    piece = turned(b["tq"][0])
+    for t in range(s.stripes):
+        b["da"][s.stripes + t, 0 : s.rows, :] = piece[t * s.rows : (t + 1) * s.rows].astype(BF)
+
+    products = [("h2", "du", o_fc1, j) for j in range(4)]
+    products += [("gyb", "z", o_fc2, j) for j in range(4)] + [("e1", "a", o_proj, 0)]
+    for sb in range(s.stripes, 2 * s.stripes):
+        take_turns(phase_d(sb))
+        share = -(-len(products) // (2 * s.stripes - sb))
+        for left, right, start, j in products[:share]:
+            cj = slice(j * d, (j + 1) * d)
+            g_ref[:, start + j * d : start + (j + 1) * d] += dot_tn(
+                b[left][...], b[right][:, cj]
+            )
+        products = products[share:]
 
     for which in range(3):
-
-        def put_b(rows, piece, which=which):
-            b["dqkv"][rows, which * d + LANES : (which + 1) * d] = piece
-
-        turn_back(lambda rows, which=which: b["dq"][which, rows, :], put_b)
-
-    def phase_e(t, carry):
+        lanes = slice(which * d + LANES, (which + 1) * d)
+        b["dqkv"][0 : s.all, lanes] = turned(b["dq"][which, s.all :, :]).astype(BF)
+
+    def phase_e(t):
         rows = rows_of(t)
         for which in range(3):
             b["dqkv"][rows, which * d : which * d + LANES] = b["dq"][which, rows, :].astype(BF)
@@ -378,25 +393,17 @@
         b["out"][rows, :] = b["dx1"][rows, :] + back * jnp.concatenate([r1, r1], axis=1)
         gv[0] += fold_rows(dh1 * n1)
         gv[1] += fold_rows(dh1)
-        return carry
-
-    lax.fori_loop(0, 0 if 'e' in SKIP else s.stripes, phase_e, 0, unroll=True)
+
+    for t in range(s.stripes):
+        phase_e(t)
 
     for r in range(s.side):
         dx_ref[0, r * s.side : (r + 1) * s.side, :] = b["out"][
             r * s.wide : r * s.wide + s.side, :
         ]
 
-    for left, right, start, width in (
-        ("h1", "dqkv", o_qkv, 3 * d),
-        ("e1", "a", o_proj, d),
-        ("h2", "du", o_fc1, ff),
-        ("gyb", "z", o_fc2, ff),
-    ):
-        if 'f' in SKIP: break
-        turned = b[left][...]
-        for j in range(0, width, d):
-            g_ref[:, start + j : start + j + d] += dot_tn(turned, b[right][:, j : j + d])
+    for j in range(0, 3 * d, d):
+        g_ref[:, o_qkv + j : o_qkv + j + d] += dot_tn(b["h1"][...], b["dqkv"][:, j : j + d])
 
 
 def place_rows(order, me, near, far, full):

time: 254 us -> 220 us (0.87); the launches traced: 250 us -> 222 us
  Pallas kernels: 116 us -> 29.3 us
  starting transfers between devices: 91 us -> 148 us
    pallas_call x1, Pallas kernels: 111 us -> 24.3 us  [run_block(): pl.pallas_call(functools.partial(block_kernel, orders, names, (len(small_...]
    ppermute x21, starting transfers between devices: 91 us -> 148 us  [swap(): return lax.ppermute(value, AXES, [(i, i ^ mask) for i in range(count)])]
  transfers between devices with their start and end apart: 21 -> 21, of which waited for: 16 -> 14; matrix products, arithmetic and copies ran while one was open for 2% -> 2% of each run, Pallas kernels for 0% -> 0%
where the time goes in v3:
time: 220 us; the launch traced here: 222 us
  starting transfers between devices  148 us (67%)
  waiting for transfers between devices  33.1 us (15%)
  Pallas kernels  29.3 us (13%)
  local copies, waits for them, and re-layouts  6.98 us (3%)
  other arithmetic  3.3 us (2%)
    ppermute x21, starting transfers between devices, swap(): return lax.ppermute(value, AXES, [(i, i ^ mask) for i in range(count)])  148 us
    ppermute x21, waiting for transfers between devices, swap(): return lax.ppermute(value, AXES, [(i, i ^ mask) for i in range(count)])  33.1 us
    pallas_call x1, Pallas kernels, run_block(): pl.pallas_call(functools.partial(block_kernel, orders, names, (len(small_...  24.3 us
    unnamed x32, local copies, waits for them, and re-layouts  6.25 us
  transfers between devices with their start and end apart: 21, of which 14 were waited for; matrix products, arithmetic and copies ran while one was open for 2% of the time, Pallas kernels for 0%

profile of v3, /device:TPU:1, one launch (start us, length us, event | category | flops | bytes accessed | tf_op | source)
XLA Modules:
  0.0 221.5 jit_solution(4953232771872450405)
XLA Ops:
  0.7 1.5 shard_map.387
  2.2 4.2 %collective-permute-start.2 = (bf16[1,8,3200]{2,1,0:T(8,128)(2,1)}, bf16[1,8,3200]{2,1,0:T(8,128)(2,1)S(1)}, u32[]{:S(2)}, u32[]{:S(2)}) collective-permute-start(bf16[1,8,3200]{2,1,0:T(8,128)(2,1)} %bitcast.30), channel_id=1, source_target_pairs={{0,6},{1,7},{2,4},{3,5},{4,2},{5,3},{6,0},{7,1},{8,14},{9,15},{10,... | collective-permute-start | bytes 153608 | tf_op jit(solution)/shard_map/ppermute | solution.py:578
  8.1 2.9 %collective-permute-done.1 = bf16[1,8,3200]{2,1,0:T(8,128)(2,1)S(1)} collective-permute-done((bf16[1,8,3200]{2,1,0:T(8,128)(2,1)}, bf16[1,8,3200]{2,1,0:T(8,128)(2,1)S(1)}, u32[]{:S(2)}, u32[]{:S(2)}) %collective-permute-start.1) | collective-permute-done | bytes 51232 | tf_op jit(solution)/shard_map/ppermute | solution.py:578
  11.8 2.2 %collective-permute-start.5 = (bf16[4,8,3200]{2,1,0:T(8,128)(2,1)S(1)}, bf16[4,8,3200]{2,1,0:T(8,128)(2,1)S(1)}, u32[]{:S(2)}, u32[]{:S(2)}) collective-permute-start(bf16[4,8,3200]{2,1,0:T(8,128)(2,1)S(1)} %pad_maximum_fusion), channel_id=1, source_target_pairs={{0,17},{1,16},{2,19},{3,18},{4,21},{5,20},{6,23},{7,22},{8,25},{9,... | collective-permute-start | bytes 614408 | tf_op jit(solution)/shard_map/ppermute | solution.py:578
  14.6 7.8 %collective-permute-done.3 = bf16[4,8,3200]{2,1,0:T(8,128)(2,1)S(1)} collective-permute-done((bf16[4,8,3200]{2,1,0:T(8,128)(2,1)S(1)}, bf16[4,8,3200]{2,1,0:T(8,128)(2,1)S(1)}, u32[]{:S(2)}, u32[]{:S(2)}) %collective-permute-start.3) | collective-permute-done | bytes 204832 | tf_op jit(solution)/shard_map/ppermute | solution.py:578
  22.3 1.3 collective-permute-done.4
  23.7 1.2 collective-permute-start.6
  27.8 24.3 %shard_map.388 = (bf16[2,196,256]{2,1,0:T(8,128)(2,1)}, bf16[8,784,256]{2,1,0:T(8,128)(2,1)}, f32[2,196,256]{2,1,0:T(8,128)}, f32[8,784,256]{2,1,0:T(8,128)}, f3...) custom-call(s32[1]{0:T(128)} %bitcast.me, s32[1,2]{1,0:T(1,128)} %counts.1, bf16[2,196,256]{2,1,0:T(8,128)(2,1)} %copy.45.xs, ...), custom_call_target="tpu_custom_call" | custom-call | tf_op jit(solution)/shard_map/pallas_call | solution.py:520
  52.2 3.7 %collective-permute-done.7 = f32[16,8,3200]{2,1,0:T(8,128)S(1)} collective-permute-done((f32[16,8,3200]{2,1,0:T(8,128)}, f32[16,8,3200]{2,1,0:T(8,128)S(1)}, u32[]{:S(2)}, u32[]{:S(2)}) %collective-permute-start.7) | collective-permute-done | bytes 1638432 | tf_op jit(solution)/shard_map/ppermute | solution.py:578
  55.9 1.7 fusion.4
  57.7 97.8 %collective-permute-start.8 = (bf16[4,8,3200]{2,1,0:T(8,128)(2,1)S(1)}, bf16[4,8,3200]{2,1,0:T(8,128)(2,1)S(1)}, u32[]{:S(2)}, u32[]{:S(2)}) collective-permute-start(bf16[4,8,3200]{2,1,0:T(8,128)(2,1)S(1)} %get-tuple-element.112), channel_id=1, source_target_pairs={{0,1},{1,0},{2,3},{3,2},{4,5},{5,4},{6,7},{7,6},{8,9},{9,8},{10,11... | collective-permute-start | bytes 614408 | tf_op jit(solution)/shard_map/ppermute | solution.py:578
  155.5 1.3 collective-permute-start.9
  156.8 3.9 %collective-permute-done.8 = bf16[4,8,3200]{2,1,0:T(8,128)(2,1)S(1)} collective-permute-done((bf16[4,8,3200]{2,1,0:T(8,128)(2,1)S(1)}, bf16[4,8,3200]{2,1,0:T(8,128)(2,1)S(1)}, u32[]{:S(2)}, u32[]{:S(2)}) %collective-permute-start.8) | collective-permute-done | bytes 204832 | tf_op jit(solution)/shard_map/ppermute | solution.py:578
  160.6 3.4 %collective-permute-done.10 = bf16[4,8,3200]{2,1,0:T(8,128)(2,1)S(1)} collective-permute-done((bf16[4,8,3200]{2,1,0:T(8,128)(2,1)S(1)}, bf16[4,8,3200]{2,1,0:T(8,128)(2,1)S(1)}, u32[]{:S(2)}, u32[]{:S(2)}) %collective-permute-start.10) | collective-permute-done | bytes 204832 | tf_op jit(solution)/shard_map/ppermute | solution.py:578
  164.0 2.0 collective-permute-done.9
  166.1 28.3 %collective-permute-start.13 = (bf16[1,8,3200]{2,1,0:T(8,128)(2,1)S(1)}, bf16[1,8,3200]{2,1,0:T(8,128)(2,1)S(1)}, u32[]{:S(2)}, u32[]{:S(2)}) collective-permute-start(bf16[1,8,3200]{2,1,0:T(8,128)(2,1)S(1)} %get-tuple-element.115), channel_id=1, source_target_pairs={{0,6},{1,7},{2,4},{3,5},{4,2},{5,3},{6,0},{7,1},{8,14},{9,15},{10,... | collective-permute-start | bytes 153608 | tf_op jit(solution)/shard_map/ppermute | solution.py:578
  196.0 3.1 %collective-permute-done.12 = bf16[1,8,3200]{2,1,0:T(8,128)(2,1)S(1)} collective-permute-done((bf16[1,8,3200]{2,1,0:T(8,128)(2,1)S(1)}, bf16[1,8,3200]{2,1,0:T(8,128)(2,1)S(1)}, u32[]{:S(2)}, u32[]{:S(2)}) %collective-permute-start.12) | collective-permute-done | bytes 51232 | tf_op jit(solution)/shard_map/ppermute | solution.py:578
  199.8 1.6 shard_map.389
  201.4 1.9 collective-permute-start.16
  203.3 1.6 collective-permute-start.14
  208.4 1.5 collective-permute-start.18
  210.9 1.4 collective-permute-done.17
  212.3 5.0 %collective-permute-start.20 = (f32[8,128]{1,0:T(8,128)S(1)}, f32[8,128]{1,0:T(8,128)S(1)}, u32[]{:S(2)}, u32[]{:S(2)}) collective-permute-start(f32[8,128]{1,0:T(8,128)S(1)} %add_add_fusion.own_squares), channel_id=1, source_target_pairs={{0,8},{1,9},{2,10},{3,11},{4,12},{5,13},{6,14},{7,15},{8,0},{9,1},... | collective-permute-start | bytes 12296 | tf_op jit(solution)/shard_map/ppermute | solution.py:578
  219.7 1.9 shard_map.390
  (63 shorter events, 15.5 us)
Async XLA Ops:
  0.7 25.0 %copy-start.5 = (bf16[2,196,256]{2,0,1:T(2,128)(2,1)S(1)}, bf16[2,196,256]{2,0,1:T(2,128)(2,1)}, u32[]{:S(2)}) copy-start(bf16[2,196,256]{2,0,1:T(2,128)(2,1)} %param.22) | copy-start | bytes 602116
  2.2 5.9 %collective-permute-start.2 = (bf16[1,8,3200]{2,1,0:T(8,128)(2,1)}, bf16[1,8,3200]{2,1,0:T(8,128)(2,1)S(1)}, u32[]{:S(2)}, u32[]{:S(2)}) collective-permute-start(bf16[1,8,3200]{2,1,0:T(8,128)(2,1)} %bitcast.30), channel_id=1, source_target_pairs={{0,6},{1,7},{2,4},{3,5},{4,2},{5,3},{6,0},{7,1},{8,14},{9,15},{10,... | collective-permute-start | bytes 153608 | tf_op jit(solution)/shard_map/ppermute | solution.py:578
  6.3 4.6 %collective-permute-start.1 = (bf16[1,8,3200]{2,1,0:T(8,128)(2,1)}, bf16[1,8,3200]{2,1,0:T(8,128)(2,1)S(1)}, u32[]{:S(2)}, u32[]{:S(2)}) collective-permute-start(bf16[1,8,3200]{2,1,0:T(8,128)(2,1)} %bitcast.31), channel_id=1, source_target_pairs={{0,4},{1,5},{2,6},{3,7},{4,0},{5,1},{6,2},{7,3},{8,12},{9,13},{10,... | collective-permute-start | bytes 153608 | tf_op jit(solution)/shard_map/ppermute | solution.py:578
  6.3 4.6 %collective-permute-start = (bf16[1,8,3200]{2,1,0:T(8,128)(2,1)}, bf16[1,8,3200]{2,1,0:T(8,128)(2,1)S(1)}, u32[]{:S(2)}, u32[]{:S(2)}) collective-permute-start(bf16[1,8,3200]{2,1,0:T(8,128)(2,1)} %bitcast.32), channel_id=1, source_target_pairs={{0,2},{1,3},{2,0},{3,1},{4,6},{5,7},{6,4},{7,5},{8,10},{9,11},{10,... | collective-permute-start | bytes 153608 | tf_op jit(solution)/shard_map/ppermute | solution.py:578
  11.8 11.9 %collective-permute-start.5 = (bf16[4,8,3200]{2,1,0:T(8,128)(2,1)S(1)}, bf16[4,8,3200]{2,1,0:T(8,128)(2,1)S(1)}, u32[]{:S(2)}, u32[]{:S(2)}) collective-permute-start(bf16[4,8,3200]{2,1,0:T(8,128)(2,1)S(1)} %pad_maximum_fusion), channel_id=1, source_target_pairs={{0,17},{1,16},{2,19},{3,18},{4,21},{5,20},{6,23},{7,22},{8,25},{9,... | collective-permute-start | bytes 614408 | tf_op jit(solution)/shard_map/ppermute | solution.py:578
  14.0 9.6 %collective-permute-start.4 = (bf16[4,8,3200]{2,1,0:T(8,128)(2,1)S(1)}, bf16[4,8,3200]{2,1,0:T(8,128)(2,1)S(1)}, u32[]{:S(2)}, u32[]{:S(2)}) collective-permute-start(bf16[4,8,3200]{2,1,0:T(8,128)(2,1)S(1)} %pad_maximum_fusion), channel_id=1, source_target_pairs={{0,16},{1,17},{2,18},{3,19},{4,20},{5,21},{6,22},{7,23},{8,24},{9,... | collective-permute-start | bytes 614408 | tf_op jit(solution)/shard_map/ppermute | solution.py:578
  14.3 8.1 %collective-permute-start.3 = (bf16[4,8,3200]{2,1,0:T(8,128)(2,1)S(1)}, bf16[4,8,3200]{2,1,0:T(8,128)(2,1)S(1)}, u32[]{:S(2)}, u32[]{:S(2)}) collective-permute-start(bf16[4,8,3200]{2,1,0:T(8,128)(2,1)S(1)} %pad_maximum_fusion), channel_id=1, source_target_pairs={{0,1},{1,0},{2,3},{3,2},{4,5},{5,4},{6,7},{7,6},{8,9},{9,8},{10,11... | collective-permute-start | bytes 614408 | tf_op jit(solution)/shard_map/ppermute | solution.py:578
  23.7 3.2 %collective-permute-start.6 = (bf16[16,8,3200]{2,1,0:T(8,128)(2,1)S(1)}, bf16[16,8,3200]{2,1,0:T(8,128)(2,1)S(1)}, u32[]{:S(2)}, u32[]{:S(2)}) collective-permute-start(bf16[16,8,3200]{2,1,0:T(8,128)(2,1)S(1)} %constant_dynamic-update-slice_fusion.near), channel_id=1, source_target_pairs={{0,8},{1,9},{2,10},{3,11},{4,12},{5,13},{6,14},{7,15},{8,0},{9,1},... | collective-permute-start | bytes 2457608 | tf_op jit(solution)/shard_map/ppermute | solution.py:578
  52.1 3.8 %collective-permute-start.7 = (f32[16,8,3200]{2,1,0:T(8,128)}, f32[16,8,3200]{2,1,0:T(8,128)S(1)}, u32[]{:S(2)}, u32[]{:S(2)}) collective-permute-start(f32[16,8,3200]{2,1,0:T(8,128)} %get-tuple-element.59), channel_id=1, source_target_pairs={{0,8},{1,9},{2,10},{3,11},{4,12},{5,13},{6,14},{7,15},{8,0},{9,1},... | collective-permute-start | bytes 4915208 | tf_op jit(solution)/shard_map/ppermute | solution.py:578
  57.6 159.7 %copy-start.3 = (bf16[2,196,256]{2,1,0:T(8,128)(2,1)S(1)}, bf16[2,196,256]{2,1,0:T(8,128)(2,1)}, u32[]{:S(2)}) copy-start(bf16[2,196,256]{2,1,0:T(8,128)(2,1)} %get-tuple-element.83) | copy-start | bytes 602116
  57.7 160.4 %copy-start.2 = (f32[2,196,256]{2,1,0:T(8,128)S(1)}, f32[2,196,256]{2,1,0:T(8,128)}, u32[]{:S(2)}) copy-start(f32[2,196,256]{2,1,0:T(8,128)} %get-tuple-element.85) | copy-start | bytes 1204228
  57.7 103.0 %collective-permute-start.8 = (bf16[4,8,3200]{2,1,0:T(8,128)(2,1)S(1)}, bf16[4,8,3200]{2,1,0:T(8,128)(2,1)S(1)}, u32[]{:S(2)}, u32[]{:S(2)}) collective-permute-start(bf16[4,8,3200]{2,1,0:T(8,128)(2,1)S(1)} %get-tuple-element.112), channel_id=1, source_target_pairs={{0,1},{1,0},{2,3},{3,2},{4,5},{5,4},{6,7},{7,6},{8,9},{9,8},{10,11... | collective-permute-start | bytes 614408 | tf_op jit(solution)/shard_map/ppermute | solution.py:578
  155.5 8.5 %collective-permute-start.10 = (bf16[4,8,3200]{2,1,0:T(8,128)(2,1)S(1)}, bf16[4,8,3200]{2,1,0:T(8,128)(2,1)S(1)}, u32[]{:S(2)}, u32[]{:S(2)}) collective-permute-start(bf16[4,8,3200]{2,1,0:T(8,128)(2,1)S(1)} %get-tuple-element.113), channel_id=1, source_target_pairs={{0,17},{1,16},{2,19},{3,18},{4,21},{5,20},{6,23},{7,22},{8,25},{9,... | collective-permute-start | bytes 614408 | tf_op jit(solution)/shard_map/ppermute | solution.py:578
  155.5 10.5 %collective-permute-start.9 = (bf16[4,8,3200]{2,1,0:T(8,128)(2,1)S(1)}, bf16[4,8,3200]{2,1,0:T(8,128)(2,1)S(1)}, u32[]{:S(2)}, u32[]{:S(2)}) collective-permute-start(bf16[4,8,3200]{2,1,0:T(8,128)(2,1)S(1)} %get-tuple-element.114), channel_id=1, source_target_pairs={{0,16},{1,17},{2,18},{3,19},{4,20},{5,21},{6,22},{7,23},{8,24},{9,... | collective-permute-start | bytes 614408 | tf_op jit(solution)/shard_map/ppermute | solution.py:578
  166.1 30.0 %collective-permute-start.13 = (bf16[1,8,3200]{2,1,0:T(8,128)(2,1)S(1)}, bf16[1,8,3200]{2,1,0:T(8,128)(2,1)S(1)}, u32[]{:S(2)}, u32[]{:S(2)}) collective-permute-start(bf16[1,8,3200]{2,1,0:T(8,128)(2,1)S(1)} %get-tuple-element.115), channel_id=1, source_target_pairs={{0,6},{1,7},{2,4},{3,5},{4,2},{5,3},{6,0},{7,1},{8,14},{9,15},{10,... | collective-permute-start | bytes 153608 | tf_op jit(solution)/shard_map/ppermute | solution.py:578
  194.4 4.7 %collective-permute-start.12 = (bf16[1,8,3200]{2,1,0:T(8,128)(2,1)S(1)}, bf16[1,8,3200]{2,1,0:T(8,128)(2,1)S(1)}, u32[]{:S(2)}, u32[]{:S(2)}) collective-permute-start(bf16[1,8,3200]{2,1,0:T(8,128)(2,1)S(1)} %get-tuple-element.116), channel_id=1, source_target_pairs={{0,4},{1,5},{2,6},{3,7},{4,0},{5,1},{6,2},{7,3},{8,12},{9,13},{10,... | collective-permute-start | bytes 153608 | tf_op jit(solution)/shard_map/ppermute | solution.py:578
  195.4 3.7 %collective-permute-start.11 = (bf16[1,8,3200]{2,1,0:T(8,128)(2,1)S(1)}, bf16[1,8,3200]{2,1,0:T(8,128)(2,1)S(1)}, u32[]{:S(2)}, u32[]{:S(2)}) collective-permute-start(bf16[1,8,3200]{2,1,0:T(8,128)(2,1)S(1)} %get-tuple-element.117), channel_id=1, source_target_pairs={{0,2},{1,3},{2,0},{3,1},{4,6},{5,7},{6,4},{7,5},{8,10},{9,11},{10,... | collective-permute-start | bytes 153608 | tf_op jit(solution)/shard_map/ppermute | solution.py:578
  201.4 4.5 %collective-permute-start.16 = (f32[8,128]{1,0:T(8,128)}, f32[8,128]{1,0:T(8,128)S(1)}, u32[]{:S(2)}, u32[]{:S(2)}) collective-permute-start(f32[8,128]{1,0:T(8,128)} %get-tuple-element.61), channel_id=1, source_target_pairs={{0,6},{1,7},{2,4},{3,5},{4,2},{5,3},{6,0},{7,1},{8,14},{9,15},{10,... | collective-permute-start | bytes 12296 | tf_op jit(solution)/shard_map/ppermute | solution.py:578
  203.3 3.6 %collective-permute-start.15 = (f32[8,128]{1,0:T(8,128)}, f32[8,128]{1,0:T(8,128)S(1)}, u32[]{:S(2)}, u32[]{:S(2)}) collective-permute-start(f32[8,128]{1,0:T(8,128)} %get-tuple-element.61), channel_id=1, source_target_pairs={{0,4},{1,5},{2,6},{3,7},{4,0},{5,1},{6,2},{7,3},{8,12},{9,13},{10,... | collective-permute-start | bytes 12296 | tf_op jit(solution)/shard_map/ppermute | solution.py:578
  203.3 3.6 %collective-permute-start.14 = (f32[8,128]{1,0:T(8,128)}, f32[8,128]{1,0:T(8,128)S(1)}, u32[]{:S(2)}, u32[]{:S(2)}) collective-permute-start(f32[8,128]{1,0:T(8,128)} %get-tuple-element.61), channel_id=1, source_target_pairs={{0,2},{1,3},{2,0},{3,1},{4,6},{5,7},{6,4},{7,5},{8,10},{9,11},{10,... | collective-permute-start | bytes 12296 | tf_op jit(solution)/shard_map/ppermute | solution.py:578
  207.5 3.4 %collective-permute-start.19 = (f32[8,128]{1,0:T(8,128)S(1)}, f32[8,128]{1,0:T(8,128)S(1)}, u32[]{:S(2)}, u32[]{:S(2)}) collective-permute-start(f32[8,128]{1,0:T(8,128)S(1)} %add_add_fusion.1), channel_id=1, source_target_pairs={{0,17},{1,16},{2,19},{3,18},{4,21},{5,20},{6,23},{7,22},{8,25},{9,... | collective-permute-start | bytes 12296 | tf_op jit(solution)/shard_map/ppermute | solution.py:578
  208.4 2.5 %collective-permute-start.18 = (f32[8,128]{1,0:T(8,128)S(1)}, f32[8,128]{1,0:T(8,128)S(1)}, u32[]{:S(2)}, u32[]{:S(2)}) collective-permute-start(f32[8,128]{1,0:T(8,128)S(1)} %add_add_fusion.1), channel_id=1, source_target_pairs={{0,16},{1,17},{2,18},{3,19},{4,20},{5,21},{6,22},{7,23},{8,24},{9,... | collective-permute-start | bytes 12296 | tf_op jit(solution)/shard_map/ppermute | solution.py:578
  209.8 2.5 %collective-permute-start.17 = (f32[8,128]{1,0:T(8,128)S(1)}, f32[8,128]{1,0:T(8,128)S(1)}, u32[]{:S(2)}, u32[]{:S(2)}) collective-permute-start(f32[8,128]{1,0:T(8,128)S(1)} %add_add_fusion.1), channel_id=1, source_target_pairs={{0,1},{1,0},{2,3},{3,2},{4,5},{5,4},{6,7},{7,6},{8,9},{9,8},{10,11... | collective-permute-start | bytes 12296 | tf_op jit(solution)/shard_map/ppermute | solution.py:578
  212.3 6.8 %collective-permute-start.20 = (f32[8,128]{1,0:T(8,128)S(1)}, f32[8,128]{1,0:T(8,128)S(1)}, u32[]{:S(2)}, u32[]{:S(2)}) collective-permute-start(f32[8,128]{1,0:T(8,128)S(1)} %add_add_fusion.own_squares), channel_id=1, source_target_pairs={{0,8},{1,9},{2,10},{3,11},{4,12},{5,13},{6,14},{7,15},{8,0},{9,1},... | collective-permute-start | bytes 12296 | tf_op jit(solution)/shard_map/ppermute | solution.py:578
  (8 other events, 40.1 us)

commit v4 on v3

--- a/solution.py
+++ b/solution.py
@@ -240,11 +240,12 @@
     masks_wide = head_masks(2 * LANES)
     masks_one = head_masks(LANES)
 
-    def phase_b(sb):
-        q = b["q"][sb]
+    def scores_of(sb):
         k = b["k"][sb, 0 : s.rows, :]
         k4 = jnp.concatenate([k * m for m in masks_wide], axis=0)
-        s4 = dot_nt(k4, q)
+        return dot_nt(k4, b["q"][sb])
+
+    def phase_b(sb, s4):
         v = b["v"][sb].astype(F32)
         vt = jnp.transpose(v).astype(BF)
         parts = []
@@ -263,18 +264,26 @@
         pos = conv_rows(v[0 : s.rows, :], taps, s, False) + offset
         b["o"][rows_of(sb), :] = o + pos
 
+    ready = scores_of(0)
     for sb in range(2 * s.stripes):
-        take_turns(phase_b(sb))
+        scores = ready
+        if sb + 1 < 2 * s.stripes:
+            ready = scores_of(sb + 1)
+        take_turns(phase_b(sb, scores))
 
     b["a"][0 : s.all, LANES:] = turned(b["o"][s.all :, :]).astype(BF)
 
-    def phase_c(t):
+    def middle_of(t):
         rows = rows_of(t)
         b["a"][rows, 0:LANES] = b["o"][rows, :].astype(BF)
         x1 = b["x"][rows, :] + dot_nt(b["a"][rows, :], w_ref[:, o_proj : o_proj + d]) + vec[4:5, :]
         centered = x1 - row_mean(x1)
         inverse = lax.rsqrt(row_mean(centered * centered) + epsilon)
         n2 = centered * inverse
+        return x1, inverse, n2
+
+    def phase_c(t, x1, inverse, n2):
+        rows = rows_of(t)
         h2 = (n2 * vec[5:6, :] + vec[6:7, :]).astype(BF)
         b["h2"][rows, :] = h2
         gy = b["gy"][rows, :]
@@ -347,10 +356,12 @@
             gk[branch, 6 + c] += fold_rows(dac[: -s.wide] * sides[c][s.wide :])
         gk[branch, 9] += fold_rows(dac)
 
-    for t in range(s.stripes + 1):
-        take_turns(
-            phase_c(t) if t < s.stripes else None, phase_d(t - 1) if t > 0 else None
-        )
+    ahead = middle_of(0)
+    for t in range(s.stripes):
+        middle = ahead
+        if t + 1 < s.stripes:
+            ahead = middle_of(t + 1)
+        take_turns(phase_c(t, *middle))
 
     for r in range(s.side):
         b["raw"][r * s.side : (r + 1) * s.side, :] = b["out"][
@@ -364,7 +375,7 @@
 
     products = [("h2", "du", o_fc1, j) for j in range(4)]
     products += [("gyb", "z", o_fc2, j) for j in range(4)] + [("e1", "a", o_proj, 0)]
-    for sb in range(s.stripes, 2 * s.stripes):
+    for sb in range(2 * s.stripes):
         take_turns(phase_d(sb))
         share = -(-len(products) // (2 * s.stripes - sb))
         for left, right, start, j in products[:share]:

time: 220 us -> 212 us (0.964); the launches traced: 222 us -> 211 us
  starting transfers between devices: 148 us -> 126 us
  Pallas kernels: 29.3 us -> 42.3 us
    ppermute x21, starting transfers between devices: 148 us -> 126 us  [swap(): return lax.ppermute(value, AXES, [(i, i ^ mask) for i in range(count)])]
    pallas_call x1, Pallas kernels: 24.3 us -> 37.3 us  [run_block(): pl.pallas_call(functools.partial(block_kernel, orders, names, (len(small_...]
  transfers between devices with their start and end apart: 21 -> 21, of which waited for: 14 -> 15; matrix products, arithmetic and copies ran while one was open for 2% -> 2% of each run, Pallas kernels for 0% -> 0%
where the time goes in v4:
time: 212 us; the launch traced here: 211 us
  starting transfers between devices  126 us (59%)
  Pallas kernels  42.3 us (20%)
  waiting for transfers between devices  31.9 us (15%)
  local copies, waits for them, and re-layouts  6.98 us (3%)
  other arithmetic  3.3 us (2%)
    ppermute x21, starting transfers between devices, swap(): return lax.ppermute(value, AXES, [(i, i ^ mask) for i in range(count)])  126 us
    pallas_call x1, Pallas kernels, run_block(): pl.pallas_call(functools.partial(block_kernel, orders, names, (len(small_...  37.3 us
    ppermute x21, waiting for transfers between devices, swap(): return lax.ppermute(value, AXES, [(i, i ^ mask) for i in range(count)])  31.9 us
    unnamed x32, local copies, waits for them, and re-layouts  6.25 us
  transfers between devices with their start and end apart: 21, of which 15 were waited for; matrix products, arithmetic and copies ran while one was open for 2% of the time, Pallas kernels for 0%

profile of v4, /device:TPU:1, one launch (start us, length us, event | category | flops | bytes accessed | tf_op | source)
XLA Modules:
  0.0 211.2 jit_solution(4834163618429555390)
XLA Ops:
  0.7 1.5 shard_map.387
  2.2 4.2 %collective-permute-start.2 = (bf16[1,8,3200]{2,1,0:T(8,128)(2,1)}, bf16[1,8,3200]{2,1,0:T(8,128)(2,1)S(1)}, u32[]{:S(2)}, u32[]{:S(2)}) collective-permute-start(bf16[1,8,3200]{2,1,0:T(8,128)(2,1)} %bitcast.30), channel_id=1, source_target_pairs={{0,6},{1,7},{2,4},{3,5},{4,2},{5,3},{6,0},{7,1},{8,14},{9,15},{10,... | collective-permute-start | bytes 153608 | tf_op jit(solution)/shard_map/ppermute | solution.py:589
  8.1 2.9 %collective-permute-done.1 = bf16[1,8,3200]{2,1,0:T(8,128)(2,1)S(1)} collective-permute-done((bf16[1,8,3200]{2,1,0:T(8,128)(2,1)}, bf16[1,8,3200]{2,1,0:T(8,128)(2,1)S(1)}, u32[]{:S(2)}, u32[]{:S(2)}) %collective-permute-start.1) | collective-permute-done | bytes 51232 | tf_op jit(solution)/shard_map/ppermute | solution.py:589
  11.8 2.2 %collective-permute-start.5 = (bf16[4,8,3200]{2,1,0:T(8,128)(2,1)S(1)}, bf16[4,8,3200]{2,1,0:T(8,128)(2,1)S(1)}, u32[]{:S(2)}, u32[]{:S(2)}) collective-permute-start(bf16[4,8,3200]{2,1,0:T(8,128)(2,1)S(1)} %pad_maximum_fusion), channel_id=1, source_target_pairs={{0,17},{1,16},{2,19},{3,18},{4,21},{5,20},{6,23},{7,22},{8,25},{9,... | collective-permute-start | bytes 614408 | tf_op jit(solution)/shard_map/ppermute | solution.py:589
  14.6 7.8 %collective-permute-done.3 = bf16[4,8,3200]{2,1,0:T(8,128)(2,1)S(1)} collective-permute-done((bf16[4,8,3200]{2,1,0:T(8,128)(2,1)S(1)}, bf16[4,8,3200]{2,1,0:T(8,128)(2,1)S(1)}, u32[]{:S(2)}, u32[]{:S(2)}) %collective-permute-start.3) | collective-permute-done | bytes 204832 | tf_op jit(solution)/shard_map/ppermute | solution.py:589
  22.3 1.3 collective-permute-done.4
  27.8 37.3 %shard_map.388 = (bf16[2,196,256]{2,1,0:T(8,128)(2,1)}, bf16[8,784,256]{2,1,0:T(8,128)(2,1)}, f32[2,196,256]{2,1,0:T(8,128)}, f32[8,784,256]{2,1,0:T(8,128)}, f3...) custom-call(s32[1]{0:T(128)} %bitcast.me, s32[1,2]{1,0:T(1,128)} %counts.1, bf16[2,196,256]{2,1,0:T(8,128)(2,1)} %copy.45.xs, ...), custom_call_target="tpu_custom_call" | custom-call | tf_op jit(solution)/shard_map/pallas_call | solution.py:531
  65.1 28.8 %collective-permute-start.7 = (f32[16,8,3200]{2,1,0:T(8,128)}, f32[16,8,3200]{2,1,0:T(8,128)S(1)}, u32[]{:S(2)}, u32[]{:S(2)}) collective-permute-start(f32[16,8,3200]{2,1,0:T(8,128)} %get-tuple-element.59), channel_id=1, source_target_pairs={{0,8},{1,9},{2,10},{3,11},{4,12},{5,13},{6,14},{7,15},{8,0},{9,1},... | collective-permute-start | bytes 4915208 | tf_op jit(solution)/shard_map/ppermute | solution.py:589
  93.9 3.3 %collective-permute-done.7 = f32[16,8,3200]{2,1,0:T(8,128)S(1)} collective-permute-done((f32[16,8,3200]{2,1,0:T(8,128)}, f32[16,8,3200]{2,1,0:T(8,128)S(1)}, u32[]{:S(2)}, u32[]{:S(2)}) %collective-permute-start.7) | collective-permute-done | bytes 1638432 | tf_op jit(solution)/shard_map/ppermute | solution.py:589
  97.3 1.7 fusion.4
  99.0 72.8 %collective-permute-start.8 = (bf16[4,8,3200]{2,1,0:T(8,128)(2,1)S(1)}, bf16[4,8,3200]{2,1,0:T(8,128)(2,1)S(1)}, u32[]{:S(2)}, u32[]{:S(2)}) collective-permute-start(bf16[4,8,3200]{2,1,0:T(8,128)(2,1)S(1)} %get-tuple-element.112), channel_id=1, source_target_pairs={{0,1},{1,0},{2,3},{3,2},{4,5},{5,4},{6,7},{7,6},{8,9},{9,8},{10,11... | collective-permute-start | bytes 614408 | tf_op jit(solution)/shard_map/ppermute | solution.py:589
  171.8 1.3 collective-permute-start.9
  173.0 3.9 %collective-permute-done.8 = bf16[4,8,3200]{2,1,0:T(8,128)(2,1)S(1)} collective-permute-done((bf16[4,8,3200]{2,1,0:T(8,128)(2,1)S(1)}, bf16[4,8,3200]{2,1,0:T(8,128)(2,1)S(1)}, u32[]{:S(2)}, u32[]{:S(2)}) %collective-permute-start.8) | collective-permute-done | bytes 204832 | tf_op jit(solution)/shard_map/ppermute | solution.py:589
  176.9 3.4 %collective-permute-done.10 = bf16[4,8,3200]{2,1,0:T(8,128)(2,1)S(1)} collective-permute-done((bf16[4,8,3200]{2,1,0:T(8,128)(2,1)S(1)}, bf16[4,8,3200]{2,1,0:T(8,128)(2,1)S(1)}, u32[]{:S(2)}, u32[]{:S(2)}) %collective-permute-start.10) | collective-permute-done | bytes 204832 | tf_op jit(solution)/shard_map/ppermute | solution.py:589
  180.3 2.0 collective-permute-done.9
  182.4 2.0 collective-permute-start.13
  184.4 1.6 collective-permute-start.11
  187.2 2.5 %collective-permute-done.12 = bf16[1,8,3200]{2,1,0:T(8,128)(2,1)S(1)} collective-permute-done((bf16[1,8,3200]{2,1,0:T(8,128)(2,1)S(1)}, bf16[1,8,3200]{2,1,0:T(8,128)(2,1)S(1)}, u32[]{:S(2)}, u32[]{:S(2)}) %collective-permute-start.12) | collective-permute-done | bytes 51232 | tf_op jit(solution)/shard_map/ppermute | solution.py:589
  190.4 1.6 shard_map.389
  192.0 2.1 collective-permute-start.16
  194.1 1.5 collective-permute-start.14
  199.6 1.4 collective-permute-start.17
  202.0 4.9 %collective-permute-start.20 = (f32[8,128]{1,0:T(8,128)S(1)}, f32[8,128]{1,0:T(8,128)S(1)}, u32[]{:S(2)}, u32[]{:S(2)}) collective-permute-start(f32[8,128]{1,0:T(8,128)S(1)} %add_add_fusion.own_squares), channel_id=1, source_target_pairs={{0,8},{1,9},{2,10},{3,11},{4,12},{5,13},{6,14},{7,15},{8,0},{9,1},... | collective-permute-start | bytes 12296 | tf_op jit(solution)/shard_map/ppermute | solution.py:589
  209.4 1.9 shard_map.390
  (63 shorter events, 16.7 us)
Async XLA Ops:
  0.7 25.0 %copy-start.5 = (bf16[2,196,256]{2,0,1:T(2,128)(2,1)S(1)}, bf16[2,196,256]{2,0,1:T(2,128)(2,1)}, u32[]{:S(2)}) copy-start(bf16[2,196,256]{2,0,1:T(2,128)(2,1)} %param.22) | copy-start | bytes 602116
  2.2 5.9 %collective-permute-start.2 = (bf16[1,8,3200]{2,1,0:T(8,128)(2,1)}, bf16[1,8,3200]{2,1,0:T(8,128)(2,1)S(1)}, u32[]{:S(2)}, u32[]{:S(2)}) collective-permute-start(bf16[1,8,3200]{2,1,0:T(8,128)(2,1)} %bitcast.30), channel_id=1, source_target_pairs={{0,6},{1,7},{2,4},{3,5},{4,2},{5,3},{6,0},{7,1},{8,14},{9,15},{10,... | collective-permute-start | bytes 153608 | tf_op jit(solution)/shard_map/ppermute | solution.py:589
  6.3 4.6 %collective-permute-start.1 = (bf16[1,8,3200]{2,1,0:T(8,128)(2,1)}, bf16[1,8,3200]{2,1,0:T(8,128)(2,1)S(1)}, u32[]{:S(2)}, u32[]{:S(2)}) collective-permute-start(bf16[1,8,3200]{2,1,0:T(8,128)(2,1)} %bitcast.31), channel_id=1, source_target_pairs={{0,4},{1,5},{2,6},{3,7},{4,0},{5,1},{6,2},{7,3},{8,12},{9,13},{10,... | collective-permute-start | bytes 153608 | tf_op jit(solution)/shard_map/ppermute | solution.py:589
  6.3 4.6 %collective-permute-start = (bf16[1,8,3200]{2,1,0:T(8,128)(2,1)}, bf16[1,8,3200]{2,1,0:T(8,128)(2,1)S(1)}, u32[]{:S(2)}, u32[]{:S(2)}) collective-permute-start(bf16[1,8,3200]{2,1,0:T(8,128)(2,1)} %bitcast.32), channel_id=1, source_target_pairs={{0,2},{1,3},{2,0},{3,1},{4,6},{5,7},{6,4},{7,5},{8,10},{9,11},{10,... | collective-permute-start | bytes 153608 | tf_op jit(solution)/shard_map/ppermute | solution.py:589
  11.8 11.9 %collective-permute-start.5 = (bf16[4,8,3200]{2,1,0:T(8,128)(2,1)S(1)}, bf16[4,8,3200]{2,1,0:T(8,128)(2,1)S(1)}, u32[]{:S(2)}, u32[]{:S(2)}) collective-permute-start(bf16[4,8,3200]{2,1,0:T(8,128)(2,1)S(1)} %pad_maximum_fusion), channel_id=1, source_target_pairs={{0,17},{1,16},{2,19},{3,18},{4,21},{5,20},{6,23},{7,22},{8,25},{9,... | collective-permute-start | bytes 614408 | tf_op jit(solution)/shard_map/ppermute | solution.py:589
  14.0 9.6 %collective-permute-start.4 = (bf16[4,8,3200]{2,1,0:T(8,128)(2,1)S(1)}, bf16[4,8,3200]{2,1,0:T(8,128)(2,1)S(1)}, u32[]{:S(2)}, u32[]{:S(2)}) collective-permute-start(bf16[4,8,3200]{2,1,0:T(8,128)(2,1)S(1)} %pad_maximum_fusion), channel_id=1, source_target_pairs={{0,16},{1,17},{2,18},{3,19},{4,20},{5,21},{6,22},{7,23},{8,24},{9,... | collective-permute-start | bytes 614408 | tf_op jit(solution)/shard_map/ppermute | solution.py:589
  14.3 8.1 %collective-permute-start.3 = (bf16[4,8,3200]{2,1,0:T(8,128)(2,1)S(1)}, bf16[4,8,3200]{2,1,0:T(8,128)(2,1)S(1)}, u32[]{:S(2)}, u32[]{:S(2)}) collective-permute-start(bf16[4,8,3200]{2,1,0:T(8,128)(2,1)S(1)} %pad_maximum_fusion), channel_id=1, source_target_pairs={{0,1},{1,0},{2,3},{3,2},{4,5},{5,4},{6,7},{7,6},{8,9},{9,8},{10,11... | collective-permute-start | bytes 614408 | tf_op jit(solution)/shard_map/ppermute | solution.py:589
  23.7 3.2 %collective-permute-start.6 = (bf16[16,8,3200]{2,1,0:T(8,128)(2,1)S(1)}, bf16[16,8,3200]{2,1,0:T(8,128)(2,1)S(1)}, u32[]{:S(2)}, u32[]{:S(2)}) collective-permute-start(bf16[16,8,3200]{2,1,0:T(8,128)(2,1)S(1)} %constant_dynamic-update-slice_fusion.near), channel_id=1, source_target_pairs={{0,8},{1,9},{2,10},{3,11},{4,12},{5,13},{6,14},{7,15},{8,0},{9,1},... | collective-permute-start | bytes 2457608 | tf_op jit(solution)/shard_map/ppermute | solution.py:589
  65.1 32.2 %collective-permute-start.7 = (f32[16,8,3200]{2,1,0:T(8,128)}, f32[16,8,3200]{2,1,0:T(8,128)S(1)}, u32[]{:S(2)}, u32[]{:S(2)}) collective-permute-start(f32[16,8,3200]{2,1,0:T(8,128)} %get-tuple-element.59), channel_id=1, source_target_pairs={{0,8},{1,9},{2,10},{3,11},{4,12},{5,13},{6,14},{7,15},{8,0},{9,1},... | collective-permute-start | bytes 4915208 | tf_op jit(solution)/shard_map/ppermute | solution.py:589
  98.9 108.0 %copy-start.3 = (bf16[2,196,256]{2,1,0:T(8,128)(2,1)S(1)}, bf16[2,196,256]{2,1,0:T(8,128)(2,1)}, u32[]{:S(2)}) copy-start(bf16[2,196,256]{2,1,0:T(8,128)(2,1)} %get-tuple-element.83) | copy-start | bytes 602116
  99.0 108.8 %copy-start.2 = (f32[2,196,256]{2,1,0:T(8,128)S(1)}, f32[2,196,256]{2,1,0:T(8,128)}, u32[]{:S(2)}) copy-start(f32[2,196,256]{2,1,0:T(8,128)} %get-tuple-element.85) | copy-start | bytes 1204228
  99.0 77.9 %collective-permute-start.8 = (bf16[4,8,3200]{2,1,0:T(8,128)(2,1)S(1)}, bf16[4,8,3200]{2,1,0:T(8,128)(2,1)S(1)}, u32[]{:S(2)}, u32[]{:S(2)}) collective-permute-start(bf16[4,8,3200]{2,1,0:T(8,128)(2,1)S(1)} %get-tuple-element.112), channel_id=1, source_target_pairs={{0,1},{1,0},{2,3},{3,2},{4,5},{5,4},{6,7},{7,6},{8,9},{9,8},{10,11... | collective-permute-start | bytes 614408 | tf_op jit(solution)/shard_map/ppermute | solution.py:589
  171.8 8.5 %collective-permute-start.10 = (bf16[4,8,3200]{2,1,0:T(8,128)(2,1)S(1)}, bf16[4,8,3200]{2,1,0:T(8,128)(2,1)S(1)}, u32[]{:S(2)}, u32[]{:S(2)}) collective-permute-start(bf16[4,8,3200]{2,1,0:T(8,128)(2,1)S(1)} %get-tuple-element.113), channel_id=1, source_target_pairs={{0,17},{1,16},{2,19},{3,18},{4,21},{5,20},{6,23},{7,22},{8,25},{9,... | collective-permute-start | bytes 614408 | tf_op jit(solution)/shard_map/ppermute | solution.py:589
  171.8 10.5 %collective-permute-start.9 = (bf16[4,8,3200]{2,1,0:T(8,128)(2,1)S(1)}, bf16[4,8,3200]{2,1,0:T(8,128)(2,1)S(1)}, u32[]{:S(2)}, u32[]{:S(2)}) collective-permute-start(bf16[4,8,3200]{2,1,0:T(8,128)(2,1)S(1)} %get-tuple-element.114), channel_id=1, source_target_pairs={{0,16},{1,17},{2,18},{3,19},{4,20},{5,21},{6,22},{7,23},{8,24},{9,... | collective-permute-start | bytes 614408 | tf_op jit(solution)/shard_map/ppermute | solution.py:589
  182.4 4.9 %collective-permute-start.13 = (bf16[1,8,3200]{2,1,0:T(8,128)(2,1)S(1)}, bf16[1,8,3200]{2,1,0:T(8,128)(2,1)S(1)}, u32[]{:S(2)}, u32[]{:S(2)}) collective-permute-start(bf16[1,8,3200]{2,1,0:T(8,128)(2,1)S(1)} %get-tuple-element.115), channel_id=1, source_target_pairs={{0,6},{1,7},{2,4},{3,5},{4,2},{5,3},{6,0},{7,1},{8,14},{9,15},{10,... | collective-permute-start | bytes 153608 | tf_op jit(solution)/shard_map/ppermute | solution.py:589
  184.4 5.4 %collective-permute-start.12 = (bf16[1,8,3200]{2,1,0:T(8,128)(2,1)S(1)}, bf16[1,8,3200]{2,1,0:T(8,128)(2,1)S(1)}, u32[]{:S(2)}, u32[]{:S(2)}) collective-permute-start(bf16[1,8,3200]{2,1,0:T(8,128)(2,1)S(1)} %get-tuple-element.116), channel_id=1, source_target_pairs={{0,4},{1,5},{2,6},{3,7},{4,0},{5,1},{6,2},{7,3},{8,12},{9,13},{10,... | collective-permute-start | bytes 153608 | tf_op jit(solution)/shard_map/ppermute | solution.py:589
  184.4 5.4 %collective-permute-start.11 = (bf16[1,8,3200]{2,1,0:T(8,128)(2,1)S(1)}, bf16[1,8,3200]{2,1,0:T(8,128)(2,1)S(1)}, u32[]{:S(2)}, u32[]{:S(2)}) collective-permute-start(bf16[1,8,3200]{2,1,0:T(8,128)(2,1)S(1)} %get-tuple-element.117), channel_id=1, source_target_pairs={{0,2},{1,3},{2,0},{3,1},{4,6},{5,7},{6,4},{7,5},{8,10},{9,11},{10,... | collective-permute-start | bytes 153608 | tf_op jit(solution)/shard_map/ppermute | solution.py:589
  192.0 4.5 %collective-permute-start.16 = (f32[8,128]{1,0:T(8,128)}, f32[8,128]{1,0:T(8,128)S(1)}, u32[]{:S(2)}, u32[]{:S(2)}) collective-permute-start(f32[8,128]{1,0:T(8,128)} %get-tuple-element.61), channel_id=1, source_target_pairs={{0,6},{1,7},{2,4},{3,5},{4,2},{5,3},{6,0},{7,1},{8,14},{9,15},{10,... | collective-permute-start | bytes 12296 | tf_op jit(solution)/shard_map/ppermute | solution.py:589
  194.1 3.6 %collective-permute-start.15 = (f32[8,128]{1,0:T(8,128)}, f32[8,128]{1,0:T(8,128)S(1)}, u32[]{:S(2)}, u32[]{:S(2)}) collective-permute-start(f32[8,128]{1,0:T(8,128)} %get-tuple-element.61), channel_id=1, source_target_pairs={{0,4},{1,5},{2,6},{3,7},{4,0},{5,1},{6,2},{7,3},{8,12},{9,13},{10,... | collective-permute-start | bytes 12296 | tf_op jit(solution)/shard_map/ppermute | solution.py:589
  194.1 3.6 %collective-permute-start.14 = (f32[8,128]{1,0:T(8,128)}, f32[8,128]{1,0:T(8,128)S(1)}, u32[]{:S(2)}, u32[]{:S(2)}) collective-permute-start(f32[8,128]{1,0:T(8,128)} %get-tuple-element.61), channel_id=1, source_target_pairs={{0,2},{1,3},{2,0},{3,1},{4,6},{5,7},{6,4},{7,5},{8,10},{9,11},{10,... | collective-permute-start | bytes 12296 | tf_op jit(solution)/shard_map/ppermute | solution.py:589
  198.3 3.4 %collective-permute-start.19 = (f32[8,128]{1,0:T(8,128)S(1)}, f32[8,128]{1,0:T(8,128)S(1)}, u32[]{:S(2)}, u32[]{:S(2)}) collective-permute-start(f32[8,128]{1,0:T(8,128)S(1)} %add_add_fusion.1), channel_id=1, source_target_pairs={{0,17},{1,16},{2,19},{3,18},{4,21},{5,20},{6,23},{7,22},{8,25},{9,... | collective-permute-start | bytes 12296 | tf_op jit(solution)/shard_map/ppermute | solution.py:589
  198.6 3.1 %collective-permute-start.18 = (f32[8,128]{1,0:T(8,128)S(1)}, f32[8,128]{1,0:T(8,128)S(1)}, u32[]{:S(2)}, u32[]{:S(2)}) collective-permute-start(f32[8,128]{1,0:T(8,128)S(1)} %add_add_fusion.1), channel_id=1, source_target_pairs={{0,16},{1,17},{2,18},{3,19},{4,20},{5,21},{6,22},{7,23},{8,24},{9,... | collective-permute-start | bytes 12296 | tf_op jit(solution)/shard_map/ppermute | solution.py:589
  199.6 2.5 %collective-permute-start.17 = (f32[8,128]{1,0:T(8,128)S(1)}, f32[8,128]{1,0:T(8,128)S(1)}, u32[]{:S(2)}, u32[]{:S(2)}) collective-permute-start(f32[8,128]{1,0:T(8,128)S(1)} %add_add_fusion.1), channel_id=1, source_target_pairs={{0,1},{1,0},{2,3},{3,2},{4,5},{5,4},{6,7},{7,6},{8,9},{9,8},{10,11... | collective-permute-start | bytes 12296 | tf_op jit(solution)/shard_map/ppermute | solution.py:589
  202.0 6.7 %collective-permute-start.20 = (f32[8,128]{1,0:T(8,128)S(1)}, f32[8,128]{1,0:T(8,128)S(1)}, u32[]{:S(2)}, u32[]{:S(2)}) collective-permute-start(f32[8,128]{1,0:T(8,128)S(1)} %add_add_fusion.own_squares), channel_id=1, source_target_pairs={{0,8},{1,9},{2,10},{3,11},{4,12},{5,13},{6,14},{7,15},{8,0},{9,1},... | collective-permute-start | bytes 12296 | tf_op jit(solution)/shard_map/ppermute | solution.py:589
  (8 other events, 39.5 us)

commit v5 on v4

--- a/solution.py
+++ b/solution.py
@@ -264,11 +264,12 @@
         pos = conv_rows(v[0 : s.rows, :], taps, s, False) + offset
         b["o"][rows_of(sb), :] = o + pos
 
-    ready = scores_of(0)
-    for sb in range(2 * s.stripes):
+    order = [*range(s.stripes, 2 * s.stripes), *range(s.stripes)]
+    ready = scores_of(order[0])
+    for i, sb in enumerate(order):
         scores = ready
-        if sb + 1 < 2 * s.stripes:
-            ready = scores_of(sb + 1)
+        if i + 1 < len(order):
+            ready = scores_of(order[i + 1])
         take_turns(phase_b(sb, scores))
 
     b["a"][0 : s.all, LANES:] = turned(b["o"][s.all :, :]).astype(BF)
@@ -389,14 +390,17 @@
         lanes = slice(which * d + LANES, (which + 1) * d)
         b["dqkv"][0 : s.all, lanes] = turned(b["dq"][which, s.all :, :]).astype(BF)
 
-    def phase_e(t):
+    def normed_grad(t):
         rows = rows_of(t)
         for which in range(3):
             b["dqkv"][rows, which * d : which * d + LANES] = b["dq"][which, rows, :].astype(BF)
         dqkv = b["dqkv"][rows, :]
         gv[2] += fold_rows(dqkv[:, 0:d].astype(F32))
         gv[3] += fold_rows(dqkv[:, 2 * d :].astype(F32))
-        dh1 = dot_nt(dqkv, w_ref[:, o_qkv : o_qkv + 3 * d])
+        return dot_nt(dqkv, w_ref[:, o_qkv : o_qkv + 3 * d])
+
+    def phase_e(t, dh1):
+        rows = rows_of(t)
         n1 = b["n1"][rows, :]
         r1 = b["r1"][rows, :]
         dn = dh1 * vec[0:1, :]
@@ -405,8 +409,12 @@
         gv[0] += fold_rows(dh1 * n1)
         gv[1] += fold_rows(dh1)
 
+    ahead = normed_grad(0)
     for t in range(s.stripes):
-        phase_e(t)
+        now = ahead
+        if t + 1 < s.stripes:
+            ahead = normed_grad(t + 1)
+        phase_e(t, now)
 
     for r in range(s.side):
         dx_ref[0, r * s.side : (r + 1) * s.side, :] = b["out"][

time: 212 us -> 205 us (0.967); the launches traced: 211 us -> 209 us
  Pallas kernels: 42.3 us -> 18.6 us
  starting transfers between devices: 126 us -> 148 us
    pallas_call x1, Pallas kernels: 37.3 us -> 13.6 us  [run_block(): pl.pallas_call(functools.partial(block_kernel, orders, names, (len(small_...]
    ppermute x21, starting transfers between devices: 126 us -> 148 us  [swap(): return lax.ppermute(value, AXES, [(i, i ^ mask) for i in range(count)])]
where the time goes in v5:
time: 205 us; the launch traced here: 209 us
  starting transfers between devices  148 us (72%)
  waiting for transfers between devices  31.5 us (15%)
  Pallas kernels  18.6 us (9%)
  local copies, waits for them, and re-layouts  6.97 us (3%)
  other arithmetic  3.3 us (2%)
    ppermute x21, starting transfers between devices, swap(): return lax.ppermute(value, AXES, [(i, i ^ mask) for i in range(count)])  148 us
    ppermute x21, waiting for transfers between devices, swap(): return lax.ppermute(value, AXES, [(i, i ^ mask) for i in range(count)])  31.5 us
    pallas_call x1, Pallas kernels, run_block(): pl.pallas_call(functools.partial(block_kernel, orders, names, (len(small_...  13.6 us
    unnamed x32, local copies, waits for them, and re-layouts  6.24 us
  transfers between devices with their start and end apart: 21, of which 15 were waited for; matrix products, arithmetic and copies ran while one was open for 2% of the time, Pallas kernels for 0%

profile of v5, /device:TPU:1, one launch (start us, length us, event | category | flops | bytes accessed | tf_op | source)
XLA Modules:
  0.0 209.1 jit_solution(10254979432026159658)
XLA Ops:
  0.7 1.5 shard_map.387
  2.2 4.2 %collective-permute-start.2 = (bf16[1,8,3200]{2,1,0:T(8,128)(2,1)}, bf16[1,8,3200]{2,1,0:T(8,128)(2,1)S(1)}, u32[]{:S(2)}, u32[]{:S(2)}) collective-permute-start(bf16[1,8,3200]{2,1,0:T(8,128)(2,1)} %bitcast.30), channel_id=1, source_target_pairs={{0,6},{1,7},{2,4},{3,5},{4,2},{5,3},{6,0},{7,1},{8,14},{9,15},{10,... | collective-permute-start | bytes 153608 | tf_op jit(solution)/shard_map/ppermute | solution.py:597
  8.1 2.9 %collective-permute-done.1 = bf16[1,8,3200]{2,1,0:T(8,128)(2,1)S(1)} collective-permute-done((bf16[1,8,3200]{2,1,0:T(8,128)(2,1)}, bf16[1,8,3200]{2,1,0:T(8,128)(2,1)S(1)}, u32[]{:S(2)}, u32[]{:S(2)}) %collective-permute-start.1) | collective-permute-done | bytes 51232 | tf_op jit(solution)/shard_map/ppermute | solution.py:597
  11.8 2.2 %collective-permute-start.5 = (bf16[4,8,3200]{2,1,0:T(8,128)(2,1)S(1)}, bf16[4,8,3200]{2,1,0:T(8,128)(2,1)S(1)}, u32[]{:S(2)}, u32[]{:S(2)}) collective-permute-start(bf16[4,8,3200]{2,1,0:T(8,128)(2,1)S(1)} %pad_maximum_fusion), channel_id=1, source_target_pairs={{0,17},{1,16},{2,19},{3,18},{4,21},{5,20},{6,23},{7,22},{8,25},{9,... | collective-permute-start | bytes 614408 | tf_op jit(solution)/shard_map/ppermute | solution.py:597
  14.6 7.8 %collective-permute-done.3 = bf16[4,8,3200]{2,1,0:T(8,128)(2,1)S(1)} collective-permute-done((bf16[4,8,3200]{2,1,0:T(8,128)(2,1)S(1)}, bf16[4,8,3200]{2,1,0:T(8,128)(2,1)S(1)}, u32[]{:S(2)}, u32[]{:S(2)}) %collective-permute-start.3) | collective-permute-done | bytes 204832 | tf_op jit(solution)/shard_map/ppermute | solution.py:597
  22.3 1.3 collective-permute-done.4
  23.7 1.2 collective-permute-start.6
  27.8 13.6 %shard_map.388 = (bf16[2,196,256]{2,1,0:T(8,128)(2,1)}, bf16[8,784,256]{2,1,0:T(8,128)(2,1)}, f32[2,196,256]{2,1,0:T(8,128)}, f32[8,784,256]{2,1,0:T(8,128)}, f3...) custom-call(s32[1]{0:T(128)} %bitcast.me, s32[1,2]{1,0:T(1,128)} %counts.1, bf16[2,196,256]{2,1,0:T(8,128)(2,1)} %copy.45.xs, ...), custom_call_target="tpu_custom_call" | custom-call | tf_op jit(solution)/shard_map/pallas_call | solution.py:539
  41.4 122.6 %collective-permute-start.7 = (f32[16,8,3200]{2,1,0:T(8,128)}, f32[16,8,3200]{2,1,0:T(8,128)S(1)}, u32[]{:S(2)}, u32[]{:S(2)}) collective-permute-start(f32[16,8,3200]{2,1,0:T(8,128)} %get-tuple-element.59), channel_id=1, source_target_pairs={{0,8},{1,9},{2,10},{3,11},{4,12},{5,13},{6,14},{7,15},{8,0},{9,1},... | collective-permute-start | bytes 4915208 | tf_op jit(solution)/shard_map/ppermute | solution.py:597
  164.1 3.3 %collective-permute-done.7 = f32[16,8,3200]{2,1,0:T(8,128)S(1)} collective-permute-done((f32[16,8,3200]{2,1,0:T(8,128)}, f32[16,8,3200]{2,1,0:T(8,128)S(1)}, u32[]{:S(2)}, u32[]{:S(2)}) %collective-permute-start.7) | collective-permute-done | bytes 1638432 | tf_op jit(solution)/shard_map/ppermute | solution.py:597
  167.4 1.7 fusion.4
  169.3 2.6 %collective-permute-start.9 = (bf16[4,8,3200]{2,1,0:T(8,128)(2,1)S(1)}, bf16[4,8,3200]{2,1,0:T(8,128)(2,1)S(1)}, u32[]{:S(2)}, u32[]{:S(2)}) collective-permute-start(bf16[4,8,3200]{2,1,0:T(8,128)(2,1)S(1)} %get-tuple-element.114), channel_id=1, source_target_pairs={{0,16},{1,17},{2,18},{3,19},{4,20},{5,21},{6,22},{7,23},{8,24},{9,... | collective-permute-start | bytes 614408 | tf_op jit(solution)/shard_map/ppermute | solution.py:597
  171.9 3.6 %collective-permute-done.8 = bf16[4,8,3200]{2,1,0:T(8,128)(2,1)S(1)} collective-permute-done((bf16[4,8,3200]{2,1,0:T(8,128)(2,1)S(1)}, bf16[4,8,3200]{2,1,0:T(8,128)(2,1)S(1)}, u32[]{:S(2)}, u32[]{:S(2)}) %collective-permute-start.8) | collective-permute-done | bytes 204832 | tf_op jit(solution)/shard_map/ppermute | solution.py:597
  175.5 2.6 %collective-permute-done.10 = bf16[4,8,3200]{2,1,0:T(8,128)(2,1)S(1)} collective-permute-done((bf16[4,8,3200]{2,1,0:T(8,128)(2,1)S(1)}, bf16[4,8,3200]{2,1,0:T(8,128)(2,1)S(1)}, u32[]{:S(2)}, u32[]{:S(2)}) %collective-permute-start.10) | collective-permute-done | bytes 204832 | tf_op jit(solution)/shard_map/ppermute | solution.py:597
  178.1 3.5 %collective-permute-done.9 = bf16[4,8,3200]{2,1,0:T(8,128)(2,1)S(1)} collective-permute-done((bf16[4,8,3200]{2,1,0:T(8,128)(2,1)S(1)}, bf16[4,8,3200]{2,1,0:T(8,128)(2,1)S(1)}, u32[]{:S(2)}, u32[]{:S(2)}) %collective-permute-start.9) | collective-permute-done | bytes 204832 | tf_op jit(solution)/shard_map/ppermute | solution.py:597
  181.8 1.0 collective-permute-start.12
  182.8 2.5 %collective-permute-start.11 = (bf16[1,8,3200]{2,1,0:T(8,128)(2,1)S(1)}, bf16[1,8,3200]{2,1,0:T(8,128)(2,1)S(1)}, u32[]{:S(2)}, u32[]{:S(2)}) collective-permute-start(bf16[1,8,3200]{2,1,0:T(8,128)(2,1)S(1)} %get-tuple-element.117), channel_id=1, source_target_pairs={{0,2},{1,3},{2,0},{3,1},{4,6},{5,7},{6,4},{7,5},{8,10},{9,11},{10,... | collective-permute-start | bytes 153608 | tf_op jit(solution)/shard_map/ppermute | solution.py:597
  186.6 1.0 collective-permute-done.11
  188.2 1.6 shard_map.389
  189.8 2.7 %collective-permute-start.16 = (f32[8,128]{1,0:T(8,128)}, f32[8,128]{1,0:T(8,128)S(1)}, u32[]{:S(2)}, u32[]{:S(2)}) collective-permute-start(f32[8,128]{1,0:T(8,128)} %get-tuple-element.61), channel_id=1, source_target_pairs={{0,6},{1,7},{2,4},{3,5},{4,2},{5,3},{6,0},{7,1},{8,14},{9,15},{10,... | collective-permute-start | bytes 12296 | tf_op jit(solution)/shard_map/ppermute | solution.py:597
  194.3 1.8 collective-permute-done.15
  197.1 2.3 %collective-permute-start.17 = (f32[8,128]{1,0:T(8,128)S(1)}, f32[8,128]{1,0:T(8,128)S(1)}, u32[]{:S(2)}, u32[]{:S(2)}) collective-permute-start(f32[8,128]{1,0:T(8,128)S(1)} %add_add_fusion.1), channel_id=1, source_target_pairs={{0,1},{1,0},{2,3},{3,2},{4,5},{5,4},{6,7},{7,6},{8,9},{9,8},{10,11... | collective-permute-start | bytes 12296 | tf_op jit(solution)/shard_map/ppermute | solution.py:597
  200.5 4.4 %collective-permute-start.20 = (f32[8,128]{1,0:T(8,128)S(1)}, f32[8,128]{1,0:T(8,128)S(1)}, u32[]{:S(2)}, u32[]{:S(2)}) collective-permute-start(f32[8,128]{1,0:T(8,128)S(1)} %add_add_fusion.own_squares), channel_id=1, source_target_pairs={{0,8},{1,9},{2,10},{3,11},{4,12},{5,13},{6,14},{7,15},{8,0},{9,1},... | collective-permute-start | bytes 12296 | tf_op jit(solution)/shard_map/ppermute | solution.py:597
  207.2 1.9 shard_map.390
  (63 shorter events, 14.5 us)
Async XLA Ops:
  0.7 25.0 %copy-start.5 = (bf16[2,196,256]{2,0,1:T(2,128)(2,1)S(1)}, bf16[2,196,256]{2,0,1:T(2,128)(2,1)}, u32[]{:S(2)}) copy-start(bf16[2,196,256]{2,0,1:T(2,128)(2,1)} %param.22) | copy-start | bytes 602116
  2.2 5.9 %collective-permute-start.2 = (bf16[1,8,3200]{2,1,0:T(8,128)(2,1)}, bf16[1,8,3200]{2,1,0:T(8,128)(2,1)S(1)}, u32[]{:S(2)}, u32[]{:S(2)}) collective-permute-start(bf16[1,8,3200]{2,1,0:T(8,128)(2,1)} %bitcast.30), channel_id=1, source_target_pairs={{0,6},{1,7},{2,4},{3,5},{4,2},{5,3},{6,0},{7,1},{8,14},{9,15},{10,... | collective-permute-start | bytes 153608 | tf_op jit(solution)/shard_map/ppermute | solution.py:597
  6.3 4.6 %collective-permute-start.1 = (bf16[1,8,3200]{2,1,0:T(8,128)(2,1)}, bf16[1,8,3200]{2,1,0:T(8,128)(2,1)S(1)}, u32[]{:S(2)}, u32[]{:S(2)}) collective-permute-start(bf16[1,8,3200]{2,1,0:T(8,128)(2,1)} %bitcast.31), channel_id=1, source_target_pairs={{0,4},{1,5},{2,6},{3,7},{4,0},{5,1},{6,2},{7,3},{8,12},{9,13},{10,... | collective-permute-start | bytes 153608 | tf_op jit(solution)/shard_map/ppermute | solution.py:597
  6.3 4.6 %collective-permute-start = (bf16[1,8,3200]{2,1,0:T(8,128)(2,1)}, bf16[1,8,3200]{2,1,0:T(8,128)(2,1)S(1)}, u32[]{:S(2)}, u32[]{:S(2)}) collective-permute-start(bf16[1,8,3200]{2,1,0:T(8,128)(2,1)} %bitcast.32), channel_id=1, source_target_pairs={{0,2},{1,3},{2,0},{3,1},{4,6},{5,7},{6,4},{7,5},{8,10},{9,11},{10,... | collective-permute-start | bytes 153608 | tf_op jit(solution)/shard_map/ppermute | solution.py:597
  11.8 11.9 %collective-permute-start.5 = (bf16[4,8,3200]{2,1,0:T(8,128)(2,1)S(1)}, bf16[4,8,3200]{2,1,0:T(8,128)(2,1)S(1)}, u32[]{:S(2)}, u32[]{:S(2)}) collective-permute-start(bf16[4,8,3200]{2,1,0:T(8,128)(2,1)S(1)} %pad_maximum_fusion), channel_id=1, source_target_pairs={{0,17},{1,16},{2,19},{3,18},{4,21},{5,20},{6,23},{7,22},{8,25},{9,... | collective-permute-start | bytes 614408 | tf_op jit(solution)/shard_map/ppermute | solution.py:597
  14.0 9.6 %collective-permute-start.4 = (bf16[4,8,3200]{2,1,0:T(8,128)(2,1)S(1)}, bf16[4,8,3200]{2,1,0:T(8,128)(2,1)S(1)}, u32[]{:S(2)}, u32[]{:S(2)}) collective-permute-start(bf16[4,8,3200]{2,1,0:T(8,128)(2,1)S(1)} %pad_maximum_fusion), channel_id=1, source_target_pairs={{0,16},{1,17},{2,18},{3,19},{4,20},{5,21},{6,22},{7,23},{8,24},{9,... | collective-permute-start | bytes 614408 | tf_op jit(solution)/shard_map/ppermute | solution.py:597
  14.3 8.1 %collective-permute-start.3 = (bf16[4,8,3200]{2,1,0:T(8,128)(2,1)S(1)}, bf16[4,8,3200]{2,1,0:T(8,128)(2,1)S(1)}, u32[]{:S(2)}, u32[]{:S(2)}) collective-permute-start(bf16[4,8,3200]{2,1,0:T(8,128)(2,1)S(1)} %pad_maximum_fusion), channel_id=1, source_target_pairs={{0,1},{1,0},{2,3},{3,2},{4,5},{5,4},{6,7},{7,6},{8,9},{9,8},{10,11... | collective-permute-start | bytes 614408 | tf_op jit(solution)/shard_map/ppermute | solution.py:597
  23.7 3.2 %collective-permute-start.6 = (bf16[16,8,3200]{2,1,0:T(8,128)(2,1)S(1)}, bf16[16,8,3200]{2,1,0:T(8,128)(2,1)S(1)}, u32[]{:S(2)}, u32[]{:S(2)}) collective-permute-start(bf16[16,8,3200]{2,1,0:T(8,128)(2,1)S(1)} %constant_dynamic-update-slice_fusion.near), channel_id=1, source_target_pairs={{0,8},{1,9},{2,10},{3,11},{4,12},{5,13},{6,14},{7,15},{8,0},{9,1},... | collective-permute-start | bytes 2457608 | tf_op jit(solution)/shard_map/ppermute | solution.py:597
  41.4 126.0 %collective-permute-start.7 = (f32[16,8,3200]{2,1,0:T(8,128)}, f32[16,8,3200]{2,1,0:T(8,128)S(1)}, u32[]{:S(2)}, u32[]{:S(2)}) collective-permute-start(f32[16,8,3200]{2,1,0:T(8,128)} %get-tuple-element.59), channel_id=1, source_target_pairs={{0,8},{1,9},{2,10},{3,11},{4,12},{5,13},{6,14},{7,15},{8,0},{9,1},... | collective-permute-start | bytes 4915208 | tf_op jit(solution)/shard_map/ppermute | solution.py:597
  169.1 35.7 %copy-start.3 = (bf16[2,196,256]{2,1,0:T(8,128)(2,1)S(1)}, bf16[2,196,256]{2,1,0:T(8,128)(2,1)}, u32[]{:S(2)}) copy-start(bf16[2,196,256]{2,1,0:T(8,128)(2,1)} %get-tuple-element.83) | copy-start | bytes 602116
  169.1 36.5 %copy-start.2 = (f32[2,196,256]{2,1,0:T(8,128)S(1)}, f32[2,196,256]{2,1,0:T(8,128)}, u32[]{:S(2)}) copy-start(f32[2,196,256]{2,1,0:T(8,128)} %get-tuple-element.85) | copy-start | bytes 1204228
  169.2 6.4 %collective-permute-start.8 = (bf16[4,8,3200]{2,1,0:T(8,128)(2,1)S(1)}, bf16[4,8,3200]{2,1,0:T(8,128)(2,1)S(1)}, u32[]{:S(2)}, u32[]{:S(2)}) collective-permute-start(bf16[4,8,3200]{2,1,0:T(8,128)(2,1)S(1)} %get-tuple-element.112), channel_id=1, source_target_pairs={{0,1},{1,0},{2,3},{3,2},{4,5},{5,4},{6,7},{7,6},{8,9},{9,8},{10,11... | collective-permute-start | bytes 614408 | tf_op jit(solution)/shard_map/ppermute | solution.py:597
  169.2 8.8 %collective-permute-start.10 = (bf16[4,8,3200]{2,1,0:T(8,128)(2,1)S(1)}, bf16[4,8,3200]{2,1,0:T(8,128)(2,1)S(1)}, u32[]{:S(2)}, u32[]{:S(2)}) collective-permute-start(bf16[4,8,3200]{2,1,0:T(8,128)(2,1)S(1)} %get-tuple-element.113), channel_id=1, source_target_pairs={{0,17},{1,16},{2,19},{3,18},{4,21},{5,20},{6,23},{7,22},{8,25},{9,... | collective-permute-start | bytes 614408 | tf_op jit(solution)/shard_map/ppermute | solution.py:597
  169.3 12.3 %collective-permute-start.9 = (bf16[4,8,3200]{2,1,0:T(8,128)(2,1)S(1)}, bf16[4,8,3200]{2,1,0:T(8,128)(2,1)S(1)}, u32[]{:S(2)}, u32[]{:S(2)}) collective-permute-start(bf16[4,8,3200]{2,1,0:T(8,128)(2,1)S(1)} %get-tuple-element.114), channel_id=1, source_target_pairs={{0,16},{1,17},{2,18},{3,19},{4,20},{5,21},{6,22},{7,23},{8,24},{9,... | collective-permute-start | bytes 614408 | tf_op jit(solution)/shard_map/ppermute | solution.py:597
  181.7 4.9 %collective-permute-start.13 = (bf16[1,8,3200]{2,1,0:T(8,128)(2,1)S(1)}, bf16[1,8,3200]{2,1,0:T(8,128)(2,1)S(1)}, u32[]{:S(2)}, u32[]{:S(2)}) collective-permute-start(bf16[1,8,3200]{2,1,0:T(8,128)(2,1)S(1)} %get-tuple-element.115), channel_id=1, source_target_pairs={{0,6},{1,7},{2,4},{3,5},{4,2},{5,3},{6,0},{7,1},{8,14},{9,15},{10,... | collective-permute-start | bytes 153608 | tf_op jit(solution)/shard_map/ppermute | solution.py:597
  181.8 4.8 %collective-permute-start.12 = (bf16[1,8,3200]{2,1,0:T(8,128)(2,1)S(1)}, bf16[1,8,3200]{2,1,0:T(8,128)(2,1)S(1)}, u32[]{:S(2)}, u32[]{:S(2)}) collective-permute-start(bf16[1,8,3200]{2,1,0:T(8,128)(2,1)S(1)} %get-tuple-element.116), channel_id=1, source_target_pairs={{0,4},{1,5},{2,6},{3,7},{4,0},{5,1},{6,2},{7,3},{8,12},{9,13},{10,... | collective-permute-start | bytes 153608 | tf_op jit(solution)/shard_map/ppermute | solution.py:597
  182.8 4.9 %collective-permute-start.11 = (bf16[1,8,3200]{2,1,0:T(8,128)(2,1)S(1)}, bf16[1,8,3200]{2,1,0:T(8,128)(2,1)S(1)}, u32[]{:S(2)}, u32[]{:S(2)}) collective-permute-start(bf16[1,8,3200]{2,1,0:T(8,128)(2,1)S(1)} %get-tuple-element.117), channel_id=1, source_target_pairs={{0,2},{1,3},{2,0},{3,1},{4,6},{5,7},{6,4},{7,5},{8,10},{9,11},{10,... | collective-permute-start | bytes 153608 | tf_op jit(solution)/shard_map/ppermute | solution.py:597
  189.8 4.5 %collective-permute-start.16 = (f32[8,128]{1,0:T(8,128)}, f32[8,128]{1,0:T(8,128)S(1)}, u32[]{:S(2)}, u32[]{:S(2)}) collective-permute-start(f32[8,128]{1,0:T(8,128)} %get-tuple-element.61), channel_id=1, source_target_pairs={{0,6},{1,7},{2,4},{3,5},{4,2},{5,3},{6,0},{7,1},{8,14},{9,15},{10,... | collective-permute-start | bytes 12296 | tf_op jit(solution)/shard_map/ppermute | solution.py:597
  192.5 3.6 %collective-permute-start.15 = (f32[8,128]{1,0:T(8,128)}, f32[8,128]{1,0:T(8,128)S(1)}, u32[]{:S(2)}, u32[]{:S(2)}) collective-permute-start(f32[8,128]{1,0:T(8,128)} %get-tuple-element.61), channel_id=1, source_target_pairs={{0,4},{1,5},{2,6},{3,7},{4,0},{5,1},{6,2},{7,3},{8,12},{9,13},{10,... | collective-permute-start | bytes 12296 | tf_op jit(solution)/shard_map/ppermute | solution.py:597
  192.5 3.6 %collective-permute-start.14 = (f32[8,128]{1,0:T(8,128)}, f32[8,128]{1,0:T(8,128)S(1)}, u32[]{:S(2)}, u32[]{:S(2)}) collective-permute-start(f32[8,128]{1,0:T(8,128)} %get-tuple-element.61), channel_id=1, source_target_pairs={{0,2},{1,3},{2,0},{3,1},{4,6},{5,7},{6,4},{7,5},{8,10},{9,11},{10,... | collective-permute-start | bytes 12296 | tf_op jit(solution)/shard_map/ppermute | solution.py:597
  196.8 3.4 %collective-permute-start.19 = (f32[8,128]{1,0:T(8,128)S(1)}, f32[8,128]{1,0:T(8,128)S(1)}, u32[]{:S(2)}, u32[]{:S(2)}) collective-permute-start(f32[8,128]{1,0:T(8,128)S(1)} %add_add_fusion.1), channel_id=1, source_target_pairs={{0,17},{1,16},{2,19},{3,18},{4,21},{5,20},{6,23},{7,22},{8,25},{9,... | collective-permute-start | bytes 12296 | tf_op jit(solution)/shard_map/ppermute | solution.py:597
  196.9 3.3 %collective-permute-start.18 = (f32[8,128]{1,0:T(8,128)S(1)}, f32[8,128]{1,0:T(8,128)S(1)}, u32[]{:S(2)}, u32[]{:S(2)}) collective-permute-start(f32[8,128]{1,0:T(8,128)S(1)} %add_add_fusion.1), channel_id=1, source_target_pairs={{0,16},{1,17},{2,18},{3,19},{4,20},{5,21},{6,22},{7,23},{8,24},{9,... | collective-permute-start | bytes 12296 | tf_op jit(solution)/shard_map/ppermute | solution.py:597
  197.1 3.3 %collective-permute-start.17 = (f32[8,128]{1,0:T(8,128)S(1)}, f32[8,128]{1,0:T(8,128)S(1)}, u32[]{:S(2)}, u32[]{:S(2)}) collective-permute-start(f32[8,128]{1,0:T(8,128)S(1)} %add_add_fusion.1), channel_id=1, source_target_pairs={{0,1},{1,0},{2,3},{3,2},{4,5},{5,4},{6,7},{7,6},{8,9},{9,8},{10,11... | collective-permute-start | bytes 12296 | tf_op jit(solution)/shard_map/ppermute | solution.py:597
  200.5 6.1 %collective-permute-start.20 = (f32[8,128]{1,0:T(8,128)S(1)}, f32[8,128]{1,0:T(8,128)S(1)}, u32[]{:S(2)}, u32[]{:S(2)}) collective-permute-start(f32[8,128]{1,0:T(8,128)S(1)} %add_add_fusion.own_squares), channel_id=1, source_target_pairs={{0,8},{1,9},{2,10},{3,11},{4,12},{5,13},{6,14},{7,15},{8,0},{9,1},... | collective-permute-start | bytes 12296 | tf_op jit(solution)/shard_map/ppermute | solution.py:597
  (8 other events, 37.8 us)
